TPU v7x, 1024 devices: a whole 4x8x16 slice. The times are simulated.
1024 devices in a mesh: tower: 16 (over y, core), hst: 64 (over x, z).
Axes of the slice: x: 4, y: 8, z: 16, core: 2. Of those that a mesh axis runs over, the one named last changes fastest.
Arguments:
- top_grad: bfloat16 [2048, 64, 256], P(('tower', 'hst')), may hold values from -6 to 6
- pooled_in: bfloat16 [64, 2048, 2048], P('hst', 'tower'), may hold values from -6 to 6
- w_down: bfloat16 [64, 2048, 256], P('hst'), may hold values from -0.125 to 0.125
- w_up: bfloat16 [64, 256, 2048], P('hst'), may hold values from -0.375 to 0.375
- cross_bias: float32 [64, 2048], P('hst'), may hold values from -3 to 3
- w_comp: bfloat16 [64, 2048, 256], P('hst'), may hold values from -0.375 to 0.375
- feature_slot: int32 [64, 16], P('hst'), may hold values from 0 to 15, each once within a row
- bag_ids: int32 [64, 16, 2048, 8], P('hst', 'tower'), may hold values from 0 to 511
- bag_lengths: int32 [64, 16, 2048], P('hst', 'tower'), may hold values from 1 to 8
Outputs:
- grad_down: float32 [64, 2048, 256], P('hst', 'tower')
- grad_up: float32 [64, 256, 2048], P('hst', None, 'tower')
- grad_bias: float32 [64, 2048], P('hst', 'tower')
- grad_comp: float32 [64, 2048, 256], P('hst', 'tower')
- table_grads: float32 [64, 16, 512, 128], P('hst', 'tower')
Inputs may be any that keep to these rules, and one draw needn't show every extreme that they name: `feature_slot`: each of a tower module's slots holds another table. `bag_ids`: slots at or past a bag's length hold row ids that count for nothing.
All inputs are finite; a program needn't handle non-finite values.
Results may differ from a plain program's by a relative error of at most 0.0065.
Values may be sent and summed in bfloat16 or wider, within the bound.
No kernel may reach another device: no remote copies, remote signals or barrier semaphores. Data moves between devices by JAX's collectives and lax.ppermute only.
A program may use at most 32 MiB of HBM per device.

v0:
```python
import jax
import jax.numpy as jnp
from jax import lax
from jax.sharding import PartitionSpec as P

EMBED = 128
FEATS = 16
TABLE_ROWS = 512
SLOTS = 8
WIDTH = 2048


def contract_rows(left, right):
    return lax.dot_general(
        left, right, (((0,), (0,)), ((), ())), preferred_element_type=jnp.float32
    )


def contract_cols(left, right):
    return lax.dot_general(
        left, right, (((1,), (1,)), ((), ())), preferred_element_type=jnp.float32
    )


def on_device(
    top_grad, pooled_in, w_down, w_up, cross_bias, w_comp, feature_slot, bag_ids, bag_lengths
):
    arrived = lax.all_to_all(top_grad, "hst", split_axis=1, concat_axis=0, tiled=True)
    out_grad = arrived.reshape(-1, arrived.shape[2])
    inputs = pooled_in[0]
    down_mat = w_down[0]
    up_mat = w_up[0]
    low_rank = jnp.dot(inputs, down_mat, preferred_element_type=jnp.float32).astype(jnp.bfloat16)
    scale_pre = jnp.dot(low_rank, up_mat, preferred_element_type=jnp.float32) + cross_bias[0]
    wide_in = inputs.astype(jnp.float32)
    crossed = (wide_in * scale_pre + wide_in).astype(jnp.bfloat16)
    cross_grad = contract_cols(out_grad, w_comp[0])
    scale_grad = (cross_grad * wide_in).astype(jnp.bfloat16)
    rank_grad = contract_cols(scale_grad, up_mat).astype(jnp.bfloat16)
    back_term = contract_cols(rank_grad, down_mat)
    input_grad = (cross_grad * (scale_pre + 1.0) + back_term).astype(jnp.bfloat16)
    tower_rows = input_grad.shape[0]
    slot_order = jnp.argsort(feature_slot[0])
    by_table = jnp.take(input_grad.reshape(tower_rows, FEATS, EMBED), slot_order, axis=1).reshape(
        tower_rows, WIDTH
    )
    owned = lax.all_to_all(by_table, "tower", split_axis=1, concat_axis=0, tiled=True)
    comp_term = contract_rows(crossed, out_grad)
    down_term = contract_rows(inputs, rank_grad)
    up_term = contract_rows(scale_grad, low_rank)
    bias_term = jnp.sum(scale_grad.astype(jnp.float32), axis=0)
    comp_part, down_part, up_part, bias_part = (
        lax.psum_scatter(comp_term, "tower", scatter_dimension=0, tiled=True),
        lax.psum_scatter(down_term, "tower", scatter_dimension=0, tiled=True),
        lax.psum_scatter(up_term, "tower", scatter_dimension=0, tiled=True),
        lax.psum_scatter(bias_term, "tower", scatter_dimension=0, tiled=True),
    )
    all_rows = owned.shape[0]
    feat_local = bag_ids.shape[1]
    local_ids = bag_ids[0]
    local_lengths = bag_lengths[0]
    inverse = 1.0 / local_lengths.astype(jnp.float32)
    table_rows = jnp.transpose(owned.reshape(all_rows, feat_local, EMBED), (1, 0, 2)).astype(
        jnp.float32
    )
    scaled = table_rows * inverse[:, :, None]
    high_part = scaled.astype(jnp.bfloat16)
    low_part = (scaled - high_part.astype(jnp.float32)).astype(jnp.bfloat16)
    split_rows = jnp.concatenate([high_part, low_part], axis=2)
    block_rows = min(512, TABLE_ROWS)
    block_count = TABLE_ROWS // block_rows

    def table_block(index):
        feature = index // block_count
        block_start = index % block_count * block_rows
        feat_ids = lax.dynamic_index_in_dim(local_ids, feature, 0, keepdims=False)
        feat_lengths = lax.dynamic_index_in_dim(local_lengths, feature, 0, keepdims=False)
        feat_rows = lax.dynamic_index_in_dim(split_rows, feature, 0, keepdims=False)
        row_values = block_start + jnp.arange(block_rows, dtype=jnp.int32)
        counts = jnp.zeros((block_rows, all_rows), jnp.float32)
        for slot in range(SLOTS):
            hits = (feat_ids[:, slot][None, :] == row_values[:, None]) & (feat_lengths > slot)[
                None, :
            ]
            counts = counts + hits.astype(jnp.float32)
        product = jnp.dot(
            counts.astype(jnp.bfloat16), feat_rows, preferred_element_type=jnp.float32
        )
        return product[:, :EMBED] + product[:, EMBED:]

    blocks = lax.map(table_block, jnp.arange(feat_local * block_count, dtype=jnp.int32))
    return (
        down_part[None],
        jnp.transpose(up_part)[None],
        bias_part[None],
        comp_part[None],
        blocks[None],
    )


def solution(mesh):
    placed = (
        P(("tower", "hst"), None, None),
        P("hst", "tower", None),
        P("hst", None, None),
        P("hst", None, None),
        P("hst", None),
        P("hst", None, None),
        P("hst", None),
        P("hst", "tower", None, None),
        P("hst", "tower", None),
    )
    return jax.shard_map(
        on_device,
        mesh=mesh,
        in_specs=placed,
        out_specs=(
            P("hst", "tower", None),
            P("hst", None, "tower"),
            P("hst", "tower"),
            P("hst", "tower", None),
            P("hst", "tower", None, None),
        ),
        check_vma=False,
    )
```

profile of v0, /device:TPU:1, one launch (start us, length us, event | category | flops | bytes accessed | tf_op | source)
XLA Modules:
  0.0 259.2 jit_solution(12871710378544058471)
XLA Ops:
  7.2 0.0 copy-start
  7.2 0.0 copy-start.1
  7.2 1.7 copy.20
  8.8 22.8 %all-to-all-start = ((bf16[2,64,256]{2,0,1:T(2,128)(2,1)}), bf16[2,64,256]{2,0,1:T(2,128)(2,1)S(1)}, u32[]{:S(2)}, u32[]{:S(2)}) async-start(bf16[2,64,256]{2,0,1:T(2,128)(2,1)} %copy.20), calls=%async_computation | async-start | bytes 131072 | tf_op jit(solution)/shard_map/all_to_all | solution.py:28
  31.6 0.0 reduce-scatter.6.cloned.1.call-start
  31.7 1.7 convolution_convert_fusion
  33.4 11.8 %all-to-all-done = bf16[2,64,256]{2,0,1:T(2,128)(2,1)S(1)} async-done(((bf16[2,64,256]{2,0,1:T(2,128)(2,1)}), bf16[2,64,256]{2,0,1:T(2,128)(2,1)S(1)}, u32[]{:S(2)}, u32[]{:S(2)}) %all-to-all-start) | async-done | bytes 65568 | tf_op jit(solution)/shard_map/all_to_all | solution.py:28
  45.2 0.0 copy-done
  45.2 0.0 copy-done.1
  45.2 1.5 convert_reduce_fusion
  46.7 1.8 fusion.39
  48.5 0.0 reduce-scatter.6.cloned.1.call-update
  48.5 0.0 reduce-scatter.4.cloned.1.call-start
  48.5 1.7 convolution_convert_fusion.1
  50.2 0.0 copy-start.5
  50.3 1.8 convolution_bitcast_fusion
  52.1 0.0 reduce-scatter.4.cloned.1.call-update
  52.1 0.0 reduce-scatter.8.cloned.1.call-start
  52.1 0.0 copy-done.5
  52.1 1.5 convolution_add_fusion.1
  53.7 0.0 copy-start.6
  53.7 0.0 copy-start.4
  53.7 1.8 fusion.30
  55.5 0.0 copy-start.2
  55.5 0.0 reduce-scatter.8.cloned.1.call-update
  55.6 1.4 dynamic-slice
  57.6 0.0 copy-done.6
  57.6 1.2 sort.17
  58.9 0.0 copy-done.4
  58.9 0.2 compare_reduce_fusion.7
  59.1 0.0 copy-done.2
  59.1 1.7 fusion.18
  60.8 0.0 copy-start.3
  60.8 0.1 copy.26
  61.0 0.6 gather_fusion
  61.6 0.9 select_bitcast_fusion
  62.5 9.2 %all-to-all-start.1 = ((bf16[128,16,128]{2,0,1:T(8,128)(2,1)}), bf16[128,16,128]{2,0,1:T(8,128)(2,1)S(1)}, u32[]{:S(2)}, u32[]{:S(2)}) async-start(bf16[128,16,128]{2,0,1:T(8,128)(2,1)} %select_bitcast_fusion), calls=%async_computation.4 | async-start | bytes 1048576 | tf_op jit(solution)/shard_map/all_to_all | solution.py:47
  71.8 0.0 copy-done.3
  71.8 31.8 %all-reduce = f32[2048]{0:T(1024)S(1)} all-reduce(f32[2048]{0:T(1024)S(1)} %get-tuple-element.45), channel_id=4, replica_groups=mesh['tower'=16,'hst'=64] {'tower'}, use_global_device_ids=true, to_apply=%region_3.4.clone | all-reduce | flops 2048 | bytes 16384
  103.6 0.6 dynamic-slice_bitcast_fusion
  104.2 0.0 all-to-all-done.1
  104.2 0.3 fusion.29
  104.6 6.6 %fusion.9 = f32[512,256]{1,0:T(8,128)S(1)} fusion(s32[2048]{0:T(1024)S(1)} %bitcast.91, s32[2048]{0:T(1024)S(1)} %bitcast.92, s32[2048]{0:T(1024)S(1)} %bitcast.93, s32[2048]{0:T(1024)S(1)} %bitcast.94, s32[2048]{0:T(1024)S(1)} %bitcast.95, s32[2048]{0:T(1024)S(1)} %bitcast.96, s32[2048]{0:T(1024)S(1)} %bitcast.97, s32[2048]{0:T(1024)S(1)} %bitcast.90, ...), kind=kOutput, calls=%fused_computation.22 | convolution fusion | flops 572522496 | bytes 1654784 | tf_op jit(solution)/shard_map/while/body/eval_jaxpr/dot_general | solution.py:86
  111.2 0.8 fusion.35
  112.0 0.1 reduce-scatter.6.cloned.1.call-done
  112.1 1.7 copy.23
  113.8 68.9 %reduce-scatter.4.cloned.1.call-done = f32[128,256]{0,1:T(8,128)} async-done(((f32[2048,256]{0,1:T(8,128)}), f32[128,256]{0,1:T(8,128)}) %reduce-scatter.4.cloned.1.call-update) | async-done | bytes 131088 | tf_op jit(solution)/shard_map/reduce_scatter | solution.py:54
  182.7 1.7 copy.22
  184.3 68.4 %reduce-scatter.8.cloned.1.call-done = f32[128,256]{1,0:T(8,128)} async-done(((f32[2048,256]{1,0:T(8,128)}), f32[128,256]{1,0:T(8,128)}) %reduce-scatter.8.cloned.1.call-update) | async-done | bytes 131088 | tf_op jit(solution)/shard_map/reduce_scatter | solution.py:53
  (7 shorter events, 0.1 us)
Async XLA Ops:
  7.2 38.0 %copy-start = (bf16[1,2048,256]{2,1,0:T(8,128)(2,1)S(1)}, bf16[1,2048,256]{2,1,0:T(8,128)(2,1)}, u32[]{:S(2)}) copy-start(bf16[1,2048,256]{2,1,0:T(8,128)(2,1)} %param.14) | copy-start | bytes 3145732
  7.2 38.0 %copy-start.1 = (bf16[1,128,2048]{2,1,0:T(8,128)(2,1)S(1)}, bf16[1,128,2048]{2,1,0:T(8,128)(2,1)}, u32[]{:S(2)}) copy-start(bf16[1,128,2048]{2,1,0:T(8,128)(2,1)} %param.10) | copy-start | bytes 1572868
  8.8 36.3 %all-to-all-start = ((bf16[2,64,256]{2,0,1:T(2,128)(2,1)}), bf16[2,64,256]{2,0,1:T(2,128)(2,1)S(1)}, u32[]{:S(2)}, u32[]{:S(2)}) async-start(bf16[2,64,256]{2,0,1:T(2,128)(2,1)} %copy.20), calls=%async_computation | async-start | bytes 131072 | tf_op jit(solution)/shard_map/all_to_all | solution.py:28
  31.6 80.5 %reduce-scatter.6.cloned.1.call-start = ((), (), s32[]{:S(2)}) async-start(), calls=%async_computation.6 | async-start | bytes 2228224 | tf_op jit(solution)/shard_map/reduce_scatter | solution.py:55
  48.5 134.2 %reduce-scatter.4.cloned.1.call-start = ((), (), s32[]{:S(2)}) async-start(), calls=%async_computation.5 | async-start | bytes 2228224 | tf_op jit(solution)/shard_map/reduce_scatter | solution.py:54
  50.2 1.9 copy-start.5
  52.1 200.6 %reduce-scatter.8.cloned.1.call-start = ((), (), s32[]{:S(2)}) async-start(), calls=%async_computation.7 | async-start | bytes 2228224 | tf_op jit(solution)/shard_map/reduce_scatter | solution.py:53
  53.7 3.9 %copy-start.6 = (s32[1,16]{1,0:T(1,128)S(1)}, s32[1,16]{1,0:T(1,128)}, u32[]{:S(2)}) copy-start(s32[1,16]{1,0:T(1,128)} %param.15) | copy-start | bytes 196
  53.7 5.2 %copy-start.4 = (s32[1,1,2048]{2,1,0:T(1,128)S(1)}, s32[1,1,2048]{2,1,0:T(1,128)}, u32[]{:S(2)}) copy-start(s32[1,1,2048]{2,1,0:T(1,128)} %param.17) | copy-start | bytes 24580
  55.5 3.5 %copy-start.2 = (f32[128,2048]{1,0:T(8,128)S(1)}, f32[128,2048]{1,0:T(8,128)}, u32[]{:S(2)}) copy-start(f32[128,2048]{1,0:T(8,128)} %get-tuple-element.57) | copy-start | bytes 3145732
  60.8 11.0 %copy-start.3 = (s32[1,1,2048,8]{2,3,1,0:T(8,128)S(1)}, s32[1,1,2048,8]{2,3,1,0:T(8,128)}, u32[]{:S(2)}) copy-start(s32[1,1,2048,8]{2,3,1,0:T(8,128)} %param.16) | copy-start | bytes 196612
  62.5 41.7 %all-to-all-start.1 = ((bf16[128,16,128]{2,0,1:T(8,128)(2,1)}), bf16[128,16,128]{2,0,1:T(8,128)(2,1)S(1)}, u32[]{:S(2)}, u32[]{:S(2)}) async-start(bf16[128,16,128]{2,0,1:T(8,128)(2,1)} %select_bitcast_fusion), calls=%async_computation.4 | async-start | bytes 1048576 | tf_op jit(solution)/shard_map/all_to_all | solution.py:47
Sparse Core Ops, SparseCore 0:
  48.6 63.4 reduce-scatter.5
  115.5 67.1 reduce-scatter.3
  186.6 66.0 reduce-scatter.7
where the time goes:
time: 260 us; the launch traced here: 259 us
  waiting for transfers between devices  149 us (57%)
  starting transfers between devices  32.1 us (12%)
  blocking collectives  31.8 us (12%)
  matrix products  20.2 us (8%)
  between operations  14.6 us (6%)
  local copies, waits for them, and re-layouts  7.82 us (3%)
  other arithmetic  3.49 us (1%)
    reduce_scatter x1, waiting for transfers between devices, on_device(): lax.psum_scatter(down_term, 'tower', scatter_dimension=0, tiled=True)  68.9 us
    reduce_scatter x1, waiting for transfers between devices, on_device(): lax.psum_scatter(comp_term, 'tower', scatter_dimension=0, tiled=True)  68.4 us
    unnamed x1, blocking collectives  31.8 us
    all_to_all x1, starting transfers between devices, on_device(): lax.all_to_all(top_grad, 'hst', split_axis=1, concat_axis=0, tiled=True)  22.8 us
    all_to_all x1, waiting for transfers between devices, on_device(): lax.all_to_all(top_grad, 'hst', split_axis=1, concat_axis=0, tiled=True)  11.8 us
    all_to_all x1, starting transfers between devices, on_device(): lax.all_to_all(by_table, 'tower', split_axis=1, concat_axis=0, tiled=True)  9.21 us
    dot_general x1, matrix products, table_block(): jnp.dot(counts.astype(jnp.bfloat16), feat_rows, preferred_element_type=jn...  6.64 us
    unnamed x18, local copies, waits for them, and re-layouts  6.37 us
  transfers between devices with their start and end apart: 5, of which 4 were waited for; matrix products, arithmetic and copies ran while one was open for 10% of the time, Pallas kernels for 0%

commit v1 on v0

v1 whole, which is shorter than its diff:
```python
import functools

import jax
import jax.numpy as jnp
from jax import lax
from jax.experimental import pallas as pl
from jax.experimental.pallas import tpu as pltpu
from jax.sharding import PartitionSpec as P

EMBED = 128
COMP = 256
RANK = 256
TABLE_ROWS = 512
SLOTS = 8
CHIPS = 8
CORES = 2
BLOCK = 128
HALF = CHIPS * BLOCK

SAME_CORE = [[chip * CORES + core for chip in range(CHIPS)] for core in range(CORES)]
SWAP = [(t, t ^ 1) for t in range(CHIPS * CORES)]


def shifted(step):
    return [
        (chip * CORES + core, (chip + step) % CHIPS * CORES + core)
        for chip in range(CHIPS)
        for core in range(CORES)
    ]


def contract_rows(left, right):
    return lax.dot_general(
        left, right, (((0,), (0,)), ((), ())), preferred_element_type=jnp.float32
    )


def contract_cols(left, right):
    return lax.dot_general(
        left, right, (((1,), (1,)), ((), ())), preferred_element_type=jnp.float32
    )


def product(left, right):
    return jnp.dot(left, right, preferred_element_type=jnp.float32)


def counts_kernel(ids_ref, lengths_ref, counts_ref):
    tile = counts_ref.shape[0]
    first = pl.program_id(0) * tile
    lengths = lengths_ref[...]
    row_values = first + lax.broadcasted_iota(jnp.int32, counts_ref.shape, 0)
    total = jnp.zeros(counts_ref.shape, jnp.float32)
    for slot in range(SLOTS):
        live = jnp.where(lengths > slot, ids_ref[slot : slot + 1, :], -1)
        total = total + jnp.where(live == row_values, 1.0, 0.0)
    counts_ref[...] = total.astype(jnp.bfloat16)


def bag_counts(ids, lengths):
    bags = ids.shape[1]
    tile = 64
    return pl.pallas_call(
        counts_kernel,
        grid=(TABLE_ROWS // tile,),
        in_specs=[
            pl.BlockSpec((SLOTS, bags), lambda i: (0, 0)),
            pl.BlockSpec((1, bags), lambda i: (0, 0)),
        ],
        out_specs=pl.BlockSpec((tile, bags), lambda i: (i, 0)),
        out_shape=jax.ShapeDtypeStruct((TABLE_ROWS, bags), jnp.bfloat16),
        cost_estimate=pl.CostEstimate(
            flops=30_000_000_00, bytes_accessed=3_000_000, transcendentals=0
        ),
        name="bag_counts",
    )(ids, lengths)


def half_kernel(
    first,
    place_ref,
    grads_ref,
    saved_ref,
    counts_ref,
    inverse_ref,
    comp_ref,
    up_ref,
    bias_ref,
    down_ref,
    *refs,
):
    if first:
        before = (None,) * 5
    else:
        before, refs = refs[:5], refs[5:]
    out_refs, (crossed_ref, scale_ref, split_ref, low_flat, x_flat, counts_flat) = refs[:5], refs[5:]
    core = place_ref[0]
    chip = place_ref[1]
    if not first:
        core = 1 - core

    @pl.loop(0, CHIPS)
    def _(k):
        rows = pl.ds(pl.multiple_of(k * BLOCK, BLOCK), BLOCK)
        block = k * CORES + core
        at = lax.rem(chip - k + CHIPS, CHIPS)
        x = saved_ref[at, 0]
        low = jnp.concatenate(
            [saved_ref[at, saved_ref.shape[1] - 2], saved_ref[at, saved_ref.shape[1] - 1]], axis=1
        )
        low_flat[rows, :] = low
        x_flat[rows, :] = x
        out_grad = grads_ref[rows, :COMP]
        rank_grad = grads_ref[rows, COMP:]
        cross = contract_cols(out_grad, comp_ref[...])
        scale = product(low, up_ref[...]) + bias_ref[...]
        back = contract_cols(rank_grad, down_ref[...])
        input_grad = (cross[:, EMBED:] * (scale[:, EMBED:] + 1.0) + back).astype(jnp.bfloat16)
        scaled = input_grad.astype(jnp.float32) * inverse_ref[block]
        high = scaled.astype(jnp.bfloat16)
        split_ref[rows, :EMBED] = high
        split_ref[rows, EMBED:] = (scaled - high.astype(jnp.float32)).astype(jnp.bfloat16)
        wide = x.astype(jnp.float32)
        crossed_ref[rows, :] = (wide * scale[:, :EMBED] + wide).astype(jnp.bfloat16)
        scale_ref[rows, :] = (cross[:, :EMBED] * wide).astype(jnp.bfloat16)
        counts_flat[:, rows] = counts_ref[
            :, pl.ds(pl.multiple_of(block * BLOCK, BLOCK), BLOCK)
        ]

    table = product(counts_flat[...], split_ref[...])
    terms = [
        contract_rows(x_flat[...], grads_ref[:, COMP:]),
        contract_rows(scale_ref[...], low_flat[...]),
        jnp.sum(scale_ref[...].astype(jnp.float32), axis=0, keepdims=True),
        contract_rows(crossed_ref[...], grads_ref[:, :COMP]),
        table[:, :EMBED] + table[:, EMBED:],
    ]
    if not first:
        terms = [term + ref[...] for term, ref in zip(terms, before)]
        terms[1] = terms[1].T
    for ref, term in zip(out_refs, terms):
        ref[...] = term


def half(place, grads, saved, counts, inverse, weights, before=None):
    first = before is None
    shapes = [(EMBED, RANK), (EMBED, RANK), (1, EMBED), (EMBED, COMP), (TABLE_ROWS, EMBED)]
    if not first:
        shapes[1] = (RANK, EMBED)
    whole = pl.BlockSpec(memory_space=pltpu.VMEM)
    operands = [grads, saved, counts, inverse, *weights] + ([] if first else list(before))
    return pl.pallas_call(
        functools.partial(half_kernel, first),
        in_specs=[pl.BlockSpec(memory_space=pltpu.SMEM)] + [whole] * len(operands),
        out_specs=[whole] * 5,
        out_shape=[jax.ShapeDtypeStruct(shape, jnp.float32) for shape in shapes],
        scratch_shapes=[
            pltpu.VMEM((HALF, EMBED), jnp.bfloat16),
            pltpu.VMEM((HALF, EMBED), jnp.bfloat16),
            pltpu.VMEM((HALF, 2 * EMBED), jnp.bfloat16),
            pltpu.VMEM((HALF, RANK), jnp.bfloat16),
            pltpu.VMEM((HALF, EMBED), jnp.bfloat16),
            pltpu.VMEM((TABLE_ROWS, HALF), jnp.bfloat16),
        ],
        compiler_params=pltpu.CompilerParams(vmem_limit_bytes=32 * 1024 * 1024),
        cost_estimate=pl.CostEstimate(
            flops=1_500_000_000, bytes_accessed=6_000_000, transcendentals=0
        ),
        name="column_half_first" if first else "column_half_second",
    )(place, *operands)


def pack_kernel(place_ref, x_ref, down_ref, blocks_ref):
    core, chip = place_ref[0], place_ref[1]
    low = product(x_ref[...], down_ref[...]).astype(jnp.bfloat16)
    for step in range(CHIPS):
        base = lax.rem(chip + step, CHIPS) * CORES
        for turn in range(CORES):
            slot = base + (core if turn == 0 else 1 - core)
            blocks_ref[step, turn] = x_ref[:, pl.ds(pl.multiple_of(slot * EMBED, EMBED), EMBED)]
        blocks_ref[step, 2] = low[:, :BLOCK]
        blocks_ref[step, 3] = low[:, BLOCK:]


def pack(place, inputs, down_mat):
    whole = pl.BlockSpec(memory_space=pltpu.VMEM)
    return pl.pallas_call(
        pack_kernel,
        in_specs=[pl.BlockSpec(memory_space=pltpu.SMEM), whole, whole],
        out_specs=whole,
        out_shape=jax.ShapeDtypeStruct((CHIPS, 4, BLOCK, EMBED), jnp.bfloat16),
        compiler_params=pltpu.CompilerParams(vmem_limit_bytes=16 * 1024 * 1024),
        cost_estimate=pl.CostEstimate(
            flops=140_000_000, bytes_accessed=2_600_000, transcendentals=0
        ),
        name="low_rank_and_columns",
    )(place, inputs, down_mat)


def on_device(
    top_grad, pooled_in, w_down, w_up, cross_bias, w_comp, feature_slot, bag_ids, bag_lengths
):
    arrived = lax.all_to_all(top_grad, "hst", split_axis=1, concat_axis=0, tiled=True)
    out_grad = arrived.reshape(BLOCK, COMP)
    me = lax.axis_index("tower")
    place = jnp.stack([me & 1, me >> 1]).astype(jnp.int32)
    inputs, down_mat, up_mat, comp_mat = pooled_in[0], w_down[0], w_up[0], w_comp[0]

    packed = pack(place, inputs, down_mat)
    arrived_blocks = [packed[0]] + [
        lax.ppermute(packed[step], "tower", shifted(step)) for step in range(1, CHIPS)
    ]

    counts = bag_counts(jnp.transpose(bag_ids[0, 0]), bag_lengths[0])
    inverse = jnp.broadcast_to(
        (1.0 / bag_lengths[0, 0].astype(jnp.float32))[:, None], (CHIPS * CORES * BLOCK, EMBED)
    ).reshape(CHIPS * CORES, BLOCK, EMBED)
    slot = jnp.sum(jnp.where(feature_slot[0] == me, jnp.arange(CHIPS * CORES, dtype=jnp.int32), 0))

    def two_slots(array, axis):
        return jnp.concatenate(
            [
                lax.dynamic_slice_in_dim(array, me * EMBED, EMBED, axis),
                lax.dynamic_slice_in_dim(array, slot * EMBED, EMBED, axis),
            ],
            axis,
        )

    weights = (
        two_slots(comp_mat, 0),
        two_slots(up_mat, 1),
        two_slots(cross_bias, 1),
        lax.dynamic_slice_in_dim(down_mat, slot * EMBED, EMBED, 0),
    )

    cross_grad = contract_cols(out_grad, comp_mat)
    scale_grad = (cross_grad * inputs.astype(jnp.float32)).astype(jnp.bfloat16)
    rank_grad = contract_cols(scale_grad, up_mat).astype(jnp.bfloat16)

    both = jnp.concatenate([out_grad, rank_grad], axis=1)
    both, *arrived_blocks = lax.optimization_barrier((both, *arrived_blocks))
    own = jnp.stack(arrived_blocks)
    other = lax.ppermute(own[:, 1:], "tower", SWAP)
    grads_own = lax.all_to_all(
        jnp.broadcast_to(both[None], (CHIPS, BLOCK, COMP + RANK)),
        "tower",
        split_axis=0,
        concat_axis=0,
        tiled=True,
        axis_index_groups=SAME_CORE,
    ).reshape(HALF, COMP + RANK)
    grads_other = lax.ppermute(grads_own, "tower", SWAP)

    first = half(place, grads_own, own, counts, inverse, weights)
    grad_down, grad_up, grad_bias, grad_comp, tables = half(
        place, grads_other, other, counts, inverse, weights, first
    )
    return grad_down[None], grad_up[None], grad_bias, grad_comp[None], tables[None, None]


def solution(mesh):
    placed = (
        P(("tower", "hst"), None, None),
        P("hst", "tower", None),
        P("hst", None, None),
        P("hst", None, None),
        P("hst", None),
        P("hst", None, None),
        P("hst", None),
        P("hst", "tower", None, None),
        P("hst", "tower", None),
    )
    return jax.shard_map(
        on_device,
        mesh=mesh,
        in_specs=placed,
        out_specs=(
            P("hst", "tower", None),
            P("hst", None, "tower"),
            P("hst", "tower"),
            P("hst", "tower", None),
            P("hst", "tower", None, None),
        ),
        check_vma=False,
    )
```

time: 260 us -> 126 us (0.48)
  waiting for transfers between devices: 149 us -> 25.1 us
  blocking collectives: 31.8 us -> 0 us
  starting transfers between devices: 32.1 us -> 61 us
  matrix products: 20.2 us -> 0.83 us
  Pallas kernels: 0 us -> 14.4 us
  local copies, waits for them, and re-layouts: 7.82 us -> 21 us
  between operations: 14.6 us -> 1.61 us
  other arithmetic: 3.49 us -> 0.77 us
    reduce_scatter x3 -> x0, waiting for transfers between devices: 137 us -> none  [the longest x1 68.9 us: on_device(): lax.psum_scatter(down_term, 'tower', scatter_dimension=0, tiled=True)]
    ppermute x0 -> x9, starting transfers between devices: none -> 35.5 us  [the longest x7 29.2 us: on_device(): lax.ppermute(packed[step], 'tower', shifted(step))]
    unnamed x1 -> x0, blocking collectives: 31.8 us -> none
    dot_general x6 -> x0, matrix products: 15.3 us -> none  [the longest x1 6.64 us: table_block(): jnp.dot(counts.astype(jnp.bfloat16), feat_rows, preferred_element_type=jn...]
    pallas_call x0 -> x4, Pallas kernels: none -> 14.4 us  [the longest x2 7.69 us: half(): pl.pallas_call(functools.partial(half_kernel, first), in_specs=[pl.BlockS...]
    all_to_all x1, waiting for transfers between devices: 0.01 us -> 11 us  [on_device(): lax.all_to_all(jnp.broadcast_to(both[None], (CHIPS, BLOCK, COMP + RANK)),...]
    unnamed x18 -> x30, local copies, waits for them, and re-layouts: 6.37 us -> 13.2 us
    all_to_all x1, starting transfers between devices: 9.21 us -> 3.56 us  [on_device(): lax.all_to_all(jnp.broadcast_to(both[None], (CHIPS, BLOCK, COMP + RANK)),...]
  transfers between devices with their start and end apart: 5 -> 11, of which waited for: 4 -> 3; matrix products, arithmetic and copies ran while one was open for 10% -> 15% of each run, Pallas kernels for 0% -> 8%
where the time goes in v1:
time: 126 us; the launch traced here: 125 us
  starting transfers between devices  61 us (48%)
  waiting for transfers between devices  25.1 us (20%)
  local copies, waits for them, and re-layouts  21 us (17%)
  Pallas kernels  14.4 us (11%)
  between operations  1.61 us (1%)
    ppermute x7, starting transfers between devices, on_device(): lax.ppermute(packed[step], 'tower', shifted(step))  29.2 us
    all_to_all x1, starting transfers between devices, on_device(): lax.all_to_all(top_grad, 'hst', split_axis=1, concat_axis=0, tiled=True)  21.9 us
    unnamed x30, local copies, waits for them, and re-layouts  13.2 us
    all_to_all x1, waiting for transfers between devices, on_device(): lax.all_to_all(jnp.broadcast_to(both[None], (CHIPS, BLOCK, COMP + RANK)),...  11 us
    all_to_all x1, waiting for transfers between devices, on_device(): lax.all_to_all(top_grad, 'hst', split_axis=1, concat_axis=0, tiled=True)  9.46 us
    pallas_call x2, Pallas kernels, half(): pl.pallas_call(functools.partial(half_kernel, first), in_specs=[pl.BlockS...  7.69 us
    pallas_call x1, Pallas kernels, bag_counts(): pl.pallas_call(counts_kernel, grid=(TABLE_ROWS // tile,), in_specs=[pl.Bl...  5.86 us
    ppermute x7, waiting for transfers between devices, on_device(): lax.ppermute(packed[step], 'tower', shifted(step))  4.59 us
  transfers between devices with their start and end apart: 11, of which 3 were waited for; matrix products, arithmetic and copies ran while one was open for 15% of the time, Pallas kernels for 8%

profile of v1, /device:TPU:1, one launch (start us, length us, event | category | flops | bytes accessed | tf_op | source)
XLA Modules:
  0.0 124.8 jit_solution(8539003651557443281)
XLA Ops:
  0.6 0.1 pad_add_fusion.place_ref
  0.7 0.0 copy-start.1
  0.7 1.0 copy-done.1
  1.8 0.0 copy-start.3
  1.8 1.2 copy-done.3
  3.0 0.0 copy-start.7
  3.0 0.0 copy-start.10
  3.0 0.0 copy-start.4
  3.0 0.0 copy-start.5
  3.0 0.9 low_rank_and_columns.1
  3.9 0.0 copy-start.2
  3.9 0.8 slice_bitcast_fusion
  4.7 4.0 %collective-permute-start = (bf16[4,128,128]{2,1,0:T(8,128)(2,1)}, bf16[4,128,128]{2,1,0:T(8,128)(2,1)}, u32[]{:S(2)}, u32[]{:S(2)}) collective-permute-start(bf16[4,128,128]{2,1,0:T(8,128)(2,1)} %get-tuple-element.53), channel_id=1, source_target_pairs={{0,128},{64,192},{128,256},{192,320},{256,384},{320,448},{384,512}... | collective-permute-start | bytes 393224 | tf_op jit(solution)/shard_map/ppermute | solution.py:211
  8.8 4.2 %collective-permute-start.1 = (bf16[4,128,128]{2,1,0:T(8,128)(2,1)S(1)}, bf16[4,128,128]{2,1,0:T(8,128)(2,1)}, u32[]{:S(2)}, u32[]{:S(2)}) collective-permute-start(bf16[4,128,128]{2,1,0:T(8,128)(2,1)S(1)} %get-tuple-element.52), channel_id=1, source_target_pairs={{0,256},{64,320},{128,384},{192,448},{256,512},{320,576},{384,640}... | collective-permute-start | bytes 393224 | tf_op jit(solution)/shard_map/ppermute | solution.py:211
  13.0 4.6 %collective-permute-start.2 = (bf16[4,128,128]{2,1,0:T(8,128)(2,1)}, bf16[4,128,128]{2,1,0:T(8,128)(2,1)}, u32[]{:S(2)}, u32[]{:S(2)}) collective-permute-start(bf16[4,128,128]{2,1,0:T(8,128)(2,1)} %get-tuple-element.51), channel_id=1, source_target_pairs={{0,384},{64,448},{128,512},{192,576},{256,640},{320,704},{384,768}... | collective-permute-start | bytes 393224 | tf_op jit(solution)/shard_map/ppermute | solution.py:211
  17.7 3.5 %collective-permute-start.3 = (bf16[4,128,128]{2,1,0:T(8,128)(2,1)}, bf16[4,128,128]{2,1,0:T(8,128)(2,1)}, u32[]{:S(2)}, u32[]{:S(2)}) collective-permute-start(bf16[4,128,128]{2,1,0:T(8,128)(2,1)} %get-tuple-element.50), channel_id=1, source_target_pairs={{0,512},{64,576},{128,640},{192,704},{256,768},{320,832},{384,896}... | collective-permute-start | bytes 393224 | tf_op jit(solution)/shard_map/ppermute | solution.py:211
  21.2 4.9 %collective-permute-start.4 = (bf16[4,128,128]{2,1,0:T(8,128)(2,1)}, bf16[4,128,128]{2,1,0:T(8,128)(2,1)}, u32[]{:S(2)}, u32[]{:S(2)}) collective-permute-start(bf16[4,128,128]{2,1,0:T(8,128)(2,1)} %get-tuple-element.49), channel_id=1, source_target_pairs={{0,640},{64,704},{128,768},{192,832},{256,896},{320,960},{384,0},{... | collective-permute-start | bytes 393224 | tf_op jit(solution)/shard_map/ppermute | solution.py:211
  26.1 0.0 copy-done.7
  26.1 0.7 copy.15
  26.8 21.9 %all-to-all-start = ((bf16[2,64,256]{2,0,1:T(2,128)(2,1)}), bf16[2,64,256]{2,0,1:T(2,128)(2,1)S(1)}, u32[]{:S(2)}, u32[]{:S(2)}) async-start(bf16[2,64,256]{2,0,1:T(2,128)(2,1)} %copy.15), calls=%async_computation | async-start | bytes 131072 | tf_op jit(solution)/shard_map/all_to_all | solution.py:203
  48.7 0.0 copy-done.10
  48.8 0.6 fusion.7
  50.0 0.0 copy-done.4
  50.1 0.9 dynamic-slice_bitcast_fusion.down_ref
  51.0 1.2 constant_dynamic-slice_fusion.1
  52.1 0.0 copy-done.5
  52.1 0.7 dynamic-slice_bitcast_fusion.4
  52.8 9.5 %all-to-all-done = bf16[2,64,256]{2,0,1:T(2,128)(2,1)S(1)} async-done(((bf16[2,64,256]{2,0,1:T(2,128)(2,1)}), bf16[2,64,256]{2,0,1:T(2,128)(2,1)S(1)}, u32[]{:S(2)}, u32[]{:S(2)}) %all-to-all-start) | async-done | bytes 65568 | tf_op jit(solution)/shard_map/all_to_all | solution.py:203
  62.3 0.0 collective-permute-done
  62.3 5.0 %collective-permute-start.5 = (bf16[4,128,128]{2,1,0:T(8,128)(2,1)S(1)}, bf16[4,128,128]{2,1,0:T(8,128)(2,1)}, u32[]{:S(2)}, u32[]{:S(2)}) collective-permute-start(bf16[4,128,128]{2,1,0:T(8,128)(2,1)S(1)} %get-tuple-element.48), channel_id=1, source_target_pairs={{0,768},{64,832},{128,896},{192,960},{256,0},{320,64},{384,128},{4... | collective-permute-start | bytes 393224 | tf_op jit(solution)/shard_map/ppermute | solution.py:211
  67.3 0.0 collective-permute-done.1
  67.3 3.0 %collective-permute-start.6 = (bf16[4,128,128]{2,1,0:T(8,128)(2,1)S(1)}, bf16[4,128,128]{2,1,0:T(8,128)(2,1)}, u32[]{:S(2)}, u32[]{:S(2)}) collective-permute-start(bf16[4,128,128]{2,1,0:T(8,128)(2,1)S(1)} %get-tuple-element.47), channel_id=1, source_target_pairs={{0,896},{64,960},{128,0},{192,64},{256,128},{320,192},{384,256},{4... | collective-permute-start | bytes 393224 | tf_op jit(solution)/shard_map/ppermute | solution.py:211
  70.3 0.0 copy-done.2
  70.3 0.8 fusion.2
  71.1 0.0 collective-permute-done.2
  71.2 0.0 collective-permute-done.3
  71.2 0.0 collective-permute-done.4
  71.2 0.0 collective-permute-done.5
  71.2 4.6 %collective-permute-done.6 = bf16[4,128,128]{2,1,0:T(8,128)(2,1)} collective-permute-done((bf16[4,128,128]{2,1,0:T(8,128)(2,1)S(1)}, bf16[4,128,128]{2,1,0:T(8,128)(2,1)}, u32[]{:S(2)}, u32[]{:S(2)}) %collective-permute-start.6) | collective-permute-done | bytes 131104 | tf_op jit(solution)/shard_map/ppermute | solution.py:211
  75.8 1.1 broadcast_in_dim.28
  76.8 3.6 %all-to-all-start.1 = ((bf16[8,128,512]{2,1,0:T(8,128)(2,1)}), bf16[8,128,512]{2,1,0:T(8,128)(2,1)S(1)}, u32[]{:S(2)}, u32[]{:S(2)}) async-start(bf16[8,128,512]{2,1,0:T(8,128)(2,1)} %broadcast_in_dim.28), calls=%async_computation.1 | async-start | bytes 2097152 | tf_op jit(solution)/shard_map/all_to_all | solution.py:244
  80.4 5.9 %bag_counts.1.counts_ref = bf16[512,2048]{1,0:T(8,128)(2,1)} custom-call(s32[8,2048]{1,0:T(8,128)} %bitcast.88, s32[1,2048]{1,0:T(1,128)} %bitcast.83), custom_call_target="tpu_custom_call" | custom-call | flops 3000000000 | bytes 3000000 | tf_op jit(solution)/shard_map/bag_counts/pallas_call | solution.py:63
  86.3 0.0 copy-start.8
  86.3 0.7 bitcast_dynamic-update-slice_fusion.7
  86.9 1.6 %bitcast_dynamic-update-slice_fusion.6 = bf16[8,4,128,128]{3,2,1,0:T(8,128)(2,1)} fusion(bf16[8,4,128,128]{3,2,1,0:T(8,128)(2,1)} %bitcast_dynamic-update-slice_fusion.7, bf16[4,128,128]{2,1,0:T(8,128)(2,1)} %collective-permute-done), kind=kLoop, calls=%fused_computation.24 | loop fusion | bytes 262144
  88.5 1.6 %bitcast_dynamic-update-slice_fusion.5 = bf16[8,4,128,128]{3,2,1,0:T(8,128)(2,1)} fusion(bf16[8,4,128,128]{3,2,1,0:T(8,128)(2,1)} %bitcast_dynamic-update-slice_fusion.6, bf16[4,128,128]{2,1,0:T(8,128)(2,1)} %collective-permute-done.1), kind=kLoop, calls=%fused_computation.23 | loop fusion | bytes 262144
  90.1 1.6 %bitcast_dynamic-update-slice_fusion.4 = bf16[8,4,128,128]{3,2,1,0:T(8,128)(2,1)} fusion(bf16[8,4,128,128]{3,2,1,0:T(8,128)(2,1)} %bitcast_dynamic-update-slice_fusion.5, bf16[4,128,128]{2,1,0:T(8,128)(2,1)} %collective-permute-done.2), kind=kLoop, calls=%fused_computation.22 | loop fusion | bytes 262144
  91.7 1.7 %bitcast_dynamic-update-slice_fusion.3 = bf16[8,4,128,128]{3,2,1,0:T(8,128)(2,1)} fusion(bf16[8,4,128,128]{3,2,1,0:T(8,128)(2,1)} %bitcast_dynamic-update-slice_fusion.4, bf16[4,128,128]{2,1,0:T(8,128)(2,1)} %collective-permute-done.3), kind=kLoop, calls=%fused_computation.21 | loop fusion | bytes 262144
  93.4 1.6 %bitcast_dynamic-update-slice_fusion.2 = bf16[8,4,128,128]{3,2,1,0:T(8,128)(2,1)} fusion(bf16[8,4,128,128]{3,2,1,0:T(8,128)(2,1)} %bitcast_dynamic-update-slice_fusion.3, bf16[4,128,128]{2,1,0:T(8,128)(2,1)} %collective-permute-done.4), kind=kLoop, calls=%fused_computation.20 | loop fusion | bytes 262144
  94.9 1.6 %bitcast_dynamic-update-slice_fusion.1 = bf16[8,4,128,128]{3,2,1,0:T(8,128)(2,1)} fusion(bf16[8,4,128,128]{3,2,1,0:T(8,128)(2,1)} %bitcast_dynamic-update-slice_fusion.2, bf16[4,128,128]{2,1,0:T(8,128)(2,1)} %collective-permute-done.5), kind=kLoop, calls=%fused_computation.19 | loop fusion | bytes 262144
  96.5 11.0 %all-to-all-done.1 = bf16[8,128,512]{2,1,0:T(8,128)(2,1)S(1)} async-done(((bf16[8,128,512]{2,1,0:T(8,128)(2,1)}), bf16[8,128,512]{2,1,0:T(8,128)(2,1)S(1)}, u32[]{:S(2)}, u32[]{:S(2)}) %all-to-all-start.1) | async-done | bytes 1048608 | tf_op jit(solution)/shard_map/all_to_all | solution.py:244
  107.5 4.4 %collective-permute-start.7 = (bf16[1024,512]{1,0:T(8,128)(2,1)S(1)}, bf16[1024,512]{1,0:T(8,128)(2,1)S(1)}, u32[]{:S(2)}, u32[]{:S(2)}) collective-permute-start(bf16[1024,512]{1,0:T(8,128)(2,1)S(1)} %bitcast.77), channel_id=1, source_target_pairs={{0,64},{64,0},{128,192},{192,128},{256,320},{320,256},{384,448},{4... | collective-permute-start | bytes 3145736 | tf_op jit(solution)/shard_map/ppermute | solution.py:252
  111.9 1.6 %bitcast_dynamic-update-slice_fusion.saved_ref = bf16[8,4,128,128]{3,2,1,0:T(8,128)(2,1)} fusion(bf16[8,4,128,128]{3,2,1,0:T(8,128)(2,1)} %bitcast_dynamic-update-slice_fusion.1, bf16[4,128,128]{2,1,0:T(8,128)(2,1)} %collective-permute-done.6), kind=kLoop, calls=%fused_computation.18 | loop fusion | bytes 262144 | tf_op jit(solution)/shard_map/stack | solution.py:242
  113.5 1.2 slice.44
  114.7 1.9 %collective-permute-start.8 = (bf16[8,3,128,128]{3,2,1,0:T(8,128)(2,1)S(1)}, bf16[8,3,128,128]{3,2,1,0:T(8,128)(2,1)S(1)}, u32[]{:S(2)}, u32[]{:S(2)}) collective-permute-start(bf16[8,3,128,128]{3,2,1,0:T(8,128)(2,1)S(1)} %slice.44), channel_id=1, source_target_pairs={{0,64},{64,0},{128,192},{192,128},{256,320},{320,256},{384,448},{4... | collective-permute-start | bytes 2359304 | tf_op jit(solution)/shard_map/ppermute | solution.py:243
  116.6 0.0 copy-done.9
  116.6 0.0 copy-done.6
  116.7 0.0 copy-done.8
  116.7 0.3 broadcast_in_dim.29.inverse_ref
  117.0 0.0 copy-done
  117.1 3.8 %column_half_first.1 = (f32[128,256]{1,0:T(8,128)S(1)}, f32[128,256]{1,0:T(8,128)S(1)}, f32[1,128]{1,0:T(1,128)S(1)}, f32[128,256]{1,0:T(8,128)S(1)}, f32[512,128]{1,0:T(8,128)S(1)}) custom-call(s32[2]{0:T(128)S(1)} %pad_add_fusion.place_ref, bf16[1024,512]{1,0:T(8,128)(2,1)S(1)} %bitcast.78, ...), custom_call_target="tpu_custom_call" | custom-call | flops 1500000000 | bytes 6000000 | tf_op jit(solution)/shard_map/column_half_first/pallas_call | solution.py:152
  120.9 0.0 collective-permute-done.8.saved_ref
  120.9 0.0 collective-permute-done.7.grads_ref
  120.9 3.9 %column_half_second.1 = (f32[128,256]{1,0:T(8,128)}, f32[256,128]{1,0:T(8,128)}, f32[1,128]{1,0:T(1,128)}, f32[128,256]{1,0:T(8,128)}, f32[512,128]{1,0:T(8,128)}) custom-call(s32[2]{0:T(128)S(1)} %pad_add_fusion.place_ref, bf16[1024,512]{1,0:T(8,128)(2,1)S(1)} %collective-permute-done.7.grads_ref, ...), custom_call_target="tpu_custom_call" | custom-call | flops 1500000000 | bytes 6000000 | tf_op jit(solution)/shard_map/column_half_second/pallas_call | solution.py:152
  (9 shorter events, 0.1 us)
Async XLA Ops:
  0.7 1.0 copy-start.1
  1.8 1.2 copy-start.3
  3.0 23.1 %copy-start.7 = (bf16[2,64,256]{2,1,0:T(8,128)(2,1)S(1)}, bf16[2,64,256]{2,1,0:T(8,128)(2,1)}, u32[]{:S(2)}) copy-start(bf16[2,64,256]{2,1,0:T(8,128)(2,1)} %param.9) | copy-start | bytes 196612
  3.0 45.8 %copy-start.10 = (s32[1,16]{1,0:T(1,128)S(1)}, s32[1,16]{1,0:T(1,128)}, u32[]{:S(2)}) copy-start(s32[1,16]{1,0:T(1,128)} %param.15) | copy-start | bytes 196
  3.0 47.1 %copy-start.4 = (bf16[1,256,2048]{2,1,0:T(8,128)(2,1)S(1)}, bf16[1,256,2048]{2,1,0:T(8,128)(2,1)}, u32[]{:S(2)}) copy-start(bf16[1,256,2048]{2,1,0:T(8,128)(2,1)} %param.12) | copy-start | bytes 3145732
  3.0 49.2 %copy-start.5 = (bf16[1,2048,256]{2,1,0:T(8,128)(2,1)S(1)}, bf16[1,2048,256]{2,1,0:T(8,128)(2,1)}, u32[]{:S(2)}) copy-start(bf16[1,2048,256]{2,1,0:T(8,128)(2,1)} %param.14) | copy-start | bytes 3145732
  3.9 66.4 %copy-start.2 = (bf16[1,128,2048]{2,1,0:T(8,128)(2,1)S(1)}, bf16[1,128,2048]{2,1,0:T(8,128)(2,1)}, u32[]{:S(2)}) copy-start(bf16[1,128,2048]{2,1,0:T(8,128)(2,1)} %param.10) | copy-start | bytes 1572868
  4.7 57.6 %collective-permute-start = (bf16[4,128,128]{2,1,0:T(8,128)(2,1)}, bf16[4,128,128]{2,1,0:T(8,128)(2,1)}, u32[]{:S(2)}, u32[]{:S(2)}) collective-permute-start(bf16[4,128,128]{2,1,0:T(8,128)(2,1)} %get-tuple-element.53), channel_id=1, source_target_pairs={{0,128},{64,192},{128,256},{192,320},{256,384},{320,448},{384,512}... | collective-permute-start | bytes 393224 | tf_op jit(solution)/shard_map/ppermute | solution.py:211
  8.8 58.5 %collective-permute-start.1 = (bf16[4,128,128]{2,1,0:T(8,128)(2,1)S(1)}, bf16[4,128,128]{2,1,0:T(8,128)(2,1)}, u32[]{:S(2)}, u32[]{:S(2)}) collective-permute-start(bf16[4,128,128]{2,1,0:T(8,128)(2,1)S(1)} %get-tuple-element.52), channel_id=1, source_target_pairs={{0,256},{64,320},{128,384},{192,448},{256,512},{320,576},{384,640}... | collective-permute-start | bytes 393224 | tf_op jit(solution)/shard_map/ppermute | solution.py:211
  13.0 58.1 %collective-permute-start.2 = (bf16[4,128,128]{2,1,0:T(8,128)(2,1)}, bf16[4,128,128]{2,1,0:T(8,128)(2,1)}, u32[]{:S(2)}, u32[]{:S(2)}) collective-permute-start(bf16[4,128,128]{2,1,0:T(8,128)(2,1)} %get-tuple-element.51), channel_id=1, source_target_pairs={{0,384},{64,448},{128,512},{192,576},{256,640},{320,704},{384,768}... | collective-permute-start | bytes 393224 | tf_op jit(solution)/shard_map/ppermute | solution.py:211
  17.7 53.5 %collective-permute-start.3 = (bf16[4,128,128]{2,1,0:T(8,128)(2,1)}, bf16[4,128,128]{2,1,0:T(8,128)(2,1)}, u32[]{:S(2)}, u32[]{:S(2)}) collective-permute-start(bf16[4,128,128]{2,1,0:T(8,128)(2,1)} %get-tuple-element.50), channel_id=1, source_target_pairs={{0,512},{64,576},{128,640},{192,704},{256,768},{320,832},{384,896}... | collective-permute-start | bytes 393224 | tf_op jit(solution)/shard_map/ppermute | solution.py:211
  21.2 50.0 %collective-permute-start.4 = (bf16[4,128,128]{2,1,0:T(8,128)(2,1)}, bf16[4,128,128]{2,1,0:T(8,128)(2,1)}, u32[]{:S(2)}, u32[]{:S(2)}) collective-permute-start(bf16[4,128,128]{2,1,0:T(8,128)(2,1)} %get-tuple-element.49), channel_id=1, source_target_pairs={{0,640},{64,704},{128,768},{192,832},{256,896},{320,960},{384,0},{... | collective-permute-start | bytes 393224 | tf_op jit(solution)/shard_map/ppermute | solution.py:211
  26.8 35.5 %all-to-all-start = ((bf16[2,64,256]{2,0,1:T(2,128)(2,1)}), bf16[2,64,256]{2,0,1:T(2,128)(2,1)S(1)}, u32[]{:S(2)}, u32[]{:S(2)}) async-start(bf16[2,64,256]{2,0,1:T(2,128)(2,1)} %copy.15), calls=%async_computation | async-start | bytes 131072 | tf_op jit(solution)/shard_map/all_to_all | solution.py:203
  62.3 8.9 %collective-permute-start.5 = (bf16[4,128,128]{2,1,0:T(8,128)(2,1)S(1)}, bf16[4,128,128]{2,1,0:T(8,128)(2,1)}, u32[]{:S(2)}, u32[]{:S(2)}) collective-permute-start(bf16[4,128,128]{2,1,0:T(8,128)(2,1)S(1)} %get-tuple-element.48), channel_id=1, source_target_pairs={{0,768},{64,832},{128,896},{192,960},{256,0},{320,64},{384,128},{4... | collective-permute-start | bytes 393224 | tf_op jit(solution)/shard_map/ppermute | solution.py:211
  67.3 8.5 %collective-permute-start.6 = (bf16[4,128,128]{2,1,0:T(8,128)(2,1)S(1)}, bf16[4,128,128]{2,1,0:T(8,128)(2,1)}, u32[]{:S(2)}, u32[]{:S(2)}) collective-permute-start(bf16[4,128,128]{2,1,0:T(8,128)(2,1)S(1)} %get-tuple-element.47), channel_id=1, source_target_pairs={{0,896},{64,960},{128,0},{192,64},{256,128},{320,192},{384,256},{4... | collective-permute-start | bytes 393224 | tf_op jit(solution)/shard_map/ppermute | solution.py:211
  76.8 30.7 %all-to-all-start.1 = ((bf16[8,128,512]{2,1,0:T(8,128)(2,1)}), bf16[8,128,512]{2,1,0:T(8,128)(2,1)S(1)}, u32[]{:S(2)}, u32[]{:S(2)}) async-start(bf16[8,128,512]{2,1,0:T(8,128)(2,1)} %broadcast_in_dim.28), calls=%async_computation.1 | async-start | bytes 2097152 | tf_op jit(solution)/shard_map/all_to_all | solution.py:244
  86.3 30.4 %copy-start.8 = (s32[1,1,2048]{2,1,0:T(1,128)S(1)}, s32[1,1,2048]{2,1,0:T(1,128)}, u32[]{:S(2)}) copy-start(s32[1,1,2048]{2,1,0:T(1,128)} %param.17) | copy-start | bytes 24580
  86.9 29.7 %copy-start.9 = (f32[1,128]{1,0:T(1,128)S(1)}, f32[1,128]{1,0:T(1,128)}, u32[]{:S(2)}) copy-start(f32[1,128]{1,0:T(1,128)} %get-tuple-element.56) | copy-start | bytes 1540
  86.9 29.7 %copy-start.6 = (bf16[128,256]{1,0:T(8,128)(2,1)S(1)}, bf16[128,256]{1,0:T(8,128)(2,1)}, u32[]{:S(2)}) copy-start(bf16[128,256]{1,0:T(8,128)(2,1)} %get-tuple-element.46) | copy-start | bytes 196612
  91.7 25.4 %copy-start = (bf16[512,2048]{1,0:T(8,128)(2,1)S(1)}, bf16[512,2048]{1,0:T(8,128)(2,1)}, u32[]{:S(2)}) copy-start(bf16[512,2048]{1,0:T(8,128)(2,1)} %bag_counts.1.counts_ref) | copy-start | bytes 6291460
  107.5 13.3 %collective-permute-start.7 = (bf16[1024,512]{1,0:T(8,128)(2,1)S(1)}, bf16[1024,512]{1,0:T(8,128)(2,1)S(1)}, u32[]{:S(2)}, u32[]{:S(2)}) collective-permute-start(bf16[1024,512]{1,0:T(8,128)(2,1)S(1)} %bitcast.77), channel_id=1, source_target_pairs={{0,64},{64,0},{128,192},{192,128},{256,320},{320,256},{384,448},{4... | collective-permute-start | bytes 3145736 | tf_op jit(solution)/shard_map/ppermute | solution.py:252
  114.7 6.2 %collective-permute-start.8 = (bf16[8,3,128,128]{3,2,1,0:T(8,128)(2,1)S(1)}, bf16[8,3,128,128]{3,2,1,0:T(8,128)(2,1)S(1)}, u32[]{:S(2)}, u32[]{:S(2)}) collective-permute-start(bf16[8,3,128,128]{3,2,1,0:T(8,128)(2,1)S(1)} %slice.44), channel_id=1, source_target_pairs={{0,64},{64,0},{128,192},{192,128},{256,320},{320,256},{384,448},{4... | collective-permute-start | bytes 2359304 | tf_op jit(solution)/shard_map/ppermute | solution.py:243

commit v2 on v1

--- a/solution.py
+++ b/solution.py
@@ -17,16 +17,20 @@
 BLOCK = 128
 HALF = CHIPS * BLOCK
 
+PACK_FLOPS = 270_000_000
+RANK_FLOPS = 270_000_000
+
+NEAR = CHIPS // 2 - 1
 SAME_CORE = [[chip * CORES + core for chip in range(CHIPS)] for core in range(CORES)]
 SWAP = [(t, t ^ 1) for t in range(CHIPS * CORES)]
 
 
-def shifted(step):
-    return [
-        (chip * CORES + core, (chip + step) % CHIPS * CORES + core)
-        for chip in range(CHIPS)
-        for core in range(CORES)
-    ]
+def both_ways(step):
+    pairs = []
+    for chip in range(CHIPS):
+        pairs.append((chip * CORES, (chip + step) % CHIPS * CORES))
+        pairs.append((chip * CORES + 1, (chip - step) % CHIPS * CORES + 1))
+    return pairs
 
 
 def contract_rows(left, right):
@@ -80,7 +84,8 @@
     first,
     place_ref,
     grads_ref,
-    saved_ref,
+    keep_ref,
+    taken_ref,
     counts_ref,
     inverse_ref,
     comp_ref,
@@ -94,22 +99,34 @@
     else:
         before, refs = refs[:5], refs[5:]
     out_refs, (crossed_ref, scale_ref, split_ref, low_flat, x_flat, counts_flat) = refs[:5], refs[5:]
-    core = place_ref[0]
-    chip = place_ref[1]
-    if not first:
-        core = 1 - core
+    mine, chip = place_ref[0], place_ref[1]
+    core = mine if first else 1 - mine
 
     @pl.loop(0, CHIPS)
     def _(k):
         rows = pl.ds(pl.multiple_of(k * BLOCK, BLOCK), BLOCK)
         block = k * CORES + core
-        at = lax.rem(chip - k + CHIPS, CHIPS)
-        x = saved_ref[at, 0]
-        low = jnp.concatenate(
-            [saved_ref[at, saved_ref.shape[1] - 2], saved_ref[at, saved_ref.shape[1] - 1]], axis=1
-        )
-        low_flat[rows, :] = low
-        x_flat[rows, :] = x
+        way = lax.rem((chip - k) * (1 - 2 * mine) + CHIPS, CHIPS)
+        given = (way > CHIPS // 2) | ((lax.rem(way, CHIPS // 2) == 0) & (core != mine))
+        near = jnp.where(way > CHIPS // 2, CHIPS - way, way)
+        holder = jnp.where(given, 1 - mine, mine)
+        inner = 2 * near - 1 + jnp.where(core == holder, 0, 1)
+        at = jnp.where(near == 0, 0, jnp.where(near == CHIPS // 2, CHIPS - 1, inner))
+
+        @pl.when(given)
+        def _():
+            x_flat[rows, :] = taken_ref[at, 2]
+            low_flat[rows, :BLOCK] = taken_ref[at, 0]
+            low_flat[rows, BLOCK:] = taken_ref[at, 1]
+
+        @pl.when(jnp.logical_not(given))
+        def _():
+            x_flat[rows, :] = keep_ref[at, 0]
+            low_flat[rows, :BLOCK] = keep_ref[at, 1]
+            low_flat[rows, BLOCK:] = keep_ref[at, 2]
+
+        x = x_flat[rows, :]
+        low = low_flat[rows, :]
         out_grad = grads_ref[rows, :COMP]
         rank_grad = grads_ref[rows, COMP:]
         cross = contract_cols(out_grad, comp_ref[...])
@@ -142,17 +159,16 @@
         ref[...] = term
 
 
-def half(place, grads, saved, counts, inverse, weights, before=None):
+def half(place, grads, keep, taken, counts, inverse, weights, before=None):
     first = before is None
     shapes = [(EMBED, RANK), (EMBED, RANK), (1, EMBED), (EMBED, COMP), (TABLE_ROWS, EMBED)]
     if not first:
         shapes[1] = (RANK, EMBED)
-    whole = pl.BlockSpec(memory_space=pltpu.VMEM)
-    operands = [grads, saved, counts, inverse, *weights] + ([] if first else list(before))
+    operands = [grads, keep, taken, counts, inverse, *weights] + ([] if first else list(before))
     return pl.pallas_call(
         functools.partial(half_kernel, first),
-        in_specs=[pl.BlockSpec(memory_space=pltpu.SMEM)] + [whole] * len(operands),
-        out_specs=[whole] * 5,
+        in_specs=[SCALARS] + [WHOLE] * len(operands),
+        out_specs=[WHOLE] * 5,
         out_shape=[jax.ShapeDtypeStruct(shape, jnp.float32) for shape in shapes],
         scratch_shapes=[
             pltpu.VMEM((HALF, EMBED), jnp.bfloat16),
@@ -170,31 +186,112 @@
     )(place, *operands)
 
 
-def pack_kernel(place_ref, x_ref, down_ref, blocks_ref):
+def pack_kernel(place_ref, x_ref, partner_ref, down_ref, self_ref, near_ref, far_ref):
     core, chip = place_ref[0], place_ref[1]
-    low = product(x_ref[...], down_ref[...]).astype(jnp.bfloat16)
-    for step in range(CHIPS):
-        base = lax.rem(chip + step, CHIPS) * CORES
-        for turn in range(CORES):
-            slot = base + (core if turn == 0 else 1 - core)
-            blocks_ref[step, turn] = x_ref[:, pl.ds(pl.multiple_of(slot * EMBED, EMBED), EMBED)]
-        blocks_ref[step, 2] = low[:, :BLOCK]
-        blocks_ref[step, 3] = low[:, BLOCK:]
-
-
-def pack(place, inputs, down_mat):
-    whole = pl.BlockSpec(memory_space=pltpu.VMEM)
+    way = 1 - 2 * core
+    sides = []
+    for ref in (x_ref, partner_ref):
+        low = product(ref[...], down_ref[...]).astype(jnp.bfloat16)
+        sides.append((ref, low))
+
+    def fill(step, side, put):
+        ref, low = sides[side]
+        base = lax.rem(chip + way * step + CHIPS, CHIPS) * CORES
+        for part, slot in ((0, base + core), (3, base + 1 - core)):
+            put(part, ref[:, pl.ds(pl.multiple_of(slot * EMBED, EMBED), EMBED)])
+        put(1, low[:, :BLOCK])
+        put(2, low[:, BLOCK:])
+
+    def put_self(part, value):
+        self_ref[part] = value
+
+    def put_far(part, value):
+        far_ref[part] = value
+
+    fill(0, 0, put_self)
+    fill(CHIPS // 2, 0, put_far)
+    for step in range(1, NEAR + 1):
+        for side in range(2):
+
+            def put_near(part, value, step=step, side=side):
+                near_ref[step - 1, side, part] = value
+
+            fill(step, side, put_near)
+
+
+WHOLE = pl.BlockSpec(memory_space=pltpu.VMEM)
+SCALARS = pl.BlockSpec(memory_space=pltpu.SMEM)
+
+
+def pack(place, inputs, partner, down_mat):
+    tile = (4, BLOCK, EMBED)
     return pl.pallas_call(
         pack_kernel,
-        in_specs=[pl.BlockSpec(memory_space=pltpu.SMEM), whole, whole],
-        out_specs=whole,
-        out_shape=jax.ShapeDtypeStruct((CHIPS, 4, BLOCK, EMBED), jnp.bfloat16),
+        in_specs=[SCALARS, WHOLE, WHOLE, WHOLE],
+        out_specs=[WHOLE] * 3,
+        out_shape=[
+            jax.ShapeDtypeStruct(tile, jnp.bfloat16),
+            jax.ShapeDtypeStruct((NEAR, 2, *tile), jnp.bfloat16),
+            jax.ShapeDtypeStruct(tile, jnp.bfloat16),
+        ],
         compiler_params=pltpu.CompilerParams(vmem_limit_bytes=16 * 1024 * 1024),
         cost_estimate=pl.CostEstimate(
-            flops=140_000_000, bytes_accessed=2_600_000, transcendentals=0
+            flops=PACK_FLOPS, bytes_accessed=3_000_000, transcendentals=0
         ),
         name="low_rank_and_columns",
-    )(place, inputs, down_mat)
+    )(place, inputs, partner, down_mat)
+
+
+def merge_kernel(self_ref, first_ref, second_ref, third_ref, far_ref, keep_ref, give_ref):
+    blocks = [self_ref]
+    for ref in (first_ref, second_ref, third_ref):
+        blocks += [ref.at[0], ref.at[1]]
+    blocks.append(far_ref)
+    for index, block in enumerate(blocks):
+        keep_ref[index] = block[0:3]
+        give_ref[index] = block[1:4]
+
+
+def merge(blocks):
+    shape = jax.ShapeDtypeStruct((CHIPS, 3, BLOCK, EMBED), jnp.bfloat16)
+    return pl.pallas_call(
+        merge_kernel,
+        in_specs=[WHOLE] * 5,
+        out_specs=[WHOLE] * 2,
+        out_shape=[shape, shape],
+        compiler_params=pltpu.CompilerParams(vmem_limit_bytes=16 * 1024 * 1024),
+        cost_estimate=pl.CostEstimate(flops=0, bytes_accessed=3_000_000, transcendentals=0),
+        name="merge_rows",
+    )(*blocks)
+
+
+def rank_kernel(grad_ref, x_ref, comp_ref, up_ref, out_ref):
+    out_grad = grad_ref[...]
+    total = jnp.zeros((BLOCK, RANK), jnp.float32)
+    width = 512
+    for start in range(0, x_ref.shape[1], width):
+        columns = pl.ds(start, width)
+        cross = contract_cols(out_grad, comp_ref[columns, :])
+        scale_grad = (cross * x_ref[:, columns].astype(jnp.float32)).astype(jnp.bfloat16)
+        total += contract_cols(scale_grad, up_ref[:, columns])
+    rank_grad = total.astype(jnp.bfloat16)
+    for chip in range(CHIPS):
+        out_ref[chip, :, :COMP] = out_grad
+        out_ref[chip, :, COMP:] = rank_grad
+
+
+def rank_rows(out_grad, inputs, comp_mat, up_mat):
+    return pl.pallas_call(
+        rank_kernel,
+        in_specs=[WHOLE] * 4,
+        out_specs=WHOLE,
+        out_shape=jax.ShapeDtypeStruct((CHIPS, BLOCK, COMP + RANK), jnp.bfloat16),
+        compiler_params=pltpu.CompilerParams(vmem_limit_bytes=16 * 1024 * 1024),
+        cost_estimate=pl.CostEstimate(
+            flops=RANK_FLOPS, bytes_accessed=3_600_000, transcendentals=0
+        ),
+        name="rank_grad_rows",
+    )(out_grad, inputs, comp_mat, up_mat)
 
 
 def on_device(
@@ -206,10 +303,12 @@
     place = jnp.stack([me & 1, me >> 1]).astype(jnp.int32)
     inputs, down_mat, up_mat, comp_mat = pooled_in[0], w_down[0], w_up[0], w_comp[0]
 
-    packed = pack(place, inputs, down_mat)
-    arrived_blocks = [packed[0]] + [
-        lax.ppermute(packed[step], "tower", shifted(step)) for step in range(1, CHIPS)
+    partner = lax.ppermute(inputs, "tower", SWAP)
+    blocks, near, far = pack(place, inputs, partner, down_mat)
+    received = [
+        lax.ppermute(near[step - 1], "tower", both_ways(step)) for step in range(1, NEAR + 1)
     ]
+    received.append(lax.ppermute(far, "tower", both_ways(CHIPS // 2)))
 
     counts = bag_counts(jnp.transpose(bag_ids[0, 0]), bag_lengths[0])
     inverse = jnp.broadcast_to(
@@ -233,16 +332,12 @@
         lax.dynamic_slice_in_dim(down_mat, slot * EMBED, EMBED, 0),
     )
 
-    cross_grad = contract_cols(out_grad, comp_mat)
-    scale_grad = (cross_grad * inputs.astype(jnp.float32)).astype(jnp.bfloat16)
-    rank_grad = contract_cols(scale_grad, up_mat).astype(jnp.bfloat16)
-
-    both = jnp.concatenate([out_grad, rank_grad], axis=1)
-    both, *arrived_blocks = lax.optimization_barrier((both, *arrived_blocks))
-    own = jnp.stack(arrived_blocks)
-    other = lax.ppermute(own[:, 1:], "tower", SWAP)
+    rows_out = rank_rows(out_grad, inputs, comp_mat, up_mat)
+    rows_out, *received = lax.optimization_barrier((rows_out, *received))
+    keep, give = merge([blocks, *received])
+    taken = lax.ppermute(give, "tower", SWAP)
     grads_own = lax.all_to_all(
-        jnp.broadcast_to(both[None], (CHIPS, BLOCK, COMP + RANK)),
+        rows_out,
         "tower",
         split_axis=0,
         concat_axis=0,
@@ -251,9 +346,9 @@
     ).reshape(HALF, COMP + RANK)
     grads_other = lax.ppermute(grads_own, "tower", SWAP)
 
-    first = half(place, grads_own, own, counts, inverse, weights)
+    first = half(place, grads_own, keep, taken, counts, inverse, weights)
     grad_down, grad_up, grad_bias, grad_comp, tables = half(
-        place, grads_other, other, counts, inverse, weights, first
+        place, grads_other, keep, taken, counts, inverse, weights, first
     )
     return grad_down[None], grad_up[None], grad_bias, grad_comp[None], tables[None, None]
 

time: 126 us -> 127 us (level)
  waiting for transfers between devices: 25.1 us -> 36.2 us
  starting transfers between devices: 61 us -> 54 us
  local copies, waits for them, and re-layouts: 21 us -> 14.3 us
  Pallas kernels: 14.4 us -> 19.5 us
    all_to_all x1, waiting for transfers between devices: 11 us -> 26.9 us  [on_device(): lax.all_to_all(rows_out, 'tower', split_axis=0, concat_axis=0, tiled=True...]
    all_to_all x1, starting transfers between devices: 21.9 us -> 9.3 us  [on_device(): lax.all_to_all(top_grad, 'hst', split_axis=1, concat_axis=0, tiled=True)]
    all_to_all x1, waiting for transfers between devices: 9.46 us -> 0.01 us  [on_device(): lax.all_to_all(top_grad, 'hst', split_axis=1, concat_axis=0, tiled=True)]
    pallas_call x3 -> x5, Pallas kernels: 8.58 us -> 13.6 us  [the longest x2 8.05 us: half(): pl.pallas_call(functools.partial(half_kernel, first), in_specs=[SCALARS]...]
    ppermute x8 -> x6, waiting for transfers between devices: 4.59 us -> 9.27 us  [the longest x1 8.1 us: on_device(): received.append(lax.ppermute(far, 'tower', both_ways(CHIPS // 2)))]
    ppermute x8 -> x6, starting transfers between devices: 31.2 us -> 35.2 us  [the longest x1 16.1 us: on_device(): partner = lax.ppermute(inputs, 'tower', SWAP)]
    all_to_all x1, starting transfers between devices: 3.56 us -> 7.04 us  [on_device(): lax.all_to_all(rows_out, 'tower', split_axis=0, concat_axis=0, tiled=True...]
    ppermute x1, starting transfers between devices: 4.37 us -> 2.39 us  [on_device(): grads_other = lax.ppermute(grads_own, 'tower', SWAP)]
  transfers between devices with their start and end apart: 11 -> 9, of which waited for: 3 -> 3; matrix products, arithmetic and copies ran while one was open for 15% -> 4% of each run, Pallas kernels for 8% -> 12%
where the time goes in v2:
time: 127 us; the launch traced here: 126 us
  starting transfers between devices  54 us (43%)
  waiting for transfers between devices  36.2 us (29%)
  Pallas kernels  19.5 us (15%)
  local copies, waits for them, and re-layouts  14.3 us (11%)
  between operations  1.51 us (1%)
    all_to_all x1, waiting for transfers between devices, on_device(): lax.all_to_all(rows_out, 'tower', split_axis=0, concat_axis=0, tiled=True...  26.9 us
    ppermute x1, starting transfers between devices, on_device(): partner = lax.ppermute(inputs, 'tower', SWAP)  16.1 us
    ppermute x3, starting transfers between devices, on_device(): lax.ppermute(near[step - 1], 'tower', both_ways(step))  11.6 us
    unnamed x33, local copies, waits for them, and re-layouts  11.4 us
    all_to_all x1, starting transfers between devices, on_device(): lax.all_to_all(top_grad, 'hst', split_axis=1, concat_axis=0, tiled=True)  9.3 us
    ppermute x1, waiting for transfers between devices, on_device(): received.append(lax.ppermute(far, 'tower', both_ways(CHIPS // 2)))  8.1 us
    pallas_call x2, Pallas kernels, half(): pl.pallas_call(functools.partial(half_kernel, first), in_specs=[SCALARS]...  8.05 us
    all_to_all x1, starting transfers between devices, on_device(): lax.all_to_all(rows_out, 'tower', split_axis=0, concat_axis=0, tiled=True...  7.04 us
  transfers between devices with their start and end apart: 9, of which 3 were waited for; matrix products, arithmetic and copies ran while one was open for 4% of the time, Pallas kernels for 12%

profile of v2, /device:TPU:1, one launch (start us, length us, event | category | flops | bytes accessed | tf_op | source)
XLA Modules:
  0.0 126.2 jit_solution(1096195506643194292)
XLA Ops:
  0.6 16.1 %collective-permute-start = (bf16[128,2048]{1,0:T(8,128)(2,1)}, bf16[128,2048]{1,0:T(8,128)(2,1)S(1)}, u32[]{:S(2)}, u32[]{:S(2)}) collective-permute-start(bf16[128,2048]{1,0:T(8,128)(2,1)} %bitcast.43), channel_id=1, source_target_pairs={{0,64},{64,0},{128,192},{192,128},{256,320},{320,256},{384,448},{4... | collective-permute-start | bytes 1572872 | tf_op jit(solution)/shard_map/ppermute | solution.py:306
  16.7 1.5 %copy.15 = bf16[2,64,256]{2,0,1:T(2,128)(2,1)} copy(bf16[2,64,256]{2,1,0:T(8,128)(2,1)} %param.9) | data formatting | bytes 131072 | tf_op args[0]
  18.2 9.3 %all-to-all-start = ((bf16[2,64,256]{2,0,1:T(2,128)(2,1)}), bf16[2,64,256]{2,0,1:T(2,128)(2,1)S(1)}, u32[]{:S(2)}, u32[]{:S(2)}) async-start(bf16[2,64,256]{2,0,1:T(2,128)(2,1)} %copy.15), calls=%async_computation | async-start | bytes 131072 | tf_op jit(solution)/shard_map/all_to_all | solution.py:300
  27.6 0.1 pad_add_fusion.place_ref
  27.6 0.0 collective-permute-done.partner_ref
  27.6 0.0 copy-start.6
  27.6 0.8 copy-done.6
  28.4 0.0 copy-start.1
  28.4 1.0 copy-done.1
  29.5 0.0 copy-start.5
  29.5 1.2 copy-done.5
  30.7 0.0 copy-start.7
  30.7 1.0 copy-done.7
  31.7 0.0 copy-start.2
  31.7 0.0 copy-start.3
  31.7 0.0 copy-start.4
  31.7 1.7 %low_rank_and_columns.1 = (bf16[4,128,128]{2,1,0:T(8,128)(2,1)S(1)}, bf16[3,2,4,128,128]{4,3,2,1,0:T(8,128)(2,1)S(1)}, bf16[4,128,128]{2,1,0:T(8,128)(2,1)}) custom-call(s32[2]{0:T(128)S(1)} %pad_add_fusion.place_ref, bf16[128,2048]{1,0:T(8,128)(2,1)S(1)} %bitcast.44, bf16[128,2048]{1,0:T(8,128)(2,1)S(1)} %copy-done.7, bf16[2048,256]{1,0:T(8,128)(2,1)S(1)} %bitcast.48), custom_call_target="tpu_custom_call" | custom-call | flops 270000000 | bytes 3000000 | tf_op jit(solution)/shard_map/low_rank_and_columns/pallas_call | solution.py:228
  33.4 0.0 copy-start.10
  33.4 1.0 slice_bitcast_fusion
  34.4 6.7 %collective-permute-start.3 = (bf16[2,4,128,128]{3,2,1,0:T(8,128)(2,1)}, bf16[2,4,128,128]{3,2,1,0:T(8,128)(2,1)S(1)}, u32[]{:S(2)}, u32[]{:S(2)}) collective-permute-start(bf16[2,4,128,128]{3,2,1,0:T(8,128)(2,1)} %get-tuple-element.49), channel_id=1, source_target_pairs={{0,384},{64,704},{128,512},{192,832},{256,640},{320,960},{384,768}... | collective-permute-start | bytes 786440 | tf_op jit(solution)/shard_map/ppermute | solution.py:309
  41.0 0.0 copy-done.10
  41.1 2.9 %collective-permute-start.2 = (bf16[2,4,128,128]{3,2,1,0:T(8,128)(2,1)}, bf16[2,4,128,128]{3,2,1,0:T(8,128)(2,1)S(1)}, u32[]{:S(2)}, u32[]{:S(2)}) collective-permute-start(bf16[2,4,128,128]{3,2,1,0:T(8,128)(2,1)} %get-tuple-element.50), channel_id=1, source_target_pairs={{0,256},{64,832},{128,384},{192,960},{256,512},{320,64},{384,640},... | collective-permute-start | bytes 786440 | tf_op jit(solution)/shard_map/ppermute | solution.py:309
  43.9 2.1 %collective-permute-start.1 = (bf16[2,4,128,128]{3,2,1,0:T(8,128)(2,1)}, bf16[2,4,128,128]{3,2,1,0:T(8,128)(2,1)}, u32[]{:S(2)}, u32[]{:S(2)}) collective-permute-start(bf16[2,4,128,128]{3,2,1,0:T(8,128)(2,1)} %get-tuple-element.51), channel_id=1, source_target_pairs={{0,128},{64,960},{128,256},{192,64},{256,384},{320,192},{384,512},... | collective-permute-start | bytes 786440 | tf_op jit(solution)/shard_map/ppermute | solution.py:309
  46.0 5.7 %collective-permute-start.4 = (bf16[4,128,128]{2,1,0:T(8,128)(2,1)}, bf16[4,128,128]{2,1,0:T(8,128)(2,1)S(1)}, u32[]{:S(2)}, u32[]{:S(2)}) collective-permute-start(bf16[4,128,128]{2,1,0:T(8,128)(2,1)} %get-tuple-element.26), channel_id=1, source_target_pairs={{0,512},{64,576},{128,640},{192,704},{256,768},{320,832},{384,896}... | collective-permute-start | bytes 393224 | tf_op jit(solution)/shard_map/ppermute | solution.py:311
  51.7 0.0 all-to-all-done
  51.7 0.0 copy-done.2
  51.7 0.0 copy-done.3
  51.7 0.0 copy-done.4
  51.7 0.0 copy-start.15
  51.8 2.0 %rank_grad_rows.1 = bf16[8,128,512]{2,1,0:T(8,128)(2,1)} custom-call(bf16[128,256]{1,0:T(8,128)(2,1)S(1)} %reshape.39.grad_ref, bf16[128,2048]{1,0:T(8,128)(2,1)S(1)} %bitcast.45, bf16[2048,256]{1,0:T(8,128)(2,1)S(1)} %bitcast.47, bf16[256,2048]{1,0:T(8,128)(2,1)S(1)} %bitcast.46), custom_call_target="tpu_custom_call" | custom-call | flops 270000000 | bytes 3600000 | tf_op jit(solution)/shard_map/rank_grad_rows/pallas_call | solution.py:284
  53.7 8.1 %collective-permute-done.4.far_ref = bf16[4,128,128]{2,1,0:T(8,128)(2,1)S(1)} collective-permute-done((bf16[4,128,128]{2,1,0:T(8,128)(2,1)}, bf16[4,128,128]{2,1,0:T(8,128)(2,1)S(1)}, u32[]{:S(2)}, u32[]{:S(2)}) %collective-permute-start.4) | collective-permute-done | bytes 131104 | tf_op jit(solution)/shard_map/ppermute | solution.py:311
  61.8 0.0 copy-start.12
  61.8 0.7 copy-done.12
  62.5 0.0 collective-permute-done.3.third_ref
  62.5 0.0 collective-permute-done.2.second_ref
  62.5 0.0 copy-start.8
  62.5 0.7 copy-done.8
  63.2 1.2 collective-permute-done.1.first_ref
  64.4 7.0 %all-to-all-start.1 = ((bf16[8,128,512]{2,1,0:T(8,128)(2,1)}), bf16[8,128,512]{2,1,0:T(8,128)(2,1)S(1)}, u32[]{:S(2)}, u32[]{:S(2)}) async-start(bf16[8,128,512]{2,1,0:T(8,128)(2,1)} %rank_grad_rows.1), calls=%async_computation.1 | async-start | bytes 2097152 | tf_op jit(solution)/shard_map/all_to_all | solution.py:339
  71.4 0.0 copy-done.15
  71.4 0.6 fusion
  72.7 0.8 dynamic-slice_bitcast_fusion.down_ref
  73.6 26.9 %all-to-all-done.1 = bf16[8,128,512]{2,1,0:T(8,128)(2,1)S(1)} async-done(((bf16[8,128,512]{2,1,0:T(8,128)(2,1)}), bf16[8,128,512]{2,1,0:T(8,128)(2,1)S(1)}, u32[]{:S(2)}, u32[]{:S(2)}) %all-to-all-start.1) | async-done | bytes 1048608 | tf_op jit(solution)/shard_map/all_to_all | solution.py:339
  100.6 2.4 %collective-permute-start.5 = (bf16[1024,512]{1,0:T(8,128)(2,1)S(1)}, bf16[1024,512]{1,0:T(8,128)(2,1)}, u32[]{:S(2)}, u32[]{:S(2)}) collective-permute-start(bf16[1024,512]{1,0:T(8,128)(2,1)S(1)} %bitcast.41), channel_id=1, source_target_pairs={{0,64},{64,0},{128,192},{192,128},{256,320},{320,256},{384,448},{4... | collective-permute-start | bytes 3145736 | tf_op jit(solution)/shard_map/ppermute | solution.py:347
  103.0 0.7 constant_dynamic-slice_fusion.1
  103.7 0.0 copy-start.9
  103.7 0.9 copy-done.9
  104.6 0.0 copy-start.11
  104.6 0.9 copy-done.11
  105.5 0.0 copy-start.13
  105.5 0.9 copy-done.13
  106.4 1.9 %merge_rows.1 = (bf16[8,3,128,128]{3,2,1,0:T(8,128)(2,1)S(1)}, bf16[8,3,128,128]{3,2,1,0:T(8,128)(2,1)}) custom-call(bf16[4,128,128]{2,1,0:T(8,128)(2,1)S(1)} %copy-done.11, bf16[2,4,128,128]{3,2,1,0:T(8,128)(2,1)} %collective-permute-done.1.first_ref, bf16[2,4,128,128]{3,2,1,0:T(8,128)(2,1)S(1)} %copy-done.9, ...), custom_call_target="tpu_custom_call" | custom-call | bytes 3000000 | tf_op jit(solution)/shard_map/merge_rows/pallas_call | solution.py:257
  108.3 1.9 %collective-permute-start.6 = (bf16[8,3,128,128]{3,2,1,0:T(8,128)(2,1)}, bf16[8,3,128,128]{3,2,1,0:T(8,128)(2,1)S(1)}, u32[]{:S(2)}, u32[]{:S(2)}) collective-permute-start(bf16[8,3,128,128]{3,2,1,0:T(8,128)(2,1)} %get-tuple-element.34), channel_id=1, source_target_pairs={{0,64},{64,0},{128,192},{192,128},{256,320},{320,256},{384,448},{4... | collective-permute-start | bytes 2359304 | tf_op jit(solution)/shard_map/ppermute | solution.py:338
  110.3 0.0 copy-start.14
  110.3 5.9 %bag_counts.1.counts_ref = bf16[512,2048]{1,0:T(8,128)(2,1)} custom-call(s32[8,2048]{1,0:T(8,128)} %bitcast.56, s32[1,2048]{1,0:T(1,128)} %bitcast.51), custom_call_target="tpu_custom_call" | custom-call | flops 3000000000 | bytes 3000000 | tf_op jit(solution)/shard_map/bag_counts/pallas_call | solution.py:67
  116.1 0.0 copy-done.14
  116.1 0.0 collective-permute-done.6.taken_ref
  116.2 0.3 broadcast_in_dim.22.inverse_ref
  116.5 0.0 copy-start
  116.5 1.6 %copy-done = bf16[512,2048]{1,0:T(8,128)(2,1)S(1)} copy-done((bf16[512,2048]{1,0:T(8,128)(2,1)S(1)}, bf16[512,2048]{1,0:T(8,128)(2,1)}, u32[]{:S(2)}) %copy-start) | copy-done | bytes 2097176
  118.1 3.3 %column_half_first.1 = (f32[128,256]{1,0:T(8,128)S(1)}, f32[128,256]{1,0:T(8,128)S(1)}, f32[1,128]{1,0:T(1,128)S(1)}, f32[128,256]{1,0:T(8,128)S(1)}, f32[512,128]{1,0:T(8,128)S(1)}) custom-call(s32[2]{0:T(128)S(1)} %pad_add_fusion.place_ref, bf16[1024,512]{1,0:T(8,128)(2,1)S(1)} %bitcast.42, bf16[8,3,128,128]{3,2,1,0:T(8,128)(2,1)S(1)} %get-tuple-element.33.keep_ref, ...), custom_call_target="tpu_custom_call" | custom-call | flops 1500000000 | bytes 6000000 | tf_op jit(solution)/shard_map/column_half_first/pallas_call | solution.py:168
  121.4 0.0 collective-permute-done.5.grads_ref
  121.4 4.8 %column_half_second.1 = (f32[128,256]{1,0:T(8,128)}, f32[256,128]{1,0:T(8,128)}, f32[1,128]{1,0:T(1,128)}, f32[128,256]{1,0:T(8,128)}, f32[512,128]{1,0:T(8,128)}) custom-call(s32[2]{0:T(128)S(1)} %pad_add_fusion.place_ref, bf16[1024,512]{1,0:T(8,128)(2,1)} %collective-permute-done.5.grads_ref, bf16[8,3,128,128]{3,2,1,0:T(8,128)(2,1)S(1)} %get-tuple-element.33.keep_ref, ...), custom_call_target="tpu_custom_call" | custom-call | flops 1500000000 | bytes 6000000 | tf_op jit(solution)/shard_map/column_half_second/pallas_call | solution.py:168
  (6 shorter events, 0.1 us)
Async XLA Ops:
  0.6 27.0 %collective-permute-start = (bf16[128,2048]{1,0:T(8,128)(2,1)}, bf16[128,2048]{1,0:T(8,128)(2,1)S(1)}, u32[]{:S(2)}, u32[]{:S(2)}) collective-permute-start(bf16[128,2048]{1,0:T(8,128)(2,1)} %bitcast.43), channel_id=1, source_target_pairs={{0,64},{64,0},{128,192},{192,128},{256,320},{320,256},{384,448},{4... | collective-permute-start | bytes 1572872 | tf_op jit(solution)/shard_map/ppermute | solution.py:306
  18.2 33.4 %all-to-all-start = ((bf16[2,64,256]{2,0,1:T(2,128)(2,1)}), bf16[2,64,256]{2,0,1:T(2,128)(2,1)S(1)}, u32[]{:S(2)}, u32[]{:S(2)}) async-start(bf16[2,64,256]{2,0,1:T(2,128)(2,1)} %copy.15), calls=%async_computation | async-start | bytes 131072 | tf_op jit(solution)/shard_map/all_to_all | solution.py:300
  27.6 0.8 copy-start.6
  28.4 1.0 copy-start.1
  29.5 1.2 copy-start.5
  30.7 1.0 copy-start.7
  31.7 20.0 %copy-start.2 = (bf16[1,128,2048]{2,1,0:T(8,128)(2,1)S(1)}, bf16[1,128,2048]{2,1,0:T(8,128)(2,1)}, u32[]{:S(2)}) copy-start(bf16[1,128,2048]{2,1,0:T(8,128)(2,1)} %param.10) | copy-start | bytes 1572868
  31.7 20.0 %copy-start.3 = (bf16[1,256,2048]{2,1,0:T(8,128)(2,1)S(1)}, bf16[1,256,2048]{2,1,0:T(8,128)(2,1)}, u32[]{:S(2)}) copy-start(bf16[1,256,2048]{2,1,0:T(8,128)(2,1)} %param.12) | copy-start | bytes 3145732
  31.7 20.0 %copy-start.4 = (bf16[1,2048,256]{2,1,0:T(8,128)(2,1)S(1)}, bf16[1,2048,256]{2,1,0:T(8,128)(2,1)}, u32[]{:S(2)}) copy-start(bf16[1,2048,256]{2,1,0:T(8,128)(2,1)} %param.14) | copy-start | bytes 3145732
  33.4 7.6 %copy-start.10 = (bf16[4,128,128]{2,1,0:T(8,128)(2,1)}, bf16[4,128,128]{2,1,0:T(8,128)(2,1)S(1)}, u32[]{:S(2)}) copy-start(bf16[4,128,128]{2,1,0:T(8,128)(2,1)S(1)} %get-tuple-element.28.self_ref) | copy-start | bytes 393220
  34.4 28.1 %collective-permute-start.3 = (bf16[2,4,128,128]{3,2,1,0:T(8,128)(2,1)}, bf16[2,4,128,128]{3,2,1,0:T(8,128)(2,1)S(1)}, u32[]{:S(2)}, u32[]{:S(2)}) collective-permute-start(bf16[2,4,128,128]{3,2,1,0:T(8,128)(2,1)} %get-tuple-element.49), channel_id=1, source_target_pairs={{0,384},{64,704},{128,512},{192,832},{256,640},{320,960},{384,768}... | collective-permute-start | bytes 786440 | tf_op jit(solution)/shard_map/ppermute | solution.py:309
  41.1 21.4 %collective-permute-start.2 = (bf16[2,4,128,128]{3,2,1,0:T(8,128)(2,1)}, bf16[2,4,128,128]{3,2,1,0:T(8,128)(2,1)S(1)}, u32[]{:S(2)}, u32[]{:S(2)}) collective-permute-start(bf16[2,4,128,128]{3,2,1,0:T(8,128)(2,1)} %get-tuple-element.50), channel_id=1, source_target_pairs={{0,256},{64,832},{128,384},{192,960},{256,512},{320,64},{384,640},... | collective-permute-start | bytes 786440 | tf_op jit(solution)/shard_map/ppermute | solution.py:309
  43.9 20.4 %collective-permute-start.1 = (bf16[2,4,128,128]{3,2,1,0:T(8,128)(2,1)}, bf16[2,4,128,128]{3,2,1,0:T(8,128)(2,1)}, u32[]{:S(2)}, u32[]{:S(2)}) collective-permute-start(bf16[2,4,128,128]{3,2,1,0:T(8,128)(2,1)} %get-tuple-element.51), channel_id=1, source_target_pairs={{0,128},{64,960},{128,256},{192,64},{256,384},{320,192},{384,512},... | collective-permute-start | bytes 786440 | tf_op jit(solution)/shard_map/ppermute | solution.py:309
  46.0 15.8 %collective-permute-start.4 = (bf16[4,128,128]{2,1,0:T(8,128)(2,1)}, bf16[4,128,128]{2,1,0:T(8,128)(2,1)S(1)}, u32[]{:S(2)}, u32[]{:S(2)}) collective-permute-start(bf16[4,128,128]{2,1,0:T(8,128)(2,1)} %get-tuple-element.26), channel_id=1, source_target_pairs={{0,512},{64,576},{128,640},{192,704},{256,768},{320,832},{384,896}... | collective-permute-start | bytes 393224 | tf_op jit(solution)/shard_map/ppermute | solution.py:311
  51.7 19.6 %copy-start.15 = (s32[1,16]{1,0:T(1,128)S(1)}, s32[1,16]{1,0:T(1,128)}, u32[]{:S(2)}) copy-start(s32[1,16]{1,0:T(1,128)} %param.15) | copy-start | bytes 196
  61.8 0.7 copy-start.12
  62.5 0.7 copy-start.8
  64.4 36.2 %all-to-all-start.1 = ((bf16[8,128,512]{2,1,0:T(8,128)(2,1)}), bf16[8,128,512]{2,1,0:T(8,128)(2,1)S(1)}, u32[]{:S(2)}, u32[]{:S(2)}) async-start(bf16[8,128,512]{2,1,0:T(8,128)(2,1)} %rank_grad_rows.1), calls=%async_computation.1 | async-start | bytes 2097152 | tf_op jit(solution)/shard_map/all_to_all | solution.py:339
  100.6 20.8 %collective-permute-start.5 = (bf16[1024,512]{1,0:T(8,128)(2,1)S(1)}, bf16[1024,512]{1,0:T(8,128)(2,1)}, u32[]{:S(2)}, u32[]{:S(2)}) collective-permute-start(bf16[1024,512]{1,0:T(8,128)(2,1)S(1)} %bitcast.41), channel_id=1, source_target_pairs={{0,64},{64,0},{128,192},{192,128},{256,320},{320,256},{384,448},{4... | collective-permute-start | bytes 3145736 | tf_op jit(solution)/shard_map/ppermute | solution.py:347
  103.7 0.9 copy-start.9
  104.6 0.9 copy-start.11
  105.5 0.9 copy-start.13
  108.3 7.8 %collective-permute-start.6 = (bf16[8,3,128,128]{3,2,1,0:T(8,128)(2,1)}, bf16[8,3,128,128]{3,2,1,0:T(8,128)(2,1)S(1)}, u32[]{:S(2)}, u32[]{:S(2)}) collective-permute-start(bf16[8,3,128,128]{3,2,1,0:T(8,128)(2,1)} %get-tuple-element.34), channel_id=1, source_target_pairs={{0,64},{64,0},{128,192},{192,128},{256,320},{320,256},{384,448},{4... | collective-permute-start | bytes 2359304 | tf_op jit(solution)/shard_map/ppermute | solution.py:338
  110.3 5.9 %copy-start.14 = (s32[1,1,2048]{2,1,0:T(1,128)S(1)}, s32[1,1,2048]{2,1,0:T(1,128)}, u32[]{:S(2)}) copy-start(s32[1,1,2048]{2,1,0:T(1,128)} %param.17) | copy-start | bytes 24580
  116.5 1.6 %copy-start = (bf16[512,2048]{1,0:T(8,128)(2,1)S(1)}, bf16[512,2048]{1,0:T(8,128)(2,1)}, u32[]{:S(2)}) copy-start(bf16[512,2048]{1,0:T(8,128)(2,1)} %bag_counts.1.counts_ref) | copy-start | bytes 6291460

commit v3 on v0

v3 whole, which is shorter than its diff:
```python
import jax
import jax.numpy as jnp
from jax import lax
from jax.experimental import pallas as pl
from jax.experimental.pallas import tpu as pltpu
from jax.sharding import PartitionSpec as P

EMBED = 128
COMP = 256
RANK = 256
TABLE_ROWS = 512
SLOTS = 8
CHIPS = 8
CORES = 2
BLOCK = 128
HALF = CHIPS * BLOCK

STEPS = 4
ROOM = 60 * 1024 * 1024
PACK_FLOPS = 270_000_000
RANK_FLOPS = 270_000_000

NEAR = CHIPS // 2 - 1
SAME_CORE = [[chip * CORES + core for chip in range(CHIPS)] for core in range(CORES)]
SWAP = [(t, t ^ 1) for t in range(CHIPS * CORES)]


def both_ways(step):
    pairs = []
    for chip in range(CHIPS):
        pairs.append((chip * CORES, (chip + step) % CHIPS * CORES))
        pairs.append((chip * CORES + 1, (chip - step) % CHIPS * CORES + 1))
    return pairs


def contract_rows(left, right):
    return lax.dot_general(
        left, right, (((0,), (0,)), ((), ())), preferred_element_type=jnp.float32
    )


def contract_cols(left, right):
    return lax.dot_general(
        left, right, (((1,), (1,)), ((), ())), preferred_element_type=jnp.float32
    )


def product(left, right):
    return jnp.dot(left, right, preferred_element_type=jnp.float32)


def half_kernel(*refs):
    grads_ref, low_ref, x_ref, crossed_ref, scale_ref, counts_ref, spread_ref, comp_ref, down_ref = (
        refs[:9]
    )
    before, out_refs = refs[9:-5], refs[-5:]

    @pl.when(pl.program_id(0) == 0)
    def _():
        for index, ref in enumerate(out_refs):
            ref[...] = before[index][...] if before else jnp.zeros(ref.shape, ref.dtype)

    out_grad = grads_ref[:, :COMP]
    rank_grad = grads_ref[:, COMP:]
    x = x_ref[0]
    cross = contract_cols(out_grad, comp_ref[...])
    back = contract_cols(rank_grad, down_ref[...])
    input_grad = (cross[:, EMBED:] * scale_ref[0] + back).astype(jnp.bfloat16)
    scaled = input_grad.astype(jnp.float32) * spread_ref[0]
    high = scaled.astype(jnp.bfloat16)
    rest = (scaled - high.astype(jnp.float32)).astype(jnp.bfloat16)
    table = product(counts_ref[0], jnp.concatenate([high, rest], axis=1))
    scale_grad = (cross[:, :EMBED] * x.astype(jnp.float32)).astype(jnp.bfloat16)
    down_out, up_out, bias_out, comp_out, table_out = out_refs
    down_out[...] += contract_rows(x, rank_grad)
    up_out[...] += contract_rows(low_ref[0], scale_grad)
    bias_out[...] += jnp.sum(scale_grad.astype(jnp.float32), axis=0, keepdims=True)
    comp_out[...] += contract_rows(crossed_ref[0], out_grad)
    table_out[...] += table[:, :EMBED] + table[:, EMBED:]


def half(side, grads, saved, before=()):
    step = HALF // STEPS
    shapes = [(EMBED, RANK), (RANK, EMBED), (1, EMBED), (EMBED, COMP), (TABLE_ROWS, EMBED)]

    def rows(width):
        return pl.BlockSpec((1, step, width), lambda i: (side, i, 0))

    in_specs = [
        pl.BlockSpec((step, COMP + RANK), lambda i: (i, 0)),
        rows(RANK),
        rows(EMBED),
        rows(EMBED),
        rows(EMBED),
        pl.BlockSpec((1, TABLE_ROWS, step), lambda i: (side, 0, i)),
        rows(EMBED),
        fetched((2 * EMBED, COMP)),
        fetched((EMBED, RANK)),
    ] + [fetched(array.shape) for array in before]
    return pl.pallas_call(
        half_kernel,
        grid=(STEPS,),
        in_specs=in_specs,
        out_specs=[fetched(shape) for shape in shapes],
        out_shape=[full_type(*shape) for shape in shapes],
        compiler_params=pltpu.CompilerParams(vmem_limit_bytes=ROOM),
        cost_estimate=pl.CostEstimate(
            flops=1_500_000_000, bytes_accessed=6_000_000, transcendentals=0
        ),
        name="column_half_second" if before else "column_half_first",
    )(grads, *saved, *before)


def pack_kernel(
    place_ref, x_ref, partner_ref, down_ref, self_ref, first_ref, second_ref, third_ref, far_ref
):
    core, chip = place_ref[0], place_ref[1]
    way = 1 - 2 * core
    sides = []
    for ref in (x_ref, partner_ref):
        low = product(ref[...], down_ref[...]).astype(jnp.bfloat16)
        sides.append((ref, low))

    def fill(step, side, target):
        ref, low = sides[side]
        base = lax.rem(chip + way * step + CHIPS, CHIPS) * CORES
        for part, slot in ((0, base + core), (3, base + 1 - core)):
            target[part] = ref[:, pl.ds(pl.multiple_of(slot * EMBED, EMBED), EMBED)]
        target[1] = low[:, :BLOCK]
        target[2] = low[:, BLOCK:]

    for step, near_ref in enumerate((first_ref, second_ref, third_ref), 1):
        for side in range(2):
            fill(step, side, near_ref.at[side])
    fill(CHIPS // 2, 0, far_ref)
    fill(0, 0, self_ref)


WHOLE = pl.BlockSpec(memory_space=pltpu.VMEM)
SCALARS = pl.BlockSpec(memory_space=pltpu.SMEM)


def fetched(shape):
    return pl.BlockSpec(shape, lambda i: (0,) * len(shape))


def call(kernel, place, operands, shapes, name, flops=1000, moved=1000):
    return pl.pallas_call(
        kernel,
        grid=(1,),
        in_specs=[SCALARS] + [fetched(operand.shape) for operand in operands],
        out_specs=[fetched(shape.shape) for shape in shapes],
        out_shape=shapes,
        compiler_params=pltpu.CompilerParams(vmem_limit_bytes=ROOM),
        cost_estimate=pl.CostEstimate(flops=flops, bytes_accessed=moved, transcendentals=0),
        name=name,
    )(place, *operands)


def half_type(*shape):
    return jax.ShapeDtypeStruct(shape, jnp.bfloat16)


def full_type(*shape):
    return jax.ShapeDtypeStruct(shape, jnp.float32)


TILE = (4, BLOCK, EMBED)


def merge_kernel(
    place_ref, self_ref, first_ref, second_ref, third_ref, far_ref, keep_ref, give_ref
):
    blocks = [self_ref]
    for ref in (first_ref, second_ref, third_ref):
        blocks += [ref.at[0], ref.at[1]]
    blocks.append(far_ref)
    for index, block in enumerate(blocks):
        keep_ref[index] = block[0:3]
        give_ref[index] = block[1:4]


def counts_kernel(place_ref, ids_ref, lengths_ref, inverse_ref, counts_ref, spread_ref):
    mine = place_ref[0]
    tile = 64

    @pl.loop(0, CHIPS * CORES)
    def _(block):
        side = jnp.where(lax.rem(block, CORES) == mine, 0, 1)
        bags = pl.ds(pl.multiple_of(block * BLOCK, BLOCK), BLOCK)
        to = pl.ds(pl.multiple_of(lax.div(block, CORES) * BLOCK, BLOCK), BLOCK)
        lengths = lengths_ref[:, bags]
        live = [
            jnp.where(lengths > slot, ids_ref[slot : slot + 1, bags], -1) for slot in range(SLOTS)
        ]
        for start in range(0, TABLE_ROWS, tile):
            row_values = start + lax.broadcasted_iota(jnp.int32, (tile, BLOCK), 0)
            total = jnp.zeros((tile, BLOCK), jnp.float32)
            for slot in range(SLOTS):
                total = total + jnp.where(live[slot] == row_values, 1.0, 0.0)
            counts_ref[side, start : start + tile, to] = total.astype(jnp.bfloat16)
        spread_ref[side, to, :] = jnp.broadcast_to(inverse_ref[:, bags], (BLOCK, BLOCK)).T


def saved_kernel(
    place_ref,
    keep_ref,
    taken_ref,
    down_ref,
    up_ref,
    bias_ref,
    comp_ref,
    low_ref,
    x_ref,
    crossed_ref,
    scale_ref,
    comp_out,
    down_out,
):
    mine, chip, me, slot = place_ref[0], place_ref[1], place_ref[2], place_ref[3]
    own = pl.ds(pl.multiple_of(me * EMBED, EMBED), EMBED)
    served = pl.ds(pl.multiple_of(slot * EMBED, EMBED), EMBED)
    comp_out[:EMBED, :] = comp_ref[own, :]
    comp_out[EMBED:, :] = comp_ref[served, :]
    down_out[...] = down_ref[served, :]
    ups = jnp.concatenate([up_ref[:, own], up_ref[:, served]], axis=1)
    bias = jnp.concatenate([bias_ref[:, own], bias_ref[:, served]], axis=1)
    for side in range(CORES):
        core = mine if side == 0 else 1 - mine

        @pl.loop(0, CHIPS)
        def _(k):
            rows = pl.ds(pl.multiple_of(k * BLOCK, BLOCK), BLOCK)
            way = lax.rem((chip - k) * (1 - 2 * mine) + CHIPS, CHIPS)
            given = (way > CHIPS // 2) | ((lax.rem(way, CHIPS // 2) == 0) & (core != mine))
            near = jnp.where(way > CHIPS // 2, CHIPS - way, way)
            holder = jnp.where(given, 1 - mine, mine)
            inner = 2 * near - 1 + jnp.where(core == holder, 0, 1)
            at = jnp.where(near == 0, 0, jnp.where(near == CHIPS // 2, CHIPS - 1, inner))

            @pl.when(given)
            def _():
                x_ref[side, rows, :] = taken_ref[at, 2]
                low_ref[side, rows, :BLOCK] = taken_ref[at, 0]
                low_ref[side, rows, BLOCK:] = taken_ref[at, 1]

            @pl.when(jnp.logical_not(given))
            def _():
                x_ref[side, rows, :] = keep_ref[at, 0]
                low_ref[side, rows, :BLOCK] = keep_ref[at, 1]
                low_ref[side, rows, BLOCK:] = keep_ref[at, 2]

        scale = product(low_ref[side], ups) + bias
        wide = x_ref[side].astype(jnp.float32)
        crossed_ref[side] = (wide * scale[:, :EMBED] + wide).astype(jnp.bfloat16)
        scale_ref[side] = scale[:, EMBED:] + 1.0


def rank_kernel(grad_ref, x_ref, comp_ref, up_ref, out_ref):
    out_grad = grad_ref[...]
    total = jnp.zeros((BLOCK, RANK), jnp.float32)
    width = 512
    for start in range(0, x_ref.shape[1], width):
        columns = pl.ds(start, width)
        cross = contract_cols(out_grad, comp_ref[columns, :])
        scale_grad = (cross * x_ref[:, columns].astype(jnp.float32)).astype(jnp.bfloat16)
        total += contract_cols(scale_grad, up_ref[:, columns])
    rank_grad = total.astype(jnp.bfloat16)
    for chip in range(CHIPS):
        out_ref[chip, :, :COMP] = out_grad
        out_ref[chip, :, COMP:] = rank_grad


def rank_rows(out_grad, inputs, comp_mat, up_mat):
    return pl.pallas_call(
        rank_kernel,
        in_specs=[WHOLE] * 4,
        out_specs=WHOLE,
        out_shape=jax.ShapeDtypeStruct((CHIPS, BLOCK, COMP + RANK), jnp.bfloat16),
        compiler_params=pltpu.CompilerParams(vmem_limit_bytes=16 * 1024 * 1024),
        cost_estimate=pl.CostEstimate(
            flops=RANK_FLOPS, bytes_accessed=3_600_000, transcendentals=0
        ),
        name="rank_grad_rows",
    )(out_grad, inputs, comp_mat, up_mat)


def on_device(
    top_grad, pooled_in, w_down, w_up, cross_bias, w_comp, feature_slot, bag_ids, bag_lengths
):
    arrived = lax.all_to_all(top_grad, "hst", split_axis=1, concat_axis=0, tiled=True)
    out_grad = arrived.reshape(BLOCK, COMP)
    me = lax.axis_index("tower")
    slot = jnp.sum(jnp.where(feature_slot[0] == me, jnp.arange(CHIPS * CORES, dtype=jnp.int32), 0))
    place = jnp.stack([me & 1, me >> 1, me, slot]).astype(jnp.int32)
    inputs, down_mat, up_mat, comp_mat = pooled_in[0], w_down[0], w_up[0], w_comp[0]

    partner = lax.ppermute(inputs, "tower", SWAP)
    mine, *sent = call(
        pack_kernel,
        place,
        [inputs, partner, down_mat],
        [half_type(*TILE)] + [half_type(2, *TILE)] * NEAR + [half_type(*TILE)],
        "low_rank_and_columns",
        PACK_FLOPS,
        3_000_000,
    )
    received = [
        lax.ppermute(block, "tower", both_ways(step)) for step, block in enumerate(sent, 1)
    ]

    rows_out = rank_rows(out_grad, inputs, comp_mat, up_mat)
    rows_out, *received = lax.optimization_barrier((rows_out, *received))
    grads_own = lax.all_to_all(
        rows_out,
        "tower",
        split_axis=0,
        concat_axis=0,
        tiled=True,
        axis_index_groups=SAME_CORE,
    ).reshape(HALF, COMP + RANK)

    eight = half_type(CHIPS, 3, BLOCK, EMBED)
    keep, give = call(merge_kernel, place, [mine, *received], [eight, eight], "merge_rows")
    taken = lax.ppermute(give, "tower", SWAP)
    lengths = bag_lengths[0]
    counts, spread = call(
        counts_kernel,
        place,
        [jnp.transpose(bag_ids[0, 0]), lengths, 1.0 / lengths.astype(jnp.float32)],
        [half_type(CORES, TABLE_ROWS, HALF), full_type(CORES, HALF, EMBED)],
        "bag_counts",
    )
    low, x, crossed, scale, comp_two, down_one = call(
        saved_kernel,
        place,
        [keep, taken, down_mat, up_mat, cross_bias, comp_mat],
        [
            half_type(CORES, HALF, RANK),
            half_type(CORES, HALF, EMBED),
            half_type(CORES, HALF, EMBED),
            full_type(CORES, HALF, EMBED),
            half_type(2 * EMBED, COMP),
            half_type(EMBED, RANK),
        ],
        "saved_rows",
    )
    saved = (low, x, crossed, scale, counts, spread, comp_two, down_one)
    grads_own, *saved = lax.optimization_barrier((grads_own, *saved))
    grads_other = lax.ppermute(grads_own, "tower", SWAP)
    first = half(0, grads_own, saved)
    grad_down, grad_up, grad_bias, grad_comp, tables = half(1, grads_other, saved, first)
    return grad_down[None], grad_up[None], grad_bias, grad_comp[None], tables[None, None]


def solution(mesh):
    placed = (
        P(("tower", "hst"), None, None),
        P("hst", "tower", None),
        P("hst", None, None),
        P("hst", None, None),
        P("hst", None),
        P("hst", None, None),
        P("hst", None),
        P("hst", "tower", None, None),
        P("hst", "tower", None),
    )
    return jax.shard_map(
        on_device,
        mesh=mesh,
        in_specs=placed,
        out_specs=(
            P("hst", "tower", None),
            P("hst", None, "tower"),
            P("hst", "tower"),
            P("hst", "tower", None),
            P("hst", "tower", None, None),
        ),
        check_vma=False,
    )
```

time: 260 us -> 114 us (0.44)
  waiting for transfers between devices: 149 us -> 16.8 us
  blocking collectives: 31.8 us -> 0 us
  Pallas kernels: 0 us -> 29.5 us
  starting transfers between devices: 32.1 us -> 57.4 us
  matrix products: 20.2 us -> 0 us
  between operations: 14.6 us -> 0.86 us
    reduce_scatter x3 -> x0, waiting for transfers between devices: 137 us -> none  [the longest x1 68.9 us: on_device(): lax.psum_scatter(down_term, 'tower', scatter_dimension=0, tiled=True)]
    ppermute x0 -> x7, starting transfers between devices: none -> 39.6 us  [the longest x4 17.2 us: on_device(): lax.ppermute(block, 'tower', both_ways(step))]
    unnamed x1 -> x0, blocking collectives: 31.8 us -> none
    pallas_call x0 -> x7, Pallas kernels: none -> 29.5 us  [the longest x4 16.8 us: call(): pl.pallas_call(kernel, grid=(1,), in_specs=[SCALARS] + [fetched(operand.s...]
    dot_general x9 -> x0, matrix products: 20.2 us -> none  [the longest x1 6.64 us: table_block(): jnp.dot(counts.astype(jnp.bfloat16), feat_rows, preferred_element_type=jn...]
    all_to_all x1, starting transfers between devices: 22.8 us -> 9.3 us  [on_device(): lax.all_to_all(top_grad, 'hst', split_axis=1, concat_axis=0, tiled=True)]
    all_to_all x1, waiting for transfers between devices: 11.8 us -> 0.01 us  [on_device(): lax.all_to_all(top_grad, 'hst', split_axis=1, concat_axis=0, tiled=True)]
    all_to_all x1, waiting for transfers between devices: 0.01 us -> 10 us  [on_device(): lax.all_to_all(rows_out, 'tower', split_axis=0, concat_axis=0, tiled=True...]
  transfers between devices with their start and end apart: 5 -> 9, of which waited for: 4 -> 2; matrix products, arithmetic and copies ran while one was open for 10% -> 4% of each run, Pallas kernels for 0% -> 21%
where the time goes in v3:
time: 114 us; the launch traced here: 113 us
  starting transfers between devices  57.4 us (50%)
  Pallas kernels  29.5 us (26%)
  waiting for transfers between devices  16.8 us (15%)
  local copies, waits for them, and re-layouts  5.31 us (5%)
  other arithmetic  3.22 us (3%)
    ppermute x4, starting transfers between devices, on_device(): lax.ppermute(block, 'tower', both_ways(step))  17.2 us
    pallas_call x4, Pallas kernels, call(): pl.pallas_call(kernel, grid=(1,), in_specs=[SCALARS] + [fetched(operand.s...  16.8 us
    ppermute x1, starting transfers between devices, on_device(): partner = lax.ppermute(inputs, 'tower', SWAP)  16.2 us
    pallas_call x2, Pallas kernels, half(): pl.pallas_call(half_kernel, grid=(STEPS,), in_specs=in_specs, out_specs=[...  10.8 us
    all_to_all x1, waiting for transfers between devices, on_device(): lax.all_to_all(rows_out, 'tower', split_axis=0, concat_axis=0, tiled=True...  10 us
    all_to_all x1, starting transfers between devices, on_device(): lax.all_to_all(top_grad, 'hst', split_axis=1, concat_axis=0, tiled=True)  9.3 us
    all_to_all x1, starting transfers between devices, on_device(): lax.all_to_all(rows_out, 'tower', split_axis=0, concat_axis=0, tiled=True...  8.47 us
    ppermute x4, waiting for transfers between devices, on_device(): lax.ppermute(block, 'tower', both_ways(step))  6.7 us
  transfers between devices with their start and end apart: 9, of which 2 were waited for; matrix products, arithmetic and copies ran while one was open for 4% of the time, Pallas kernels for 21%

profile of v3, /device:TPU:1, one launch (start us, length us, event | category | flops | bytes accessed | tf_op | source)
XLA Modules:
  0.0 113.1 jit_solution(6160859583865425774)
XLA Ops:
  0.6 0.0 copy-start
  0.6 0.0 copy-start.1
  0.7 16.2 %collective-permute-start = (bf16[128,2048]{1,0:T(8,128)(2,1)}, bf16[128,2048]{1,0:T(8,128)(2,1)S(1)}, u32[]{:S(2)}, u32[]{:S(2)}) collective-permute-start(bf16[128,2048]{1,0:T(8,128)(2,1)} %bitcast.31), channel_id=1, source_target_pairs={{0,64},{64,0},{128,192},{192,128},{256,320},{320,256},{384,448},{4... | collective-permute-start | bytes 1572872 | tf_op jit(solution)/shard_map/ppermute | solution.py:298
  16.9 1.5 %copy.15 = bf16[2,64,256]{2,0,1:T(2,128)(2,1)} copy(bf16[2,64,256]{2,1,0:T(8,128)(2,1)} %param.9) | data formatting | bytes 131072 | tf_op args[0]
  18.4 9.3 %all-to-all-start = ((bf16[2,64,256]{2,0,1:T(2,128)(2,1)}), bf16[2,64,256]{2,0,1:T(2,128)(2,1)S(1)}, u32[]{:S(2)}, u32[]{:S(2)}) async-start(bf16[2,64,256]{2,0,1:T(2,128)(2,1)} %copy.15), calls=%async_computation | async-start | bytes 131072 | tf_op jit(solution)/shard_map/all_to_all | solution.py:291
  27.7 1.3 %fusion = s32[]{:T(128)} fusion(s32[1,16]{1,0:T(1,128)} %param.15, s32[]{:T(128)} %axis_index.15), kind=kLoop, calls=%fused_computation.2 | loop fusion | flops 47 | bytes 72 | tf_op jit(solution)/shard_map/reduce_sum | solution.py:294
  29.0 1.3 %pad_add_fusion.place_ref = s32[4]{0:T(128)} fusion(s32[1]{0:T(128)} %bitcast.9, s32[1]{0:T(128)} %bitcast.7, s32[1]{0:T(128)} %bitcast.6, s32[1]{0:T(128)} %bitcast.5), kind=kLoop, calls=%fused_computation.3 | loop fusion | flops 12 | bytes 32 | tf_op jit(solution)/shard_map/stack | solution.py:295
  30.3 0.0 collective-permute-done.partner_ref
  30.3 0.0 copy-start.6
  30.3 0.8 copy-done.6
  31.1 3.0 %low_rank_and_columns.1 = (bf16[4,128,128]{2,1,0:T(8,128)(2,1)}, bf16[2,4,128,128]{3,2,1,0:T(8,128)(2,1)}, bf16[2,4,128,128]{3,2,1,0:T(8,128)(2,1)}, bf16[2,4,12...) custom-call(s32[4]{0:T(128)} %pad_add_fusion.place_ref, bf16[128,2048]{1,0:T(8,128)(2,1)} %bitcast.32, ...), custom_call_target="tpu_custom_call" | custom-call | flops 270000000 | bytes 3000000 | tf_op jit(solution)/shard_map/low_rank_and_columns/pallas_call | solution.py:148
  34.1 5.1 %collective-permute-start.1 = (bf16[2,4,128,128]{3,2,1,0:T(8,128)(2,1)}, bf16[2,4,128,128]{3,2,1,0:T(8,128)(2,1)S(1)}, u32[]{:S(2)}, u32[]{:S(2)}) collective-permute-start(bf16[2,4,128,128]{3,2,1,0:T(8,128)(2,1)} %get-tuple-element.44), channel_id=1, source_target_pairs={{0,128},{64,960},{128,256},{192,64},{256,384},{320,192},{384,512},... | collective-permute-start | bytes 786440 | tf_op jit(solution)/shard_map/ppermute | solution.py:309
  39.2 3.8 %collective-permute-start.2 = (bf16[2,4,128,128]{3,2,1,0:T(8,128)(2,1)}, bf16[2,4,128,128]{3,2,1,0:T(8,128)(2,1)S(1)}, u32[]{:S(2)}, u32[]{:S(2)}) collective-permute-start(bf16[2,4,128,128]{3,2,1,0:T(8,128)(2,1)} %get-tuple-element.45), channel_id=1, source_target_pairs={{0,256},{64,832},{128,384},{192,960},{256,512},{320,64},{384,640},... | collective-permute-start | bytes 786440 | tf_op jit(solution)/shard_map/ppermute | solution.py:309
  43.0 2.7 %collective-permute-start.3 = (bf16[2,4,128,128]{3,2,1,0:T(8,128)(2,1)}, bf16[2,4,128,128]{3,2,1,0:T(8,128)(2,1)S(1)}, u32[]{:S(2)}, u32[]{:S(2)}) collective-permute-start(bf16[2,4,128,128]{3,2,1,0:T(8,128)(2,1)} %get-tuple-element.46), channel_id=1, source_target_pairs={{0,384},{64,704},{128,512},{192,832},{256,640},{320,960},{384,768}... | collective-permute-start | bytes 786440 | tf_op jit(solution)/shard_map/ppermute | solution.py:309
  45.7 5.7 %collective-permute-start.4 = (bf16[4,128,128]{2,1,0:T(8,128)(2,1)}, bf16[4,128,128]{2,1,0:T(8,128)(2,1)S(1)}, u32[]{:S(2)}, u32[]{:S(2)}) collective-permute-start(bf16[4,128,128]{2,1,0:T(8,128)(2,1)} %get-tuple-element.47), channel_id=1, source_target_pairs={{0,512},{64,576},{128,640},{192,704},{256,768},{320,832},{384,896}... | collective-permute-start | bytes 393224 | tf_op jit(solution)/shard_map/ppermute | solution.py:309
  51.4 0.0 all-to-all-done
  51.4 0.0 copy-done
  51.5 0.0 copy-done.1
  51.5 0.0 copy-start.2
  51.5 1.0 copy-done.2
  52.5 2.0 %rank_grad_rows.1 = bf16[8,128,512]{2,1,0:T(8,128)(2,1)} custom-call(bf16[128,256]{1,0:T(8,128)(2,1)S(1)} %reshape.35.grad_ref, bf16[128,2048]{1,0:T(8,128)(2,1)S(1)} %bitcast.33, bf16[2048,256]{1,0:T(8,128)(2,1)S(1)} %bitcast.28, bf16[256,2048]{1,0:T(8,128)(2,1)S(1)} %bitcast.30), custom_call_target="tpu_custom_call" | custom-call | flops 270000000 | bytes 3600000 | tf_op jit(solution)/shard_map/rank_grad_rows/pallas_call | solution.py:275
  54.5 0.0 copy-start.11
  54.5 6.7 %collective-permute-done.4.far_ref = bf16[4,128,128]{2,1,0:T(8,128)(2,1)S(1)} collective-permute-done((bf16[4,128,128]{2,1,0:T(8,128)(2,1)}, bf16[4,128,128]{2,1,0:T(8,128)(2,1)S(1)}, u32[]{:S(2)}, u32[]{:S(2)}) %collective-permute-start.4) | collective-permute-done | bytes 131104 | tf_op jit(solution)/shard_map/ppermute | solution.py:309
  61.2 0.0 copy-start.10
  61.2 0.0 collective-permute-done.1.first_ref
  61.2 0.0 copy-start.7
  61.2 0.0 collective-permute-done.2.second_ref
  61.2 0.0 copy-start.8
  61.2 0.0 collective-permute-done.3.third_ref
  61.2 0.0 copy-start.9
  61.2 8.5 %all-to-all-start.1 = ((bf16[8,128,512]{2,1,0:T(8,128)(2,1)}), bf16[8,128,512]{2,1,0:T(8,128)(2,1)S(1)}, u32[]{:S(2)}, u32[]{:S(2)}) async-start(bf16[8,128,512]{2,1,0:T(8,128)(2,1)} %rank_grad_rows.1), calls=%async_computation.1 | async-start | bytes 2097152 | tf_op jit(solution)/shard_map/all_to_all | solution.py:314
  69.7 0.0 copy-done.10
  69.7 0.0 copy-done.7
  69.7 0.0 copy-done.8
  69.7 0.0 copy-done.9
  69.7 2.5 %merge_rows.1 = (bf16[8,3,128,128]{3,2,1,0:T(8,128)(2,1)}, bf16[8,3,128,128]{3,2,1,0:T(8,128)(2,1)}) custom-call(s32[4]{0:T(128)} %pad_add_fusion.place_ref, bf16[4,128,128]{2,1,0:T(8,128)(2,1)} %get-tuple-element.49.self_ref, bf16[2,4,128,128]{3,2,1,0:T(8,128)(2,1)} %copy-done.7, bf16[2,4,128,128]{3,2,1,0:T(8,128)(2,1)} %copy-done.8, ...), custom_call_target="tpu_custom_call" | custom-call | flops 1000 | bytes 1000 | tf_op jit(solution)/shard_map/merge_rows/pallas_call | solution.py:148
  72.2 3.8 %collective-permute-start.5 = (bf16[8,3,128,128]{3,2,1,0:T(8,128)(2,1)}, bf16[8,3,128,128]{3,2,1,0:T(8,128)(2,1)S(1)}, u32[]{:S(2)}, u32[]{:S(2)}) collective-permute-start(bf16[8,3,128,128]{3,2,1,0:T(8,128)(2,1)} %get-tuple-element.55), channel_id=1, source_target_pairs={{0,64},{64,0},{128,192},{192,128},{256,320},{320,256},{384,448},{4... | collective-permute-start | bytes 2359304 | tf_op jit(solution)/shard_map/ppermute | solution.py:325
  76.1 0.0 copy-done.11
  76.1 0.6 convert_divide_fusion.inverse_ref
  76.7 6.0 %bag_counts.1 = (bf16[2,512,1024]{2,1,0:T(8,128)(2,1)}, f32[2,1024,128]{2,1,0:T(8,128)}) custom-call(s32[4]{0:T(128)} %pad_add_fusion.place_ref, s32[8,2048]{1,0:T(8,128)} %bitcast.39, s32[1,2048]{1,0:T(1,128)} %bitcast.40, f32[1,2048]{1,0:T(1,128)} %convert_divide_fusion.inverse_ref), custom_call_target="tpu_custom_call" | custom-call | flops 1000 | bytes 1000 | tf_op jit(solution)/shard_map/bag_counts/pallas_call | solution.py:148
  82.7 0.0 collective-permute-done.5.taken_ref
  82.7 0.0 copy-start.5
  82.7 0.9 copy-done.5
  83.6 5.2 %saved_rows.1 = (bf16[2,1024,256]{2,1,0:T(8,128)(2,1)}, bf16[2,1024,128]{2,1,0:T(8,128)(2,1)}, bf16[2,1024,128]{2,1,0:T(8,128)(2,1)}, f32[2,1024,128]{2,1,0:T(8,...) custom-call(s32[4]{0:T(128)} %pad_add_fusion.place_ref, bf16[8,3,128,128]{3,2,1,0:T(8,128)(2,1)} %get-tuple-element.54.keep_ref, ...), custom_call_target="tpu_custom_call" | custom-call | flops 1000 | bytes 1000 | tf_op jit(solution)/shard_map/saved_rows/pallas_call | solution.py:148
  88.8 10.0 %all-to-all-done.1 = bf16[8,128,512]{2,1,0:T(8,128)(2,1)S(1)} async-done(((bf16[8,128,512]{2,1,0:T(8,128)(2,1)}), bf16[8,128,512]{2,1,0:T(8,128)(2,1)S(1)}, u32[]{:S(2)}, u32[]{:S(2)}) %all-to-all-start.1) | async-done | bytes 1048608 | tf_op jit(solution)/shard_map/all_to_all | solution.py:314
  98.9 0.0 copy-start.3
  98.9 2.4 %collective-permute-start.6 = (bf16[1024,512]{1,0:T(8,128)(2,1)S(1)}, bf16[1024,512]{1,0:T(8,128)(2,1)S(1)}, u32[]{:S(2)}, u32[]{:S(2)}) collective-permute-start(bf16[1024,512]{1,0:T(8,128)(2,1)S(1)} %bitcast.36), channel_id=1, source_target_pairs={{0,64},{64,0},{128,192},{192,128},{256,320},{320,256},{384,448},{4... | collective-permute-start | bytes 3145736 | tf_op jit(solution)/shard_map/ppermute | solution.py:350
  101.3 0.0 copy-done.3
  101.3 5.3 %column_half_first.1 = (f32[128,256]{1,0:T(8,128)}, f32[256,128]{1,0:T(8,128)}, f32[1,128]{1,0:T(1,128)}, f32[128,256]{1,0:T(8,128)}, f32[512,128]{1,0:T(8,128)}) custom-call(bf16[1024,512]{1,0:T(8,128)(2,1)} %bitcast.37, bf16[2,1024,256]{2,1,0:T(8,128)(2,1)} %get-tuple-element.65.refs_1_, bf16[2,1024,128]{2,1,0:T(8,128)(2,1)} %get-tuple-element.66.refs_2_, ...), custom_call_target="tpu_custom_call" | custom-call | flops 1500000000 | bytes 6000000 | tf_op jit(solution)/shard_map/column_half_first/pallas_call | solution.py:100
  106.6 0.0 collective-permute-done.6.refs_0_
  106.6 0.0 copy-start.4
  106.6 1.0 copy-done.4
  107.5 5.5 %column_half_second.1 = (f32[128,256]{1,0:T(8,128)}, f32[256,128]{1,0:T(8,128)}, f32[1,128]{1,0:T(1,128)}, f32[128,256]{1,0:T(8,128)}, f32[512,128]{1,0:T(8,128)}) custom-call(bf16[1024,512]{1,0:T(8,128)(2,1)} %copy-done.4, bf16[2,1024,256]{2,1,0:T(8,128)(2,1)} %get-tuple-element.65.refs_1_, bf16[2,1024,128]{2,1,0:T(8,128)(2,1)} %get-tuple-element.66.refs_2_, ...), custom_call_target="tpu_custom_call" | custom-call | flops 1500000000 | bytes 6000000 | tf_op jit(solution)/shard_map/column_half_second/pallas_call | solution.py:100
  (1 shorter events, 0.0 us)
Async XLA Ops:
  0.6 50.8 %copy-start = (bf16[1,2048,256]{2,1,0:T(8,128)(2,1)S(1)}, bf16[1,2048,256]{2,1,0:T(8,128)(2,1)}, u32[]{:S(2)}) copy-start(bf16[1,2048,256]{2,1,0:T(8,128)(2,1)} %param.14) | copy-start | bytes 3145732
  0.6 50.8 %copy-start.1 = (bf16[1,256,2048]{2,1,0:T(8,128)(2,1)S(1)}, bf16[1,256,2048]{2,1,0:T(8,128)(2,1)}, u32[]{:S(2)}) copy-start(bf16[1,256,2048]{2,1,0:T(8,128)(2,1)} %param.12) | copy-start | bytes 3145732
  0.7 29.7 %collective-permute-start = (bf16[128,2048]{1,0:T(8,128)(2,1)}, bf16[128,2048]{1,0:T(8,128)(2,1)S(1)}, u32[]{:S(2)}, u32[]{:S(2)}) collective-permute-start(bf16[128,2048]{1,0:T(8,128)(2,1)} %bitcast.31), channel_id=1, source_target_pairs={{0,64},{64,0},{128,192},{192,128},{256,320},{320,256},{384,448},{4... | collective-permute-start | bytes 1572872 | tf_op jit(solution)/shard_map/ppermute | solution.py:298
  18.4 33.0 %all-to-all-start = ((bf16[2,64,256]{2,0,1:T(2,128)(2,1)}), bf16[2,64,256]{2,0,1:T(2,128)(2,1)S(1)}, u32[]{:S(2)}, u32[]{:S(2)}) async-start(bf16[2,64,256]{2,0,1:T(2,128)(2,1)} %copy.15), calls=%async_computation | async-start | bytes 131072 | tf_op jit(solution)/shard_map/all_to_all | solution.py:291
  30.3 0.8 copy-start.6
  34.1 27.1 %collective-permute-start.1 = (bf16[2,4,128,128]{3,2,1,0:T(8,128)(2,1)}, bf16[2,4,128,128]{3,2,1,0:T(8,128)(2,1)S(1)}, u32[]{:S(2)}, u32[]{:S(2)}) collective-permute-start(bf16[2,4,128,128]{3,2,1,0:T(8,128)(2,1)} %get-tuple-element.44), channel_id=1, source_target_pairs={{0,128},{64,960},{128,256},{192,64},{256,384},{320,192},{384,512},... | collective-permute-start | bytes 786440 | tf_op jit(solution)/shard_map/ppermute | solution.py:309
  39.2 22.0 %collective-permute-start.2 = (bf16[2,4,128,128]{3,2,1,0:T(8,128)(2,1)}, bf16[2,4,128,128]{3,2,1,0:T(8,128)(2,1)S(1)}, u32[]{:S(2)}, u32[]{:S(2)}) collective-permute-start(bf16[2,4,128,128]{3,2,1,0:T(8,128)(2,1)} %get-tuple-element.45), channel_id=1, source_target_pairs={{0,256},{64,832},{128,384},{192,960},{256,512},{320,64},{384,640},... | collective-permute-start | bytes 786440 | tf_op jit(solution)/shard_map/ppermute | solution.py:309
  43.0 18.2 %collective-permute-start.3 = (bf16[2,4,128,128]{3,2,1,0:T(8,128)(2,1)}, bf16[2,4,128,128]{3,2,1,0:T(8,128)(2,1)S(1)}, u32[]{:S(2)}, u32[]{:S(2)}) collective-permute-start(bf16[2,4,128,128]{3,2,1,0:T(8,128)(2,1)} %get-tuple-element.46), channel_id=1, source_target_pairs={{0,384},{64,704},{128,512},{192,832},{256,640},{320,960},{384,768}... | collective-permute-start | bytes 786440 | tf_op jit(solution)/shard_map/ppermute | solution.py:309
  45.7 15.4 %collective-permute-start.4 = (bf16[4,128,128]{2,1,0:T(8,128)(2,1)}, bf16[4,128,128]{2,1,0:T(8,128)(2,1)S(1)}, u32[]{:S(2)}, u32[]{:S(2)}) collective-permute-start(bf16[4,128,128]{2,1,0:T(8,128)(2,1)} %get-tuple-element.47), channel_id=1, source_target_pairs={{0,512},{64,576},{128,640},{192,704},{256,768},{320,832},{384,896}... | collective-permute-start | bytes 393224 | tf_op jit(solution)/shard_map/ppermute | solution.py:309
  51.5 1.0 copy-start.2
  54.5 21.6 %copy-start.11 = (s32[1,1,2048]{2,1,0:T(1,128)S(1)}, s32[1,1,2048]{2,1,0:T(1,128)}, u32[]{:S(2)}) copy-start(s32[1,1,2048]{2,1,0:T(1,128)} %param.17) | copy-start | bytes 24580
  61.2 8.5 %copy-start.10 = (bf16[4,128,128]{2,1,0:T(8,128)(2,1)}, bf16[4,128,128]{2,1,0:T(8,128)(2,1)S(1)}, u32[]{:S(2)}) copy-start(bf16[4,128,128]{2,1,0:T(8,128)(2,1)S(1)} %collective-permute-done.4.far_ref) | copy-start | bytes 393220
  61.2 8.5 %copy-start.7 = (bf16[2,4,128,128]{3,2,1,0:T(8,128)(2,1)}, bf16[2,4,128,128]{3,2,1,0:T(8,128)(2,1)S(1)}, u32[]{:S(2)}) copy-start(bf16[2,4,128,128]{3,2,1,0:T(8,128)(2,1)S(1)} %collective-permute-done.1.first_ref) | copy-start | bytes 786436
  61.2 8.5 %copy-start.8 = (bf16[2,4,128,128]{3,2,1,0:T(8,128)(2,1)}, bf16[2,4,128,128]{3,2,1,0:T(8,128)(2,1)S(1)}, u32[]{:S(2)}) copy-start(bf16[2,4,128,128]{3,2,1,0:T(8,128)(2,1)S(1)} %collective-permute-done.2.second_ref) | copy-start | bytes 786436
  61.2 8.5 %copy-start.9 = (bf16[2,4,128,128]{3,2,1,0:T(8,128)(2,1)}, bf16[2,4,128,128]{3,2,1,0:T(8,128)(2,1)S(1)}, u32[]{:S(2)}) copy-start(bf16[2,4,128,128]{3,2,1,0:T(8,128)(2,1)S(1)} %collective-permute-done.3.third_ref) | copy-start | bytes 786436
  61.2 37.7 %all-to-all-start.1 = ((bf16[8,128,512]{2,1,0:T(8,128)(2,1)}), bf16[8,128,512]{2,1,0:T(8,128)(2,1)S(1)}, u32[]{:S(2)}, u32[]{:S(2)}) async-start(bf16[8,128,512]{2,1,0:T(8,128)(2,1)} %rank_grad_rows.1), calls=%async_computation.1 | async-start | bytes 2097152 | tf_op jit(solution)/shard_map/all_to_all | solution.py:314
  72.2 10.5 %collective-permute-start.5 = (bf16[8,3,128,128]{3,2,1,0:T(8,128)(2,1)}, bf16[8,3,128,128]{3,2,1,0:T(8,128)(2,1)S(1)}, u32[]{:S(2)}, u32[]{:S(2)}) collective-permute-start(bf16[8,3,128,128]{3,2,1,0:T(8,128)(2,1)} %get-tuple-element.55), channel_id=1, source_target_pairs={{0,64},{64,0},{128,192},{192,128},{256,320},{320,256},{384,448},{4... | collective-permute-start | bytes 2359304 | tf_op jit(solution)/shard_map/ppermute | solution.py:325
  82.7 0.9 copy-start.5
  98.9 2.4 %copy-start.3 = (bf16[8,128,512]{2,1,0:T(8,128)(2,1)}, bf16[8,128,512]{2,1,0:T(8,128)(2,1)S(1)}, u32[]{:S(2)}) copy-start(bf16[8,128,512]{2,1,0:T(8,128)(2,1)S(1)} %all-to-all-done.1) | copy-start | bytes 3145732
  98.9 7.7 %collective-permute-start.6 = (bf16[1024,512]{1,0:T(8,128)(2,1)S(1)}, bf16[1024,512]{1,0:T(8,128)(2,1)S(1)}, u32[]{:S(2)}, u32[]{:S(2)}) collective-permute-start(bf16[1024,512]{1,0:T(8,128)(2,1)S(1)} %bitcast.36), channel_id=1, source_target_pairs={{0,64},{64,0},{128,192},{192,128},{256,320},{320,256},{384,448},{4... | collective-permute-start | bytes 3145736 | tf_op jit(solution)/shard_map/ppermute | solution.py:350
  106.6 1.0 copy-start.4

commit v4 on v3

--- a/solution.py
+++ b/solution.py
@@ -15,10 +15,11 @@
 BLOCK = 128
 HALF = CHIPS * BLOCK
 
-STEPS = 4
+STEPS = 2
 ROOM = 60 * 1024 * 1024
 PACK_FLOPS = 270_000_000
 RANK_FLOPS = 270_000_000
+COUNTS_FLOPS = 32_000_000_000
 
 NEAR = CHIPS // 2 - 1
 SAME_CORE = [[chip * CORES + core for chip in range(CHIPS)] for core in range(CORES)]
@@ -112,9 +113,9 @@
 
 
 def pack_kernel(
-    place_ref, x_ref, partner_ref, down_ref, self_ref, first_ref, second_ref, third_ref, far_ref
+    x_ref, partner_ref, down_ref, self_ref, first_ref, second_ref, third_ref, far_ref
 ):
-    core, chip = place_ref[0], place_ref[1]
+    _, core, chip = where_am_i()
     way = 1 - 2 * core
     sides = []
     for ref in (x_ref, partner_ref):
@@ -144,17 +145,22 @@
     return pl.BlockSpec(shape, lambda i: (0,) * len(shape))
 
 
-def call(kernel, place, operands, shapes, name, flops=1000, moved=1000):
+def where_am_i():
+    me = lax.axis_index("tower")
+    return me, me & 1, me >> 1
+
+
+def call(kernel, operands, shapes, name, flops=1000, moved=1000, scalars=()):
     return pl.pallas_call(
         kernel,
         grid=(1,),
-        in_specs=[SCALARS] + [fetched(operand.shape) for operand in operands],
+        in_specs=[SCALARS] * len(scalars) + [fetched(operand.shape) for operand in operands],
         out_specs=[fetched(shape.shape) for shape in shapes],
         out_shape=shapes,
         compiler_params=pltpu.CompilerParams(vmem_limit_bytes=ROOM),
         cost_estimate=pl.CostEstimate(flops=flops, bytes_accessed=moved, transcendentals=0),
         name=name,
-    )(place, *operands)
+    )(*scalars, *operands)
 
 
 def half_type(*shape):
@@ -169,7 +175,7 @@
 
 
 def merge_kernel(
-    place_ref, self_ref, first_ref, second_ref, third_ref, far_ref, keep_ref, give_ref
+    self_ref, first_ref, second_ref, third_ref, far_ref, keep_ref, give_ref
 ):
     blocks = [self_ref]
     for ref in (first_ref, second_ref, third_ref):
@@ -180,8 +186,8 @@
         give_ref[index] = block[1:4]
 
 
-def counts_kernel(place_ref, ids_ref, lengths_ref, inverse_ref, counts_ref, spread_ref):
-    mine = place_ref[0]
+def counts_kernel(ids_ref, lengths_ref, inverse_ref, counts_ref, spread_ref):
+    _, mine, _ = where_am_i()
     tile = 64
 
     @pl.loop(0, CHIPS * CORES)
@@ -203,7 +209,7 @@
 
 
 def saved_kernel(
-    place_ref,
+    slots_ref,
     keep_ref,
     taken_ref,
     down_ref,
@@ -217,7 +223,10 @@
     comp_out,
     down_out,
 ):
-    mine, chip, me, slot = place_ref[0], place_ref[1], place_ref[2], place_ref[3]
+    me, mine, chip = where_am_i()
+    slot = jnp.int32(0)
+    for index in range(CHIPS * CORES):
+        slot = jnp.where(slots_ref[0, index] == me, index, slot)
     own = pl.ds(pl.multiple_of(me * EMBED, EMBED), EMBED)
     served = pl.ds(pl.multiple_of(slot * EMBED, EMBED), EMBED)
     comp_out[:EMBED, :] = comp_ref[own, :]
@@ -290,15 +299,11 @@
 ):
     arrived = lax.all_to_all(top_grad, "hst", split_axis=1, concat_axis=0, tiled=True)
     out_grad = arrived.reshape(BLOCK, COMP)
-    me = lax.axis_index("tower")
-    slot = jnp.sum(jnp.where(feature_slot[0] == me, jnp.arange(CHIPS * CORES, dtype=jnp.int32), 0))
-    place = jnp.stack([me & 1, me >> 1, me, slot]).astype(jnp.int32)
     inputs, down_mat, up_mat, comp_mat = pooled_in[0], w_down[0], w_up[0], w_comp[0]
 
     partner = lax.ppermute(inputs, "tower", SWAP)
     mine, *sent = call(
         pack_kernel,
-        place,
         [inputs, partner, down_mat],
         [half_type(*TILE)] + [half_type(2, *TILE)] * NEAR + [half_type(*TILE)],
         "low_rank_and_columns",
@@ -310,7 +315,6 @@
     ]
 
     rows_out = rank_rows(out_grad, inputs, comp_mat, up_mat)
-    rows_out, *received = lax.optimization_barrier((rows_out, *received))
     grads_own = lax.all_to_all(
         rows_out,
         "tower",
@@ -321,19 +325,18 @@
     ).reshape(HALF, COMP + RANK)
 
     eight = half_type(CHIPS, 3, BLOCK, EMBED)
-    keep, give = call(merge_kernel, place, [mine, *received], [eight, eight], "merge_rows")
+    keep, give = call(merge_kernel, [mine, *received], [eight, eight], "merge_rows")
     taken = lax.ppermute(give, "tower", SWAP)
     lengths = bag_lengths[0]
     counts, spread = call(
         counts_kernel,
-        place,
         [jnp.transpose(bag_ids[0, 0]), lengths, 1.0 / lengths.astype(jnp.float32)],
         [half_type(CORES, TABLE_ROWS, HALF), full_type(CORES, HALF, EMBED)],
         "bag_counts",
+        COUNTS_FLOPS,
     )
     low, x, crossed, scale, comp_two, down_one = call(
         saved_kernel,
-        place,
         [keep, taken, down_mat, up_mat, cross_bias, comp_mat],
         [
             half_type(CORES, HALF, RANK),
@@ -344,6 +347,7 @@
             half_type(EMBED, RANK),
         ],
         "saved_rows",
+        scalars=[feature_slot],
     )
     saved = (low, x, crossed, scale, counts, spread, comp_two, down_one)
     grads_own, *saved = lax.optimization_barrier((grads_own, *saved))

time: 114 us -> 99.7 us (0.87)
  the two profiles are of different devices: /device:TPU:1 before, /device:TPU:23 now
where the time goes in v4:
time: 99.7 us; the launch traced here: 99.1 us
  starting transfers between devices  62.4 us (63%)
  Pallas kernels  27.1 us (27%)
  local copies, waits for them, and re-layouts  6.2 us (6%)
  waiting for transfers between devices  1.93 us (2%)
    all_to_all x1, starting transfers between devices, on_device(): lax.all_to_all(top_grad, 'hst', split_axis=1, concat_axis=0, tiled=True)  21.9 us
    pallas_call x4, Pallas kernels, call(): pl.pallas_call(kernel, grid=(1,), in_specs=[SCALARS] * len(scalars) + [fe...  16.8 us
    ppermute x1, starting transfers between devices, on_device(): taken = lax.ppermute(give, 'tower', SWAP)  15.1 us
    ppermute x4, starting transfers between devices, on_device(): lax.ppermute(block, 'tower', both_ways(step))  13.5 us
    pallas_call x2, Pallas kernels, half(): pl.pallas_call(half_kernel, grid=(STEPS,), in_specs=in_specs, out_specs=[...  8.34 us
    all_to_all x1, starting transfers between devices, on_device(): lax.all_to_all(rows_out, 'tower', split_axis=0, concat_axis=0, tiled=True...  7.25 us
    unnamed x25, local copies, waits for them, and re-layouts  6.17 us
    ppermute x1, starting transfers between devices, on_device(): partner = lax.ppermute(inputs, 'tower', SWAP)  2.72 us
  transfers between devices with their start and end apart: 9, of which 1 were waited for; matrix products, arithmetic and copies ran while one was open for 2% of the time, Pallas kernels for 23%

profile of v4, /device:TPU:23, one launch (start us, length us, event | category | flops | bytes accessed | tf_op | source)
XLA Modules:
  0.0 99.1 jit_solution(17958072134466041930)
XLA Ops:
  0.6 0.0 copy-start.11
  0.6 0.0 copy-start
  0.7 0.0 copy-start.1
  0.7 2.7 %collective-permute-start = (bf16[128,2048]{1,0:T(8,128)(2,1)}, bf16[128,2048]{1,0:T(8,128)(2,1)S(1)}, u32[]{:S(2)}, u32[]{:S(2)}) collective-permute-start(bf16[128,2048]{1,0:T(8,128)(2,1)} %bitcast.23), channel_id=1, source_target_pairs={{0,64},{64,0},{128,192},{192,128},{256,320},{320,256},{384,448},{4... | collective-permute-start | bytes 1572872 | tf_op jit(solution)/shard_map/ppermute | solution.py:304
  3.4 1.5 %copy.15 = bf16[2,64,256]{2,0,1:T(2,128)(2,1)} copy(bf16[2,64,256]{2,1,0:T(8,128)(2,1)} %param.9) | data formatting | bytes 131072 | tf_op args[0]
  4.9 21.9 %all-to-all-start = ((bf16[2,64,256]{2,0,1:T(2,128)(2,1)}), bf16[2,64,256]{2,0,1:T(2,128)(2,1)S(1)}, u32[]{:S(2)}, u32[]{:S(2)}) async-start(bf16[2,64,256]{2,0,1:T(2,128)(2,1)} %copy.15), calls=%async_computation | async-start | bytes 131072 | tf_op jit(solution)/shard_map/all_to_all | solution.py:300
  26.8 0.0 collective-permute-done.partner_ref
  26.9 0.0 copy-start.6
  26.9 0.8 copy-done.6
  27.7 3.0 %low_rank_and_columns.1 = (bf16[4,128,128]{2,1,0:T(8,128)(2,1)}, bf16[2,4,128,128]{3,2,1,0:T(8,128)(2,1)}, bf16[2,4,128,128]{3,2,1,0:T(8,128)(2,1)}, bf16[2,4,12...) custom-call(bf16[128,2048]{1,0:T(8,128)(2,1)} %bitcast.24, bf16[128,2048]{1,0:T(8,128)(2,1)} %copy-done.6, bf16[2048,256]{1,0:T(8,128)(2,1)} %bitcast.26), custom_call_target="tpu_custom_call" | custom-call | flops 270000000 | bytes 3000000 | tf_op jit(solution)/shard_map/low_rank_and_columns/pallas_call | solution.py:154
  30.6 2.1 %collective-permute-start.1 = (bf16[2,4,128,128]{3,2,1,0:T(8,128)(2,1)}, bf16[2,4,128,128]{3,2,1,0:T(8,128)(2,1)S(1)}, u32[]{:S(2)}, u32[]{:S(2)}) collective-permute-start(bf16[2,4,128,128]{3,2,1,0:T(8,128)(2,1)} %get-tuple-element.40), channel_id=1, source_target_pairs={{0,128},{64,960},{128,256},{192,64},{256,384},{320,192},{384,512},... | collective-permute-start | bytes 786440 | tf_op jit(solution)/shard_map/ppermute | solution.py:314
  32.7 5.0 %collective-permute-start.2 = (bf16[2,4,128,128]{3,2,1,0:T(8,128)(2,1)}, bf16[2,4,128,128]{3,2,1,0:T(8,128)(2,1)S(1)}, u32[]{:S(2)}, u32[]{:S(2)}) collective-permute-start(bf16[2,4,128,128]{3,2,1,0:T(8,128)(2,1)} %get-tuple-element.41), channel_id=1, source_target_pairs={{0,256},{64,832},{128,384},{192,960},{256,512},{320,64},{384,640},... | collective-permute-start | bytes 786440 | tf_op jit(solution)/shard_map/ppermute | solution.py:314
  37.7 4.6 %collective-permute-start.3 = (bf16[2,4,128,128]{3,2,1,0:T(8,128)(2,1)}, bf16[2,4,128,128]{3,2,1,0:T(8,128)(2,1)S(1)}, u32[]{:S(2)}, u32[]{:S(2)}) collective-permute-start(bf16[2,4,128,128]{3,2,1,0:T(8,128)(2,1)} %get-tuple-element.42), channel_id=1, source_target_pairs={{0,384},{64,704},{128,512},{192,832},{256,640},{320,960},{384,768}... | collective-permute-start | bytes 786440 | tf_op jit(solution)/shard_map/ppermute | solution.py:314
  42.3 1.9 %collective-permute-start.4 = (bf16[4,128,128]{2,1,0:T(8,128)(2,1)}, bf16[4,128,128]{2,1,0:T(8,128)(2,1)S(1)}, u32[]{:S(2)}, u32[]{:S(2)}) collective-permute-start(bf16[4,128,128]{2,1,0:T(8,128)(2,1)} %get-tuple-element.43), channel_id=1, source_target_pairs={{0,512},{64,576},{128,640},{192,704},{256,768},{320,832},{384,896}... | collective-permute-start | bytes 393224 | tf_op jit(solution)/shard_map/ppermute | solution.py:314
  44.2 0.0 copy-done.11
  44.2 0.6 convert_divide_fusion.inverse_ref
  44.8 0.0 all-to-all-done
  44.9 0.0 copy-done
  44.9 0.0 copy-done.1
  44.9 0.0 copy-start.2
  44.9 1.0 %copy-done.2 = bf16[1,128,2048]{2,1,0:T(8,128)(2,1)S(1)} copy-done((bf16[1,128,2048]{2,1,0:T(8,128)(2,1)S(1)}, bf16[1,128,2048]{2,1,0:T(8,128)(2,1)}, u32[]{:S(2)}) %copy-start.2) | copy-done | bytes 524312
  45.9 2.0 %rank_grad_rows.1 = bf16[8,128,512]{2,1,0:T(8,128)(2,1)} custom-call(bf16[128,256]{1,0:T(8,128)(2,1)S(1)} %reshape.33.grad_ref, bf16[128,2048]{1,0:T(8,128)(2,1)S(1)} %bitcast.25, bf16[2048,256]{1,0:T(8,128)(2,1)S(1)} %bitcast.20, bf16[256,2048]{1,0:T(8,128)(2,1)S(1)} %bitcast.22), custom_call_target="tpu_custom_call" | custom-call | flops 270000000 | bytes 3600000 | tf_op jit(solution)/shard_map/rank_grad_rows/pallas_call | solution.py:284
  47.9 7.3 %all-to-all-start.1 = ((bf16[8,128,512]{2,1,0:T(8,128)(2,1)}), bf16[8,128,512]{2,1,0:T(8,128)(2,1)S(1)}, u32[]{:S(2)}, u32[]{:S(2)}) async-start(bf16[8,128,512]{2,1,0:T(8,128)(2,1)} %rank_grad_rows.1), calls=%async_computation.1 | async-start | bytes 2097152 | tf_op jit(solution)/shard_map/all_to_all | solution.py:318
  55.2 1.9 %collective-permute-done.4.far_ref = bf16[4,128,128]{2,1,0:T(8,128)(2,1)S(1)} collective-permute-done((bf16[4,128,128]{2,1,0:T(8,128)(2,1)}, bf16[4,128,128]{2,1,0:T(8,128)(2,1)S(1)}, u32[]{:S(2)}, u32[]{:S(2)}) %collective-permute-start.4) | collective-permute-done | bytes 131104 | tf_op jit(solution)/shard_map/ppermute | solution.py:314
  57.1 0.0 copy-start.10
  57.1 0.0 collective-permute-done.1.first_ref
  57.1 0.0 copy-start.7
  57.1 0.0 collective-permute-done.2.second_ref
  57.1 0.0 copy-start.8
  57.1 0.0 collective-permute-done.3.third_ref
  57.1 0.0 copy-start.9
  57.1 0.6 copy-done.10
  57.7 0.1 copy-done.7
  57.8 0.1 copy-done.8
  57.9 0.1 copy-done.9
  58.0 2.5 %merge_rows.1 = (bf16[8,3,128,128]{3,2,1,0:T(8,128)(2,1)}, bf16[8,3,128,128]{3,2,1,0:T(8,128)(2,1)}) custom-call(bf16[4,128,128]{2,1,0:T(8,128)(2,1)} %get-tuple-element.39.self_ref, bf16[2,4,128,128]{3,2,1,0:T(8,128)(2,1)} %copy-done.7, bf16[2,4,128,128]{3,2,1,0:T(8,128)(2,1)} %copy-done.8, bf16[2,4,128,128]{3,2,1,0:T(8,128)(2,1)} %copy-done.9, ...), custom_call_target="tpu_custom_call" | custom-call | flops 1000 | bytes 1000 | tf_op jit(solution)/shard_map/merge_rows/pallas_call | solution.py:154
  60.5 15.1 %collective-permute-start.5 = (bf16[8,3,128,128]{3,2,1,0:T(8,128)(2,1)}, bf16[8,3,128,128]{3,2,1,0:T(8,128)(2,1)S(1)}, u32[]{:S(2)}, u32[]{:S(2)}) collective-permute-start(bf16[8,3,128,128]{3,2,1,0:T(8,128)(2,1)} %get-tuple-element.45), channel_id=1, source_target_pairs={{0,64},{64,0},{128,192},{192,128},{256,320},{320,256},{384,448},{4... | collective-permute-start | bytes 2359304 | tf_op jit(solution)/shard_map/ppermute | solution.py:329
  75.6 6.0 %bag_counts.1 = (bf16[2,512,1024]{2,1,0:T(8,128)(2,1)}, f32[2,1024,128]{2,1,0:T(8,128)}) custom-call(s32[8,2048]{1,0:T(8,128)} %bitcast.36, s32[1,2048]{1,0:T(1,128)} %bitcast.31, f32[1,2048]{1,0:T(1,128)} %convert_divide_fusion.inverse_ref), custom_call_target="tpu_custom_call" | custom-call | flops 32000000000 | bytes 1000 | tf_op jit(solution)/shard_map/bag_counts/pallas_call | solution.py:154
  81.6 0.0 collective-permute-done.5.taken_ref
  81.6 0.0 copy-start.5
  81.6 0.9 copy-done.5
  82.5 5.2 %saved_rows.1 = (bf16[2,1024,256]{2,1,0:T(8,128)(2,1)}, bf16[2,1024,128]{2,1,0:T(8,128)(2,1)}, bf16[2,1024,128]{2,1,0:T(8,128)(2,1)}, f32[2,1024,128]{2,1,0:T(8,...) custom-call(s32[1,16]{1,0:T(1,128)} %slots_ref.1, bf16[8,3,128,128]{3,2,1,0:T(8,128)(2,1)} %get-tuple-element.44.keep_ref, ...), custom_call_target="tpu_custom_call" | custom-call | flops 1000 | bytes 1000 | tf_op jit(solution)/shard_map/saved_rows/pallas_call | solution.py:154
  87.8 0.0 all-to-all-done.1
  87.8 0.0 copy-start.3
  87.8 1.9 %collective-permute-start.6 = (bf16[1024,512]{1,0:T(8,128)(2,1)S(1)}, bf16[1024,512]{1,0:T(8,128)(2,1)S(1)}, u32[]{:S(2)}, u32[]{:S(2)}) collective-permute-start(bf16[1024,512]{1,0:T(8,128)(2,1)S(1)} %bitcast.28), channel_id=1, source_target_pairs={{0,64},{64,0},{128,192},{192,128},{256,320},{320,256},{384,448},{4... | collective-permute-start | bytes 3145736 | tf_op jit(solution)/shard_map/ppermute | solution.py:354
  89.7 0.0 copy-done.3
  89.7 4.0 %column_half_first.1 = (f32[128,256]{1,0:T(8,128)}, f32[256,128]{1,0:T(8,128)}, f32[1,128]{1,0:T(1,128)}, f32[128,256]{1,0:T(8,128)}, f32[512,128]{1,0:T(8,128)}) custom-call(bf16[1024,512]{1,0:T(8,128)(2,1)} %bitcast.29, bf16[2,1024,256]{2,1,0:T(8,128)(2,1)} %get-tuple-element.55.refs_1_, bf16[2,1024,128]{2,1,0:T(8,128)(2,1)} %get-tuple-element.56.refs_2_, ...), custom_call_target="tpu_custom_call" | custom-call | flops 1500000000 | bytes 6000000 | tf_op jit(solution)/shard_map/column_half_first/pallas_call | solution.py:101
  93.8 0.0 collective-permute-done.6.refs_0_
  93.8 0.0 copy-start.4
  93.8 1.0 copy-done.4
  94.8 4.3 %column_half_second.1 = (f32[128,256]{1,0:T(8,128)}, f32[256,128]{1,0:T(8,128)}, f32[1,128]{1,0:T(1,128)}, f32[128,256]{1,0:T(8,128)}, f32[512,128]{1,0:T(8,128)}) custom-call(bf16[1024,512]{1,0:T(8,128)(2,1)} %copy-done.4, bf16[2,1024,256]{2,1,0:T(8,128)(2,1)} %get-tuple-element.55.refs_1_, bf16[2,1024,128]{2,1,0:T(8,128)(2,1)} %get-tuple-element.56.refs_2_, ...), custom_call_target="tpu_custom_call" | custom-call | flops 1500000000 | bytes 6000000 | tf_op jit(solution)/shard_map/column_half_second/pallas_call | solution.py:101
  (1 shorter events, 0.0 us)
Async XLA Ops:
  0.6 43.6 %copy-start.11 = (s32[1,1,2048]{2,1,0:T(1,128)S(1)}, s32[1,1,2048]{2,1,0:T(1,128)}, u32[]{:S(2)}) copy-start(s32[1,1,2048]{2,1,0:T(1,128)} %param.17) | copy-start | bytes 24580
  0.6 44.2 %copy-start = (bf16[1,2048,256]{2,1,0:T(8,128)(2,1)S(1)}, bf16[1,2048,256]{2,1,0:T(8,128)(2,1)}, u32[]{:S(2)}) copy-start(bf16[1,2048,256]{2,1,0:T(8,128)(2,1)} %param.14) | copy-start | bytes 3145732
  0.7 44.2 %copy-start.1 = (bf16[1,256,2048]{2,1,0:T(8,128)(2,1)S(1)}, bf16[1,256,2048]{2,1,0:T(8,128)(2,1)}, u32[]{:S(2)}) copy-start(bf16[1,256,2048]{2,1,0:T(8,128)(2,1)} %param.12) | copy-start | bytes 3145732
  0.7 26.2 %collective-permute-start = (bf16[128,2048]{1,0:T(8,128)(2,1)}, bf16[128,2048]{1,0:T(8,128)(2,1)S(1)}, u32[]{:S(2)}, u32[]{:S(2)}) collective-permute-start(bf16[128,2048]{1,0:T(8,128)(2,1)} %bitcast.23), channel_id=1, source_target_pairs={{0,64},{64,0},{128,192},{192,128},{256,320},{320,256},{384,448},{4... | collective-permute-start | bytes 1572872 | tf_op jit(solution)/shard_map/ppermute | solution.py:304
  4.9 39.9 %all-to-all-start = ((bf16[2,64,256]{2,0,1:T(2,128)(2,1)}), bf16[2,64,256]{2,0,1:T(2,128)(2,1)S(1)}, u32[]{:S(2)}, u32[]{:S(2)}) async-start(bf16[2,64,256]{2,0,1:T(2,128)(2,1)} %copy.15), calls=%async_computation | async-start | bytes 131072 | tf_op jit(solution)/shard_map/all_to_all | solution.py:300
  26.9 0.8 copy-start.6
  30.6 26.4 %collective-permute-start.1 = (bf16[2,4,128,128]{3,2,1,0:T(8,128)(2,1)}, bf16[2,4,128,128]{3,2,1,0:T(8,128)(2,1)S(1)}, u32[]{:S(2)}, u32[]{:S(2)}) collective-permute-start(bf16[2,4,128,128]{3,2,1,0:T(8,128)(2,1)} %get-tuple-element.40), channel_id=1, source_target_pairs={{0,128},{64,960},{128,256},{192,64},{256,384},{320,192},{384,512},... | collective-permute-start | bytes 786440 | tf_op jit(solution)/shard_map/ppermute | solution.py:314
  32.7 24.4 %collective-permute-start.2 = (bf16[2,4,128,128]{3,2,1,0:T(8,128)(2,1)}, bf16[2,4,128,128]{3,2,1,0:T(8,128)(2,1)S(1)}, u32[]{:S(2)}, u32[]{:S(2)}) collective-permute-start(bf16[2,4,128,128]{3,2,1,0:T(8,128)(2,1)} %get-tuple-element.41), channel_id=1, source_target_pairs={{0,256},{64,832},{128,384},{192,960},{256,512},{320,64},{384,640},... | collective-permute-start | bytes 786440 | tf_op jit(solution)/shard_map/ppermute | solution.py:314
  37.7 19.4 %collective-permute-start.3 = (bf16[2,4,128,128]{3,2,1,0:T(8,128)(2,1)}, bf16[2,4,128,128]{3,2,1,0:T(8,128)(2,1)S(1)}, u32[]{:S(2)}, u32[]{:S(2)}) collective-permute-start(bf16[2,4,128,128]{3,2,1,0:T(8,128)(2,1)} %get-tuple-element.42), channel_id=1, source_target_pairs={{0,384},{64,704},{128,512},{192,832},{256,640},{320,960},{384,768}... | collective-permute-start | bytes 786440 | tf_op jit(solution)/shard_map/ppermute | solution.py:314
  42.3 14.8 %collective-permute-start.4 = (bf16[4,128,128]{2,1,0:T(8,128)(2,1)}, bf16[4,128,128]{2,1,0:T(8,128)(2,1)S(1)}, u32[]{:S(2)}, u32[]{:S(2)}) collective-permute-start(bf16[4,128,128]{2,1,0:T(8,128)(2,1)} %get-tuple-element.43), channel_id=1, source_target_pairs={{0,512},{64,576},{128,640},{192,704},{256,768},{320,832},{384,896}... | collective-permute-start | bytes 393224 | tf_op jit(solution)/shard_map/ppermute | solution.py:314
  44.9 1.0 %copy-start.2 = (bf16[1,128,2048]{2,1,0:T(8,128)(2,1)S(1)}, bf16[1,128,2048]{2,1,0:T(8,128)(2,1)}, u32[]{:S(2)}) copy-start(bf16[1,128,2048]{2,1,0:T(8,128)(2,1)} %param.10) | copy-start | bytes 1572868
  47.9 39.9 %all-to-all-start.1 = ((bf16[8,128,512]{2,1,0:T(8,128)(2,1)}), bf16[8,128,512]{2,1,0:T(8,128)(2,1)S(1)}, u32[]{:S(2)}, u32[]{:S(2)}) async-start(bf16[8,128,512]{2,1,0:T(8,128)(2,1)} %rank_grad_rows.1), calls=%async_computation.1 | async-start | bytes 2097152 | tf_op jit(solution)/shard_map/all_to_all | solution.py:318
  57.1 0.7 copy-start.10
  57.1 0.7 copy-start.7
  57.1 0.8 copy-start.8
  57.1 0.9 copy-start.9
  60.5 21.1 %collective-permute-start.5 = (bf16[8,3,128,128]{3,2,1,0:T(8,128)(2,1)}, bf16[8,3,128,128]{3,2,1,0:T(8,128)(2,1)S(1)}, u32[]{:S(2)}, u32[]{:S(2)}) collective-permute-start(bf16[8,3,128,128]{3,2,1,0:T(8,128)(2,1)} %get-tuple-element.45), channel_id=1, source_target_pairs={{0,64},{64,0},{128,192},{192,128},{256,320},{320,256},{384,448},{4... | collective-permute-start | bytes 2359304 | tf_op jit(solution)/shard_map/ppermute | solution.py:329
  81.6 0.9 copy-start.5
  87.8 1.9 %copy-start.3 = (bf16[8,128,512]{2,1,0:T(8,128)(2,1)}, bf16[8,128,512]{2,1,0:T(8,128)(2,1)S(1)}, u32[]{:S(2)}) copy-start(bf16[8,128,512]{2,1,0:T(8,128)(2,1)S(1)} %all-to-all-done.1) | copy-start | bytes 3145732
  87.8 6.0 %collective-permute-start.6 = (bf16[1024,512]{1,0:T(8,128)(2,1)S(1)}, bf16[1024,512]{1,0:T(8,128)(2,1)S(1)}, u32[]{:S(2)}, u32[]{:S(2)}) collective-permute-start(bf16[1024,512]{1,0:T(8,128)(2,1)S(1)} %bitcast.28), channel_id=1, source_target_pairs={{0,64},{64,0},{128,192},{192,128},{256,320},{320,256},{384,448},{4... | collective-permute-start | bytes 3145736 | tf_op jit(solution)/shard_map/ppermute | solution.py:354
  93.8 1.0 copy-start.4

commit v5 on v4

--- a/solution.py
+++ b/solution.py
@@ -19,7 +19,8 @@
 ROOM = 60 * 1024 * 1024
 PACK_FLOPS = 270_000_000
 RANK_FLOPS = 270_000_000
-COUNTS_FLOPS = 32_000_000_000
+MERGE_FLOPS = 16_000_000_000
+COUNTS_FLOPS = 6_000_000_000
 
 NEAR = CHIPS // 2 - 1
 SAME_CORE = [[chip * CORES + core for chip in range(CHIPS)] for core in range(CORES)]
@@ -54,11 +55,13 @@
     grads_ref, low_ref, x_ref, crossed_ref, scale_ref, counts_ref, spread_ref, comp_ref, down_ref = (
         refs[:9]
     )
-    before, out_refs = refs[9:-5], refs[-5:]
+    before, out_refs, up_sum = refs[9:-6], refs[-6:-1], refs[-1]
+    sums = list(out_refs)
+    sums[1] = up_sum
 
     @pl.when(pl.program_id(0) == 0)
     def _():
-        for index, ref in enumerate(out_refs):
+        for index, ref in enumerate(sums):
             ref[...] = before[index][...] if before else jnp.zeros(ref.shape, ref.dtype)
 
     out_grad = grads_ref[:, :COMP]
@@ -73,16 +76,22 @@
     table = product(counts_ref[0], jnp.concatenate([high, rest], axis=1))
     scale_grad = (cross[:, :EMBED] * x.astype(jnp.float32)).astype(jnp.bfloat16)
     down_out, up_out, bias_out, comp_out, table_out = out_refs
+    up_sum[...] += contract_rows(scale_grad, low_ref[0])
     down_out[...] += contract_rows(x, rank_grad)
-    up_out[...] += contract_rows(low_ref[0], scale_grad)
     bias_out[...] += jnp.sum(scale_grad.astype(jnp.float32), axis=0, keepdims=True)
     comp_out[...] += contract_rows(crossed_ref[0], out_grad)
     table_out[...] += table[:, :EMBED] + table[:, EMBED:]
 
+    @pl.when(pl.program_id(0) == pl.num_programs(0) - 1)
+    def _():
+        up_out[...] = up_sum[...].T if before else up_sum[...]
+
 
 def half(side, grads, saved, before=()):
     step = HALF // STEPS
-    shapes = [(EMBED, RANK), (RANK, EMBED), (1, EMBED), (EMBED, COMP), (TABLE_ROWS, EMBED)]
+    shapes = [(EMBED, RANK), (EMBED, RANK), (1, EMBED), (EMBED, COMP), (TABLE_ROWS, EMBED)]
+    if before:
+        shapes[1] = (RANK, EMBED)
 
     def rows(width):
         return pl.BlockSpec((1, step, width), lambda i: (side, i, 0))
@@ -104,6 +113,7 @@
         in_specs=in_specs,
         out_specs=[fetched(shape) for shape in shapes],
         out_shape=[full_type(*shape) for shape in shapes],
+        scratch_shapes=[pltpu.VMEM((EMBED, RANK), jnp.float32)],
         compiler_params=pltpu.CompilerParams(vmem_limit_bytes=ROOM),
         cost_estimate=pl.CostEstimate(
             flops=1_500_000_000, bytes_accessed=6_000_000, transcendentals=0
@@ -174,21 +184,24 @@
 TILE = (4, BLOCK, EMBED)
 
 
-def merge_kernel(
-    self_ref, first_ref, second_ref, third_ref, far_ref, keep_ref, give_ref
-):
+def in_order(self_ref, first_ref, second_ref, third_ref, far_ref):
     blocks = [self_ref]
     for ref in (first_ref, second_ref, third_ref):
         blocks += [ref.at[0], ref.at[1]]
-    blocks.append(far_ref)
-    for index, block in enumerate(blocks):
-        keep_ref[index] = block[0:3]
+    return blocks + [far_ref]
+
+
+def merge_kernel(*refs):
+    give_ref = refs[-1]
+    for index, block in enumerate(in_order(*refs[:-1])):
         give_ref[index] = block[1:4]
 
 
 def counts_kernel(ids_ref, lengths_ref, inverse_ref, counts_ref, spread_ref):
     _, mine, _ = where_am_i()
     tile = 64
+    middle = TABLE_ROWS // 2
+    narrow = jnp.bfloat16
 
     @pl.loop(0, CHIPS * CORES)
     def _(block):
@@ -197,20 +210,31 @@
         to = pl.ds(pl.multiple_of(lax.div(block, CORES) * BLOCK, BLOCK), BLOCK)
         lengths = lengths_ref[:, bags]
         live = [
-            jnp.where(lengths > slot, ids_ref[slot : slot + 1, bags], -1) for slot in range(SLOTS)
+            jnp.broadcast_to(
+                jnp.where(lengths > slot, ids_ref[slot : slot + 1, bags] - middle, TABLE_ROWS)
+                .astype(jnp.float32)
+                .astype(narrow),
+                (tile, BLOCK),
+            )
+            for slot in range(SLOTS)
         ]
+        offsets = lax.broadcasted_iota(jnp.int32, (tile, BLOCK), 0).astype(jnp.float32)
         for start in range(0, TABLE_ROWS, tile):
-            row_values = start + lax.broadcasted_iota(jnp.int32, (tile, BLOCK), 0)
-            total = jnp.zeros((tile, BLOCK), jnp.float32)
+            row_values = (offsets + float(start - middle)).astype(narrow)
+            total = jnp.zeros((tile, BLOCK), narrow)
             for slot in range(SLOTS):
-                total = total + jnp.where(live[slot] == row_values, 1.0, 0.0)
-            counts_ref[side, start : start + tile, to] = total.astype(jnp.bfloat16)
+                total = total + jnp.where(live[slot] == row_values, narrow(1), narrow(0))
+            counts_ref[side, start : start + tile, to] = total
         spread_ref[side, to, :] = jnp.broadcast_to(inverse_ref[:, bags], (BLOCK, BLOCK)).T
 
 
 def saved_kernel(
     slots_ref,
-    keep_ref,
+    self_ref,
+    first_ref,
+    second_ref,
+    third_ref,
+    far_ref,
     taken_ref,
     down_ref,
     up_ref,
@@ -234,31 +258,23 @@
     down_out[...] = down_ref[served, :]
     ups = jnp.concatenate([up_ref[:, own], up_ref[:, served]], axis=1)
     bias = jnp.concatenate([bias_ref[:, own], bias_ref[:, served]], axis=1)
+    kept = in_order(self_ref, first_ref, second_ref, third_ref, far_ref)
+    for given in range(2):
+        holder = 1 - mine if given else mine
+        for index in range(CHIPS):
+            near = (index + 1) // 2
+            opposite = index % 2 == 0 and index > 0
+            side = given ^ opposite
+            k = lax.rem(chip + (2 * holder - 1) * near + CHIPS, CHIPS)
+            rows = pl.ds(pl.multiple_of(k * BLOCK, BLOCK), BLOCK)
+            if given:
+                low_low, low_high, x = (taken_ref[index, part] for part in range(3))
+            else:
+                x, low_low, low_high = (kept[index][part] for part in range(3))
+            x_ref[side, rows, :] = x
+            low_ref[side, rows, :BLOCK] = low_low
+            low_ref[side, rows, BLOCK:] = low_high
     for side in range(CORES):
-        core = mine if side == 0 else 1 - mine
-
-        @pl.loop(0, CHIPS)
-        def _(k):
-            rows = pl.ds(pl.multiple_of(k * BLOCK, BLOCK), BLOCK)
-            way = lax.rem((chip - k) * (1 - 2 * mine) + CHIPS, CHIPS)
-            given = (way > CHIPS // 2) | ((lax.rem(way, CHIPS // 2) == 0) & (core != mine))
-            near = jnp.where(way > CHIPS // 2, CHIPS - way, way)
-            holder = jnp.where(given, 1 - mine, mine)
-            inner = 2 * near - 1 + jnp.where(core == holder, 0, 1)
-            at = jnp.where(near == 0, 0, jnp.where(near == CHIPS // 2, CHIPS - 1, inner))
-
-            @pl.when(given)
-            def _():
-                x_ref[side, rows, :] = taken_ref[at, 2]
-                low_ref[side, rows, :BLOCK] = taken_ref[at, 0]
-                low_ref[side, rows, BLOCK:] = taken_ref[at, 1]
-
-            @pl.when(jnp.logical_not(given))
-            def _():
-                x_ref[side, rows, :] = keep_ref[at, 0]
-                low_ref[side, rows, :BLOCK] = keep_ref[at, 1]
-                low_ref[side, rows, BLOCK:] = keep_ref[at, 2]
-
         scale = product(low_ref[side], ups) + bias
         wide = x_ref[side].astype(jnp.float32)
         crossed_ref[side] = (wide * scale[:, :EMBED] + wide).astype(jnp.bfloat16)
@@ -324,9 +340,6 @@
         axis_index_groups=SAME_CORE,
     ).reshape(HALF, COMP + RANK)
 
-    eight = half_type(CHIPS, 3, BLOCK, EMBED)
-    keep, give = call(merge_kernel, [mine, *received], [eight, eight], "merge_rows")
-    taken = lax.ppermute(give, "tower", SWAP)
     lengths = bag_lengths[0]
     counts, spread = call(
         counts_kernel,
@@ -335,9 +348,13 @@
         "bag_counts",
         COUNTS_FLOPS,
     )
+    counts, *received = lax.optimization_barrier((counts, *received))
+    eight = half_type(CHIPS, 3, BLOCK, EMBED)
+    (give,) = call(merge_kernel, [mine, *received], [eight], "merge_rows", MERGE_FLOPS)
+    taken = lax.ppermute(give, "tower", SWAP)
     low, x, crossed, scale, comp_two, down_one = call(
         saved_kernel,
-        [keep, taken, down_mat, up_mat, cross_bias, comp_mat],
+        [mine, *received, taken, down_mat, up_mat, cross_bias, comp_mat],
         [
             half_type(CORES, HALF, RANK),
             half_type(CORES, HALF, EMBED),

time: 99.7 us -> 103 us (1.033)
  the two profiles are of different devices: /device:TPU:23 before, /device:TPU:1 now
where the time goes in v5:
time: 103 us; the launch traced here: 102 us
  starting transfers between devices  53.6 us (52%)
  Pallas kernels  25.1 us (24%)
  waiting for transfers between devices  16.4 us (16%)
  local copies, waits for them, and re-layouts  5.12 us (5%)
  other arithmetic  1.31 us (1%)
    ppermute x4, starting transfers between devices, on_device(): lax.ppermute(block, 'tower', both_ways(step))  17.3 us
    ppermute x1, starting transfers between devices, on_device(): partner = lax.ppermute(inputs, 'tower', SWAP)  16.1 us
    pallas_call x4, Pallas kernels, call(): pl.pallas_call(kernel, grid=(1,), in_specs=[SCALARS] * len(scalars) + [fe...  14.5 us
    all_to_all x1, waiting for transfers between devices, on_device(): lax.all_to_all(rows_out, 'tower', split_axis=0, concat_axis=0, tiled=True...  14.3 us
    all_to_all x1, starting transfers between devices, on_device(): lax.all_to_all(top_grad, 'hst', split_axis=1, concat_axis=0, tiled=True)  9.3 us
    pallas_call x2, Pallas kernels, half(): pl.pallas_call(half_kernel, grid=(STEPS,), in_specs=in_specs, out_specs=[...  8.61 us
    unnamed x21, local copies, waits for them, and re-layouts  5.09 us
    ppermute x1, starting transfers between devices, on_device(): taken = lax.ppermute(give, 'tower', SWAP)  4.3 us
  transfers between devices with their start and end apart: 9, of which 2 were waited for; matrix products, arithmetic and copies ran while one was open for 3% of the time, Pallas kernels for 20%

profile of v5, /device:TPU:1, one launch (start us, length us, event | category | flops | bytes accessed | tf_op | source)
XLA Modules:
  0.0 102.4 jit_solution(3019741056342834071)
XLA Ops:
  0.6 16.1 %collective-permute-start = (bf16[128,2048]{1,0:T(8,128)(2,1)}, bf16[128,2048]{1,0:T(8,128)(2,1)S(1)}, u32[]{:S(2)}, u32[]{:S(2)}) collective-permute-start(bf16[128,2048]{1,0:T(8,128)(2,1)} %bitcast.23), channel_id=1, source_target_pairs={{0,64},{64,0},{128,192},{192,128},{256,320},{320,256},{384,448},{4... | collective-permute-start | bytes 1572872 | tf_op jit(solution)/shard_map/ppermute | solution.py:320
  16.7 1.5 %copy.15 = bf16[2,64,256]{2,0,1:T(2,128)(2,1)} copy(bf16[2,64,256]{2,1,0:T(8,128)(2,1)} %param.9) | data formatting | bytes 131072 | tf_op args[0]
  18.2 9.3 %all-to-all-start = ((bf16[2,64,256]{2,0,1:T(2,128)(2,1)}), bf16[2,64,256]{2,0,1:T(2,128)(2,1)S(1)}, u32[]{:S(2)}, u32[]{:S(2)}) async-start(bf16[2,64,256]{2,0,1:T(2,128)(2,1)} %copy.15), calls=%async_computation | async-start | bytes 131072 | tf_op jit(solution)/shard_map/all_to_all | solution.py:316
  27.5 1.3 %convert_divide_fusion.inverse_ref = f32[1,2048]{1,0:T(1,128)} fusion(s32[1,1,2048]{2,1,0:T(1,128)} %param.17), kind=kLoop, calls=%fused_computation | loop fusion | flops 4096 | bytes 16384 | tf_op jit(solution)/shard_map/div | solution.py:346
  28.9 0.0 collective-permute-done.partner_ref
  28.9 0.0 copy-start.6
  28.9 0.8 copy-done.6
  29.7 3.0 %low_rank_and_columns.1 = (bf16[4,128,128]{2,1,0:T(8,128)(2,1)}, bf16[2,4,128,128]{3,2,1,0:T(8,128)(2,1)}, bf16[2,4,128,128]{3,2,1,0:T(8,128)(2,1)}, bf16[2,4,12...) custom-call(bf16[128,2048]{1,0:T(8,128)(2,1)} %bitcast.24, bf16[128,2048]{1,0:T(8,128)(2,1)} %copy-done.6, bf16[2048,256]{1,0:T(8,128)(2,1)} %bitcast.26), custom_call_target="tpu_custom_call" | custom-call | flops 270000000 | bytes 3000000 | tf_op jit(solution)/shard_map/low_rank_and_columns/pallas_call | solution.py:164
  32.7 5.1 %collective-permute-start.1 = (bf16[2,4,128,128]{3,2,1,0:T(8,128)(2,1)}, bf16[2,4,128,128]{3,2,1,0:T(8,128)(2,1)S(1)}, u32[]{:S(2)}, u32[]{:S(2)}) collective-permute-start(bf16[2,4,128,128]{3,2,1,0:T(8,128)(2,1)} %get-tuple-element.44), channel_id=1, source_target_pairs={{0,128},{64,960},{128,256},{192,64},{256,384},{320,192},{384,512},... | collective-permute-start | bytes 786440 | tf_op jit(solution)/shard_map/ppermute | solution.py:330
  37.7 3.8 %collective-permute-start.2 = (bf16[2,4,128,128]{3,2,1,0:T(8,128)(2,1)}, bf16[2,4,128,128]{3,2,1,0:T(8,128)(2,1)S(1)}, u32[]{:S(2)}, u32[]{:S(2)}) collective-permute-start(bf16[2,4,128,128]{3,2,1,0:T(8,128)(2,1)} %get-tuple-element.45), channel_id=1, source_target_pairs={{0,256},{64,832},{128,384},{192,960},{256,512},{320,64},{384,640},... | collective-permute-start | bytes 786440 | tf_op jit(solution)/shard_map/ppermute | solution.py:330
  41.5 2.7 %collective-permute-start.3 = (bf16[2,4,128,128]{3,2,1,0:T(8,128)(2,1)}, bf16[2,4,128,128]{3,2,1,0:T(8,128)(2,1)S(1)}, u32[]{:S(2)}, u32[]{:S(2)}) collective-permute-start(bf16[2,4,128,128]{3,2,1,0:T(8,128)(2,1)} %get-tuple-element.46), channel_id=1, source_target_pairs={{0,384},{64,704},{128,512},{192,832},{256,640},{320,960},{384,768}... | collective-permute-start | bytes 786440 | tf_op jit(solution)/shard_map/ppermute | solution.py:330
  44.3 5.7 %collective-permute-start.4 = (bf16[4,128,128]{2,1,0:T(8,128)(2,1)}, bf16[4,128,128]{2,1,0:T(8,128)(2,1)}, u32[]{:S(2)}, u32[]{:S(2)}) collective-permute-start(bf16[4,128,128]{2,1,0:T(8,128)(2,1)} %get-tuple-element.47), channel_id=1, source_target_pairs={{0,512},{64,576},{128,640},{192,704},{256,768},{320,832},{384,896}... | collective-permute-start | bytes 393224 | tf_op jit(solution)/shard_map/ppermute | solution.py:330
  49.9 0.0 copy-start
  50.0 0.0 copy-start.1
  50.0 0.0 copy-start.2
  50.0 4.8 %bag_counts.1 = (bf16[2,512,1024]{2,1,0:T(8,128)(2,1)}, f32[2,1024,128]{2,1,0:T(8,128)}) custom-call(s32[8,2048]{1,0:T(8,128)} %bitcast.36, s32[1,2048]{1,0:T(1,128)} %bitcast.31, f32[1,2048]{1,0:T(1,128)} %convert_divide_fusion.inverse_ref), custom_call_target="tpu_custom_call" | custom-call | flops 6000000000 | bytes 1000 | tf_op jit(solution)/shard_map/bag_counts/pallas_call | solution.py:164
  54.8 0.0 all-to-all-done
  54.9 0.0 copy-done
  54.9 0.0 copy-done.1
  54.9 0.0 copy-done.2
  54.9 2.0 %rank_grad_rows.1 = bf16[8,128,512]{2,1,0:T(8,128)(2,1)} custom-call(bf16[128,256]{1,0:T(8,128)(2,1)S(1)} %reshape.33.grad_ref, bf16[128,2048]{1,0:T(8,128)(2,1)S(1)} %bitcast.25, bf16[2048,256]{1,0:T(8,128)(2,1)S(1)} %bitcast.20, bf16[256,2048]{1,0:T(8,128)(2,1)S(1)} %bitcast.22), custom_call_target="tpu_custom_call" | custom-call | flops 270000000 | bytes 3600000 | tf_op jit(solution)/shard_map/rank_grad_rows/pallas_call | solution.py:300
  56.9 3.6 %all-to-all-start.1 = ((bf16[8,128,512]{2,1,0:T(8,128)(2,1)}), bf16[8,128,512]{2,1,0:T(8,128)(2,1)S(1)}, u32[]{:S(2)}, u32[]{:S(2)}) async-start(bf16[8,128,512]{2,1,0:T(8,128)(2,1)} %rank_grad_rows.1), calls=%async_computation.1 | async-start | bytes 2097152 | tf_op jit(solution)/shard_map/all_to_all | solution.py:334
  60.4 0.0 collective-permute-done.4.refs_4_.far_ref
  60.5 0.0 collective-permute-done.1.refs_1_.first_ref
  60.5 0.0 copy-start.7
  60.5 0.0 collective-permute-done.2.refs_2_.second_ref
  60.5 0.0 copy-start.8
  60.5 0.0 collective-permute-done.3.refs_3_.third_ref
  60.5 0.0 copy-start.9
  60.5 0.7 copy-done.7
  61.2 0.1 copy-done.8
  61.3 0.1 copy-done.9
  61.4 2.1 %merge_rows.1 = bf16[8,3,128,128]{3,2,1,0:T(8,128)(2,1)} custom-call(bf16[4,128,128]{2,1,0:T(8,128)(2,1)} %get-tuple-element.42.refs_0_.self_ref, bf16[2,4,128,128]{3,2,1,0:T(8,128)(2,1)} %copy-done.7, bf16[2,4,128,128]{3,2,1,0:T(8,128)(2,1)} %copy-done.8, bf16[2,4,128,128]{3,2,1,0:T(8,128)(2,1)} %copy-done.9, ...), custom_call_target="tpu_custom_call" | custom-call | flops 16000000000 | bytes 1000 | tf_op jit(solution)/shard_map/merge_rows/pallas_call | solution.py:164
  63.5 4.3 %collective-permute-start.5 = (bf16[8,3,128,128]{3,2,1,0:T(8,128)(2,1)}, bf16[8,3,128,128]{3,2,1,0:T(8,128)(2,1)S(1)}, u32[]{:S(2)}, u32[]{:S(2)}) collective-permute-start(bf16[8,3,128,128]{3,2,1,0:T(8,128)(2,1)} %merge_rows.1), channel_id=1, source_target_pairs={{0,64},{64,0},{128,192},{192,128},{256,320},{320,256},{384,448},{4... | collective-permute-start | bytes 2359304 | tf_op jit(solution)/shard_map/ppermute | solution.py:354
  67.8 2.1 %collective-permute-done.5.taken_ref = bf16[8,3,128,128]{3,2,1,0:T(8,128)(2,1)S(1)} collective-permute-done((bf16[8,3,128,128]{3,2,1,0:T(8,128)(2,1)}, bf16[8,3,128,128]{3,2,1,0:T(8,128)(2,1)S(1)}, u32[]{:S(2)}, u32[]{:S(2)}) %collective-permute-start.5) | collective-permute-done | bytes 786464 | tf_op jit(solution)/shard_map/ppermute | solution.py:354
  69.9 0.0 copy-start.5
  69.9 0.9 copy-done.5
  70.8 4.6 %saved_rows.1 = (bf16[2,1024,256]{2,1,0:T(8,128)(2,1)}, bf16[2,1024,128]{2,1,0:T(8,128)(2,1)}, bf16[2,1024,128]{2,1,0:T(8,128)(2,1)}, f32[2,1024,128]{2,1,0:T(8,...) custom-call(s32[1,16]{1,0:T(1,128)} %slots_ref.1, bf16[4,128,128]{2,1,0:T(8,128)(2,1)} %get-tuple-element.42.refs_0_.self_ref, ...), custom_call_target="tpu_custom_call" | custom-call | flops 1000 | bytes 1000 | tf_op jit(solution)/shard_map/saved_rows/pallas_call | solution.py:164
  75.3 14.3 %all-to-all-done.1 = bf16[8,128,512]{2,1,0:T(8,128)(2,1)S(1)} async-done(((bf16[8,128,512]{2,1,0:T(8,128)(2,1)}), bf16[8,128,512]{2,1,0:T(8,128)(2,1)S(1)}, u32[]{:S(2)}, u32[]{:S(2)}) %all-to-all-start.1) | async-done | bytes 1048608 | tf_op jit(solution)/shard_map/all_to_all | solution.py:334
  89.7 0.0 copy-start.3
  89.7 3.1 %collective-permute-start.6 = (bf16[1024,512]{1,0:T(8,128)(2,1)S(1)}, bf16[1024,512]{1,0:T(8,128)(2,1)S(1)}, u32[]{:S(2)}, u32[]{:S(2)}) collective-permute-start(bf16[1024,512]{1,0:T(8,128)(2,1)S(1)} %bitcast.28), channel_id=1, source_target_pairs={{0,64},{64,0},{128,192},{192,128},{256,320},{320,256},{384,448},{4... | collective-permute-start | bytes 3145736 | tf_op jit(solution)/shard_map/ppermute | solution.py:371
  92.8 0.0 copy-done.3
  92.8 4.1 %column_half_first.1 = (f32[128,256]{1,0:T(8,128)}, f32[128,256]{1,0:T(8,128)}, f32[1,128]{1,0:T(1,128)}, f32[128,256]{1,0:T(8,128)}, f32[512,128]{1,0:T(8,128)}) custom-call(bf16[1024,512]{1,0:T(8,128)(2,1)} %bitcast.29, bf16[2,1024,256]{2,1,0:T(8,128)(2,1)} %get-tuple-element.61.refs_1_, bf16[2,1024,128]{2,1,0:T(8,128)(2,1)} %get-tuple-element.62.refs_2_, ...), custom_call_target="tpu_custom_call" | custom-call | flops 1500000000 | bytes 6000000 | tf_op jit(solution)/shard_map/column_half_first/pallas_call | solution.py:110
  96.9 0.0 collective-permute-done.6.refs_0_
  96.9 0.0 copy-start.4
  96.9 1.0 copy-done.4
  97.9 4.5 %column_half_second.1 = (f32[128,256]{1,0:T(8,128)}, f32[256,128]{1,0:T(8,128)}, f32[1,128]{1,0:T(1,128)}, f32[128,256]{1,0:T(8,128)}, f32[512,128]{1,0:T(8,128)}) custom-call(bf16[1024,512]{1,0:T(8,128)(2,1)} %copy-done.4, bf16[2,1024,256]{2,1,0:T(8,128)(2,1)} %get-tuple-element.61.refs_1_, bf16[2,1024,128]{2,1,0:T(8,128)(2,1)} %get-tuple-element.62.refs_2_, ...), custom_call_target="tpu_custom_call" | custom-call | flops 1500000000 | bytes 6000000 | tf_op jit(solution)/shard_map/column_half_second/pallas_call | solution.py:110
  (1 shorter events, 0.0 us)
Async XLA Ops:
  0.6 28.2 %collective-permute-start = (bf16[128,2048]{1,0:T(8,128)(2,1)}, bf16[128,2048]{1,0:T(8,128)(2,1)S(1)}, u32[]{:S(2)}, u32[]{:S(2)}) collective-permute-start(bf16[128,2048]{1,0:T(8,128)(2,1)} %bitcast.23), channel_id=1, source_target_pairs={{0,64},{64,0},{128,192},{192,128},{256,320},{320,256},{384,448},{4... | collective-permute-start | bytes 1572872 | tf_op jit(solution)/shard_map/ppermute | solution.py:320
  18.2 36.6 %all-to-all-start = ((bf16[2,64,256]{2,0,1:T(2,128)(2,1)}), bf16[2,64,256]{2,0,1:T(2,128)(2,1)S(1)}, u32[]{:S(2)}, u32[]{:S(2)}) async-start(bf16[2,64,256]{2,0,1:T(2,128)(2,1)} %copy.15), calls=%async_computation | async-start | bytes 131072 | tf_op jit(solution)/shard_map/all_to_all | solution.py:316
  28.9 0.8 copy-start.6
  32.7 27.8 %collective-permute-start.1 = (bf16[2,4,128,128]{3,2,1,0:T(8,128)(2,1)}, bf16[2,4,128,128]{3,2,1,0:T(8,128)(2,1)S(1)}, u32[]{:S(2)}, u32[]{:S(2)}) collective-permute-start(bf16[2,4,128,128]{3,2,1,0:T(8,128)(2,1)} %get-tuple-element.44), channel_id=1, source_target_pairs={{0,128},{64,960},{128,256},{192,64},{256,384},{320,192},{384,512},... | collective-permute-start | bytes 786440 | tf_op jit(solution)/shard_map/ppermute | solution.py:330
  37.7 22.7 %collective-permute-start.2 = (bf16[2,4,128,128]{3,2,1,0:T(8,128)(2,1)}, bf16[2,4,128,128]{3,2,1,0:T(8,128)(2,1)S(1)}, u32[]{:S(2)}, u32[]{:S(2)}) collective-permute-start(bf16[2,4,128,128]{3,2,1,0:T(8,128)(2,1)} %get-tuple-element.45), channel_id=1, source_target_pairs={{0,256},{64,832},{128,384},{192,960},{256,512},{320,64},{384,640},... | collective-permute-start | bytes 786440 | tf_op jit(solution)/shard_map/ppermute | solution.py:330
  41.5 19.0 %collective-permute-start.3 = (bf16[2,4,128,128]{3,2,1,0:T(8,128)(2,1)}, bf16[2,4,128,128]{3,2,1,0:T(8,128)(2,1)S(1)}, u32[]{:S(2)}, u32[]{:S(2)}) collective-permute-start(bf16[2,4,128,128]{3,2,1,0:T(8,128)(2,1)} %get-tuple-element.46), channel_id=1, source_target_pairs={{0,384},{64,704},{128,512},{192,832},{256,640},{320,960},{384,768}... | collective-permute-start | bytes 786440 | tf_op jit(solution)/shard_map/ppermute | solution.py:330
  44.3 16.2 %collective-permute-start.4 = (bf16[4,128,128]{2,1,0:T(8,128)(2,1)}, bf16[4,128,128]{2,1,0:T(8,128)(2,1)}, u32[]{:S(2)}, u32[]{:S(2)}) collective-permute-start(bf16[4,128,128]{2,1,0:T(8,128)(2,1)} %get-tuple-element.47), channel_id=1, source_target_pairs={{0,512},{64,576},{128,640},{192,704},{256,768},{320,832},{384,896}... | collective-permute-start | bytes 393224 | tf_op jit(solution)/shard_map/ppermute | solution.py:330
  49.9 4.9 %copy-start = (bf16[1,2048,256]{2,1,0:T(8,128)(2,1)S(1)}, bf16[1,2048,256]{2,1,0:T(8,128)(2,1)}, u32[]{:S(2)}) copy-start(bf16[1,2048,256]{2,1,0:T(8,128)(2,1)} %param.14) | copy-start | bytes 3145732
  50.0 4.9 %copy-start.1 = (bf16[1,256,2048]{2,1,0:T(8,128)(2,1)S(1)}, bf16[1,256,2048]{2,1,0:T(8,128)(2,1)}, u32[]{:S(2)}) copy-start(bf16[1,256,2048]{2,1,0:T(8,128)(2,1)} %param.12) | copy-start | bytes 3145732
  50.0 4.9 %copy-start.2 = (bf16[1,128,2048]{2,1,0:T(8,128)(2,1)S(1)}, bf16[1,128,2048]{2,1,0:T(8,128)(2,1)}, u32[]{:S(2)}) copy-start(bf16[1,128,2048]{2,1,0:T(8,128)(2,1)} %param.10) | copy-start | bytes 1572868
  56.9 32.8 %all-to-all-start.1 = ((bf16[8,128,512]{2,1,0:T(8,128)(2,1)}), bf16[8,128,512]{2,1,0:T(8,128)(2,1)S(1)}, u32[]{:S(2)}, u32[]{:S(2)}) async-start(bf16[8,128,512]{2,1,0:T(8,128)(2,1)} %rank_grad_rows.1), calls=%async_computation.1 | async-start | bytes 2097152 | tf_op jit(solution)/shard_map/all_to_all | solution.py:334
  60.5 0.7 copy-start.7
  60.5 0.8 copy-start.8
  60.5 0.8 copy-start.9
  63.5 6.4 %collective-permute-start.5 = (bf16[8,3,128,128]{3,2,1,0:T(8,128)(2,1)}, bf16[8,3,128,128]{3,2,1,0:T(8,128)(2,1)S(1)}, u32[]{:S(2)}, u32[]{:S(2)}) collective-permute-start(bf16[8,3,128,128]{3,2,1,0:T(8,128)(2,1)} %merge_rows.1), channel_id=1, source_target_pairs={{0,64},{64,0},{128,192},{192,128},{256,320},{320,256},{384,448},{4... | collective-permute-start | bytes 2359304 | tf_op jit(solution)/shard_map/ppermute | solution.py:354
  69.9 0.9 copy-start.5
  89.7 3.1 %copy-start.3 = (bf16[8,128,512]{2,1,0:T(8,128)(2,1)}, bf16[8,128,512]{2,1,0:T(8,128)(2,1)S(1)}, u32[]{:S(2)}) copy-start(bf16[8,128,512]{2,1,0:T(8,128)(2,1)S(1)} %all-to-all-done.1) | copy-start | bytes 3145732
  89.7 7.3 %collective-permute-start.6 = (bf16[1024,512]{1,0:T(8,128)(2,1)S(1)}, bf16[1024,512]{1,0:T(8,128)(2,1)S(1)}, u32[]{:S(2)}, u32[]{:S(2)}) collective-permute-start(bf16[1024,512]{1,0:T(8,128)(2,1)S(1)} %bitcast.28), channel_id=1, source_target_pairs={{0,64},{64,0},{128,192},{192,128},{256,320},{320,256},{384,448},{4... | collective-permute-start | bytes 3145736 | tf_op jit(solution)/shard_map/ppermute | solution.py:371
  96.9 1.0 copy-start.4

commit v6 on v5

--- a/solution.py
+++ b/solution.py
@@ -17,10 +17,11 @@
 
 STEPS = 2
 ROOM = 60 * 1024 * 1024
+HALF_ROOM = 60 * 1024 * 1024
 PACK_FLOPS = 270_000_000
 RANK_FLOPS = 270_000_000
 MERGE_FLOPS = 16_000_000_000
-COUNTS_FLOPS = 6_000_000_000
+COUNTS_FLOPS = 500_000_000
 
 NEAR = CHIPS // 2 - 1
 SAME_CORE = [[chip * CORES + core for chip in range(CHIPS)] for core in range(CORES)]
@@ -114,7 +115,7 @@
         out_specs=[fetched(shape) for shape in shapes],
         out_shape=[full_type(*shape) for shape in shapes],
         scratch_shapes=[pltpu.VMEM((EMBED, RANK), jnp.float32)],
-        compiler_params=pltpu.CompilerParams(vmem_limit_bytes=ROOM),
+        compiler_params=pltpu.CompilerParams(vmem_limit_bytes=HALF_ROOM),
         cost_estimate=pl.CostEstimate(
             flops=1_500_000_000, bytes_accessed=6_000_000, transcendentals=0
         ),
@@ -197,7 +198,7 @@
         give_ref[index] = block[1:4]
 
 
-def counts_kernel(ids_ref, lengths_ref, inverse_ref, counts_ref, spread_ref):
+def counts_kernel(ids_ref, lengths_ref, counts_ref, spread_ref):
     _, mine, _ = where_am_i()
     tile = 64
     middle = TABLE_ROWS // 2
@@ -225,7 +226,9 @@
             for slot in range(SLOTS):
                 total = total + jnp.where(live[slot] == row_values, narrow(1), narrow(0))
             counts_ref[side, start : start + tile, to] = total
-        spread_ref[side, to, :] = jnp.broadcast_to(inverse_ref[:, bags], (BLOCK, BLOCK)).T
+        spread_ref[side, to, :] = jnp.broadcast_to(
+            1.0 / lengths.astype(jnp.float32), (BLOCK, BLOCK)
+        ).T
 
 
 def saved_kernel(
@@ -331,6 +334,15 @@
     ]
 
     rows_out = rank_rows(out_grad, inputs, comp_mat, up_mat)
+    rows_out, ids, lengths = lax.optimization_barrier((rows_out, bag_ids[0, 0], bag_lengths[0]))
+    counts, spread = call(
+        counts_kernel,
+        [jnp.transpose(ids), lengths],
+        [half_type(CORES, TABLE_ROWS, HALF), full_type(CORES, HALF, EMBED)],
+        "bag_counts",
+        COUNTS_FLOPS,
+    )
+    counts, *received = lax.optimization_barrier((counts, *received))
     grads_own = lax.all_to_all(
         rows_out,
         "tower",
@@ -340,15 +352,6 @@
         axis_index_groups=SAME_CORE,
     ).reshape(HALF, COMP + RANK)
 
-    lengths = bag_lengths[0]
-    counts, spread = call(
-        counts_kernel,
-        [jnp.transpose(bag_ids[0, 0]), lengths, 1.0 / lengths.astype(jnp.float32)],
-        [half_type(CORES, TABLE_ROWS, HALF), full_type(CORES, HALF, EMBED)],
-        "bag_counts",
-        COUNTS_FLOPS,
-    )
-    counts, *received = lax.optimization_barrier((counts, *received))
     eight = half_type(CHIPS, 3, BLOCK, EMBED)
     (give,) = call(merge_kernel, [mine, *received], [eight], "merge_rows", MERGE_FLOPS)
     taken = lax.ppermute(give, "tower", SWAP)

time: 103 us -> 98.1 us (0.952)
  waiting for transfers between devices: 16.4 us -> 9.26 us
  Pallas kernels: 25.1 us -> 26.6 us
  other arithmetic: 1.31 us -> 0 us
  local copies, waits for them, and re-layouts: 5.12 us -> 6.15 us
    all_to_all x1, waiting for transfers between devices: 14.3 us -> 7.15 us  [on_device(): lax.all_to_all(rows_out, 'tower', split_axis=0, concat_axis=0, tiled=True...]
    pallas_call x4, Pallas kernels: 14.5 us -> 16 us  [call(): pl.pallas_call(kernel, grid=(1,), in_specs=[SCALARS] * len(scalars) + [fe...]
    ppermute x1, starting transfers between devices: 4.3 us -> 5.7 us  [on_device(): taken = lax.ppermute(give, 'tower', SWAP)]
    div x1 -> x0, other arithmetic: 1.31 us -> none  [on_device(): 1.0 / lengths.astype(jnp.float32)]
    unnamed x21 -> x23, local copies, waits for them, and re-layouts: 5.09 us -> 6.12 us
  transfers between devices with their start and end apart: 9 -> 9, of which waited for: 2 -> 2; matrix products, arithmetic and copies ran while one was open for 3% -> 2% of each run, Pallas kernels for 20% -> 23%
where the time goes in v6:
time: 98.1 us; the launch traced here: 97.5 us
  starting transfers between devices  54.6 us (56%)
  Pallas kernels  26.6 us (27%)
  waiting for transfers between devices  9.26 us (9%)
  local copies, waits for them, and re-layouts  6.15 us (6%)
    ppermute x4, starting transfers between devices, on_device(): lax.ppermute(block, 'tower', both_ways(step))  17.3 us
    ppermute x1, starting transfers between devices, on_device(): partner = lax.ppermute(inputs, 'tower', SWAP)  16.2 us
    pallas_call x4, Pallas kernels, call(): pl.pallas_call(kernel, grid=(1,), in_specs=[SCALARS] * len(scalars) + [fe...  16 us
    all_to_all x1, starting transfers between devices, on_device(): lax.all_to_all(top_grad, 'hst', split_axis=1, concat_axis=0, tiled=True)  9.3 us
    pallas_call x2, Pallas kernels, half(): pl.pallas_call(half_kernel, grid=(STEPS,), in_specs=in_specs, out_specs=[...  8.62 us
    all_to_all x1, waiting for transfers between devices, on_device(): lax.all_to_all(rows_out, 'tower', split_axis=0, concat_axis=0, tiled=True...  7.15 us
    unnamed x23, local copies, waits for them, and re-layouts  6.12 us
    ppermute x1, starting transfers between devices, on_device(): taken = lax.ppermute(give, 'tower', SWAP)  5.7 us
  transfers between devices with their start and end apart: 9, of which 2 were waited for; matrix products, arithmetic and copies ran while one was open for 2% of the time, Pallas kernels for 23%

profile of v6, /device:TPU:1, one launch (start us, length us, event | category | flops | bytes accessed | tf_op | source)
XLA Modules:
  0.0 97.5 jit_solution(2598087829821467179)
XLA Ops:
  0.6 0.0 copy-start
  0.6 0.0 copy-start.1
  0.7 16.2 %collective-permute-start = (bf16[128,2048]{1,0:T(8,128)(2,1)}, bf16[128,2048]{1,0:T(8,128)(2,1)S(1)}, u32[]{:S(2)}, u32[]{:S(2)}) collective-permute-start(bf16[128,2048]{1,0:T(8,128)(2,1)} %bitcast.21), channel_id=1, source_target_pairs={{0,64},{64,0},{128,192},{192,128},{256,320},{320,256},{384,448},{4... | collective-permute-start | bytes 1572872 | tf_op jit(solution)/shard_map/ppermute | solution.py:323
  16.9 1.5 %copy.15 = bf16[2,64,256]{2,0,1:T(2,128)(2,1)} copy(bf16[2,64,256]{2,1,0:T(8,128)(2,1)} %param.9) | data formatting | bytes 131072 | tf_op args[0]
  18.4 9.3 %all-to-all-start = ((bf16[2,64,256]{2,0,1:T(2,128)(2,1)}), bf16[2,64,256]{2,0,1:T(2,128)(2,1)S(1)}, u32[]{:S(2)}, u32[]{:S(2)}) async-start(bf16[2,64,256]{2,0,1:T(2,128)(2,1)} %copy.15), calls=%async_computation | async-start | bytes 131072 | tf_op jit(solution)/shard_map/all_to_all | solution.py:319
  27.7 0.0 collective-permute-done.partner_ref
  27.7 0.0 copy-start.6
  27.7 0.8 copy-done.6
  28.5 3.0 %low_rank_and_columns.1 = (bf16[4,128,128]{2,1,0:T(8,128)(2,1)}, bf16[2,4,128,128]{3,2,1,0:T(8,128)(2,1)}, bf16[2,4,128,128]{3,2,1,0:T(8,128)(2,1)}, bf16[2,4,12...) custom-call(bf16[128,2048]{1,0:T(8,128)(2,1)} %bitcast.22, bf16[128,2048]{1,0:T(8,128)(2,1)} %copy-done.6, bf16[2048,256]{1,0:T(8,128)(2,1)} %bitcast.24), custom_call_target="tpu_custom_call" | custom-call | flops 270000000 | bytes 3000000 | tf_op jit(solution)/shard_map/low_rank_and_columns/pallas_call | solution.py:165
  31.5 5.1 %collective-permute-start.1 = (bf16[2,4,128,128]{3,2,1,0:T(8,128)(2,1)}, bf16[2,4,128,128]{3,2,1,0:T(8,128)(2,1)S(1)}, u32[]{:S(2)}, u32[]{:S(2)}) collective-permute-start(bf16[2,4,128,128]{3,2,1,0:T(8,128)(2,1)} %get-tuple-element.50), channel_id=1, source_target_pairs={{0,128},{64,960},{128,256},{192,64},{256,384},{320,192},{384,512},... | collective-permute-start | bytes 786440 | tf_op jit(solution)/shard_map/ppermute | solution.py:333
  36.6 3.8 %collective-permute-start.2 = (bf16[2,4,128,128]{3,2,1,0:T(8,128)(2,1)}, bf16[2,4,128,128]{3,2,1,0:T(8,128)(2,1)S(1)}, u32[]{:S(2)}, u32[]{:S(2)}) collective-permute-start(bf16[2,4,128,128]{3,2,1,0:T(8,128)(2,1)} %get-tuple-element.51), channel_id=1, source_target_pairs={{0,256},{64,832},{128,384},{192,960},{256,512},{320,64},{384,640},... | collective-permute-start | bytes 786440 | tf_op jit(solution)/shard_map/ppermute | solution.py:333
  40.4 2.7 %collective-permute-start.3 = (bf16[2,4,128,128]{3,2,1,0:T(8,128)(2,1)}, bf16[2,4,128,128]{3,2,1,0:T(8,128)(2,1)S(1)}, u32[]{:S(2)}, u32[]{:S(2)}) collective-permute-start(bf16[2,4,128,128]{3,2,1,0:T(8,128)(2,1)} %get-tuple-element.52), channel_id=1, source_target_pairs={{0,384},{64,704},{128,512},{192,832},{256,640},{320,960},{384,768}... | collective-permute-start | bytes 786440 | tf_op jit(solution)/shard_map/ppermute | solution.py:333
  43.1 5.7 %collective-permute-start.4 = (bf16[4,128,128]{2,1,0:T(8,128)(2,1)}, bf16[4,128,128]{2,1,0:T(8,128)(2,1)S(1)}, u32[]{:S(2)}, u32[]{:S(2)}) collective-permute-start(bf16[4,128,128]{2,1,0:T(8,128)(2,1)} %get-tuple-element.53), channel_id=1, source_target_pairs={{0,512},{64,576},{128,640},{192,704},{256,768},{320,832},{384,896}... | collective-permute-start | bytes 393224 | tf_op jit(solution)/shard_map/ppermute | solution.py:333
  48.8 0.0 all-to-all-done
  48.8 0.0 copy-done
  48.8 0.0 copy-done.1
  48.9 0.0 copy-start.2
  48.9 1.0 %copy-done.2 = bf16[1,128,2048]{2,1,0:T(8,128)(2,1)S(1)} copy-done((bf16[1,128,2048]{2,1,0:T(8,128)(2,1)S(1)}, bf16[1,128,2048]{2,1,0:T(8,128)(2,1)}, u32[]{:S(2)}) %copy-start.2) | copy-done | bytes 524312
  49.9 2.0 %rank_grad_rows.1 = bf16[8,128,512]{2,1,0:T(8,128)(2,1)} custom-call(bf16[128,256]{1,0:T(8,128)(2,1)S(1)} %reshape.17.grad_ref, bf16[128,2048]{1,0:T(8,128)(2,1)S(1)} %bitcast.23, bf16[2048,256]{1,0:T(8,128)(2,1)S(1)} %bitcast.18, bf16[256,2048]{1,0:T(8,128)(2,1)S(1)} %bitcast.20), custom_call_target="tpu_custom_call" | custom-call | flops 270000000 | bytes 3600000 | tf_op jit(solution)/shard_map/rank_grad_rows/pallas_call | solution.py:303
  51.9 3.6 %all-to-all-start.1 = ((bf16[8,128,512]{2,1,0:T(8,128)(2,1)}), bf16[8,128,512]{2,1,0:T(8,128)(2,1)S(1)}, u32[]{:S(2)}, u32[]{:S(2)}) async-start(bf16[8,128,512]{2,1,0:T(8,128)(2,1)} %rank_grad_rows.1), calls=%async_computation.1 | async-start | bytes 2097152 | tf_op jit(solution)/shard_map/all_to_all | solution.py:346
  55.4 6.3 %bag_counts.1 = (bf16[2,512,1024]{2,1,0:T(8,128)(2,1)}, f32[2,1024,128]{2,1,0:T(8,128)}) custom-call(s32[8,2048]{1,0:T(8,128)} %bitcast.33, s32[1,2048]{1,0:T(1,128)} %bitcast.34), custom_call_target="tpu_custom_call" | custom-call | flops 500000000 | bytes 1000 | tf_op jit(solution)/shard_map/bag_counts/pallas_call | solution.py:165
  61.7 0.0 collective-permute-done.4.refs_4_.far_ref
  61.7 0.0 copy-start.10
  61.7 0.0 collective-permute-done.1.refs_1_.first_ref
  61.7 0.0 copy-start.7
  61.7 0.0 collective-permute-done.2.refs_2_.second_ref
  61.7 0.0 copy-start.8
  61.7 0.0 collective-permute-done.3.refs_3_.third_ref
  61.8 0.0 copy-start.9
  61.8 0.6 copy-done.10
  62.4 0.1 copy-done.7
  62.5 0.1 copy-done.8
  62.6 0.0 copy-done.9
  62.6 2.1 %merge_rows.1 = bf16[8,3,128,128]{3,2,1,0:T(8,128)(2,1)} custom-call(bf16[4,128,128]{2,1,0:T(8,128)(2,1)} %get-tuple-element.46.refs_0_.self_ref, bf16[2,4,128,128]{3,2,1,0:T(8,128)(2,1)} %copy-done.7, bf16[2,4,128,128]{3,2,1,0:T(8,128)(2,1)} %copy-done.8, bf16[2,4,128,128]{3,2,1,0:T(8,128)(2,1)} %copy-done.9, bf16[4,128,128]{2,1,0:T(8,128)(2,1)} %copy-done.10), custom_call_target="tpu_custom_call" | custom-call | flops 16000000000 | bytes 1000 | tf_op jit(solution)/shard_map/merge_rows/pallas_call | solution.py:165
  64.8 5.7 %collective-permute-start.5 = (bf16[8,3,128,128]{3,2,1,0:T(8,128)(2,1)}, bf16[8,3,128,128]{3,2,1,0:T(8,128)(2,1)S(1)}, u32[]{:S(2)}, u32[]{:S(2)}) collective-permute-start(bf16[8,3,128,128]{3,2,1,0:T(8,128)(2,1)} %merge_rows.1), channel_id=1, source_target_pairs={{0,64},{64,0},{128,192},{192,128},{256,320},{320,256},{384,448},{4... | collective-permute-start | bytes 2359304 | tf_op jit(solution)/shard_map/ppermute | solution.py:357
  70.5 2.1 %collective-permute-done.5.taken_ref = bf16[8,3,128,128]{3,2,1,0:T(8,128)(2,1)S(1)} collective-permute-done((bf16[8,3,128,128]{3,2,1,0:T(8,128)(2,1)}, bf16[8,3,128,128]{3,2,1,0:T(8,128)(2,1)S(1)}, u32[]{:S(2)}, u32[]{:S(2)}) %collective-permute-start.5) | collective-permute-done | bytes 786464 | tf_op jit(solution)/shard_map/ppermute | solution.py:357
  72.6 0.0 copy-start.5
  72.6 0.9 copy-done.5
  73.4 4.6 %saved_rows.1 = (bf16[2,1024,256]{2,1,0:T(8,128)(2,1)}, bf16[2,1024,128]{2,1,0:T(8,128)(2,1)}, bf16[2,1024,128]{2,1,0:T(8,128)(2,1)}, f32[2,1024,128]{2,1,0:T(8,...) custom-call(s32[1,16]{1,0:T(1,128)} %slots_ref.1, bf16[4,128,128]{2,1,0:T(8,128)(2,1)} %get-tuple-element.46.refs_0_.self_ref, ...), custom_call_target="tpu_custom_call" | custom-call | flops 1000 | bytes 1000 | tf_op jit(solution)/shard_map/saved_rows/pallas_call | solution.py:165
  78.1 7.1 %all-to-all-done.1 = bf16[8,128,512]{2,1,0:T(8,128)(2,1)S(1)} async-done(((bf16[8,128,512]{2,1,0:T(8,128)(2,1)}), bf16[8,128,512]{2,1,0:T(8,128)(2,1)S(1)}, u32[]{:S(2)}, u32[]{:S(2)}) %all-to-all-start.1) | async-done | bytes 1048608 | tf_op jit(solution)/shard_map/all_to_all | solution.py:346
  85.2 0.0 copy-start.3
  85.2 2.6 %collective-permute-start.6 = (bf16[1024,512]{1,0:T(8,128)(2,1)S(1)}, bf16[1024,512]{1,0:T(8,128)(2,1)S(1)}, u32[]{:S(2)}, u32[]{:S(2)}) collective-permute-start(bf16[1024,512]{1,0:T(8,128)(2,1)S(1)} %bitcast.26), channel_id=1, source_target_pairs={{0,64},{64,0},{128,192},{192,128},{256,320},{320,256},{384,448},{4... | collective-permute-start | bytes 3145736 | tf_op jit(solution)/shard_map/ppermute | solution.py:374
  87.8 0.0 copy-done.3
  87.9 4.2 %column_half_first.1 = (f32[128,256]{1,0:T(8,128)}, f32[128,256]{1,0:T(8,128)}, f32[1,128]{1,0:T(1,128)}, f32[128,256]{1,0:T(8,128)}, f32[512,128]{1,0:T(8,128)}) custom-call(bf16[1024,512]{1,0:T(8,128)(2,1)} %bitcast.27, bf16[2,1024,256]{2,1,0:T(8,128)(2,1)} %get-tuple-element.67.refs_1_, bf16[2,1024,128]{2,1,0:T(8,128)(2,1)} %get-tuple-element.68.refs_2_, ...), custom_call_target="tpu_custom_call" | custom-call | flops 1500000000 | bytes 6000000 | tf_op jit(solution)/shard_map/column_half_first/pallas_call | solution.py:111
  92.0 0.0 collective-permute-done.6.refs_0_
  92.0 0.0 copy-start.4
  92.0 1.0 copy-done.4
  93.0 4.5 %column_half_second.1 = (f32[128,256]{1,0:T(8,128)}, f32[256,128]{1,0:T(8,128)}, f32[1,128]{1,0:T(1,128)}, f32[128,256]{1,0:T(8,128)}, f32[512,128]{1,0:T(8,128)}) custom-call(bf16[1024,512]{1,0:T(8,128)(2,1)} %copy-done.4, bf16[2,1024,256]{2,1,0:T(8,128)(2,1)} %get-tuple-element.67.refs_1_, bf16[2,1024,128]{2,1,0:T(8,128)(2,1)} %get-tuple-element.68.refs_2_, ...), custom_call_target="tpu_custom_call" | custom-call | flops 1500000000 | bytes 6000000 | tf_op jit(solution)/shard_map/column_half_second/pallas_call | solution.py:111
  (1 shorter events, 0.0 us)
Async XLA Ops:
  0.6 48.2 %copy-start = (bf16[1,2048,256]{2,1,0:T(8,128)(2,1)S(1)}, bf16[1,2048,256]{2,1,0:T(8,128)(2,1)}, u32[]{:S(2)}) copy-start(bf16[1,2048,256]{2,1,0:T(8,128)(2,1)} %param.14) | copy-start | bytes 3145732
  0.6 48.2 %copy-start.1 = (bf16[1,256,2048]{2,1,0:T(8,128)(2,1)S(1)}, bf16[1,256,2048]{2,1,0:T(8,128)(2,1)}, u32[]{:S(2)}) copy-start(bf16[1,256,2048]{2,1,0:T(8,128)(2,1)} %param.12) | copy-start | bytes 3145732
  0.7 27.1 %collective-permute-start = (bf16[128,2048]{1,0:T(8,128)(2,1)}, bf16[128,2048]{1,0:T(8,128)(2,1)S(1)}, u32[]{:S(2)}, u32[]{:S(2)}) collective-permute-start(bf16[128,2048]{1,0:T(8,128)(2,1)} %bitcast.21), channel_id=1, source_target_pairs={{0,64},{64,0},{128,192},{192,128},{256,320},{320,256},{384,448},{4... | collective-permute-start | bytes 1572872 | tf_op jit(solution)/shard_map/ppermute | solution.py:323
  18.4 30.4 %all-to-all-start = ((bf16[2,64,256]{2,0,1:T(2,128)(2,1)}), bf16[2,64,256]{2,0,1:T(2,128)(2,1)S(1)}, u32[]{:S(2)}, u32[]{:S(2)}) async-start(bf16[2,64,256]{2,0,1:T(2,128)(2,1)} %copy.15), calls=%async_computation | async-start | bytes 131072 | tf_op jit(solution)/shard_map/all_to_all | solution.py:319
  27.7 0.8 copy-start.6
  31.5 30.2 %collective-permute-start.1 = (bf16[2,4,128,128]{3,2,1,0:T(8,128)(2,1)}, bf16[2,4,128,128]{3,2,1,0:T(8,128)(2,1)S(1)}, u32[]{:S(2)}, u32[]{:S(2)}) collective-permute-start(bf16[2,4,128,128]{3,2,1,0:T(8,128)(2,1)} %get-tuple-element.50), channel_id=1, source_target_pairs={{0,128},{64,960},{128,256},{192,64},{256,384},{320,192},{384,512},... | collective-permute-start | bytes 786440 | tf_op jit(solution)/shard_map/ppermute | solution.py:333
  36.6 25.1 %collective-permute-start.2 = (bf16[2,4,128,128]{3,2,1,0:T(8,128)(2,1)}, bf16[2,4,128,128]{3,2,1,0:T(8,128)(2,1)S(1)}, u32[]{:S(2)}, u32[]{:S(2)}) collective-permute-start(bf16[2,4,128,128]{3,2,1,0:T(8,128)(2,1)} %get-tuple-element.51), channel_id=1, source_target_pairs={{0,256},{64,832},{128,384},{192,960},{256,512},{320,64},{384,640},... | collective-permute-start | bytes 786440 | tf_op jit(solution)/shard_map/ppermute | solution.py:333
  40.4 21.4 %collective-permute-start.3 = (bf16[2,4,128,128]{3,2,1,0:T(8,128)(2,1)}, bf16[2,4,128,128]{3,2,1,0:T(8,128)(2,1)S(1)}, u32[]{:S(2)}, u32[]{:S(2)}) collective-permute-start(bf16[2,4,128,128]{3,2,1,0:T(8,128)(2,1)} %get-tuple-element.52), channel_id=1, source_target_pairs={{0,384},{64,704},{128,512},{192,832},{256,640},{320,960},{384,768}... | collective-permute-start | bytes 786440 | tf_op jit(solution)/shard_map/ppermute | solution.py:333
  43.1 18.6 %collective-permute-start.4 = (bf16[4,128,128]{2,1,0:T(8,128)(2,1)}, bf16[4,128,128]{2,1,0:T(8,128)(2,1)S(1)}, u32[]{:S(2)}, u32[]{:S(2)}) collective-permute-start(bf16[4,128,128]{2,1,0:T(8,128)(2,1)} %get-tuple-element.53), channel_id=1, source_target_pairs={{0,512},{64,576},{128,640},{192,704},{256,768},{320,832},{384,896}... | collective-permute-start | bytes 393224 | tf_op jit(solution)/shard_map/ppermute | solution.py:333
  48.9 1.0 %copy-start.2 = (bf16[1,128,2048]{2,1,0:T(8,128)(2,1)S(1)}, bf16[1,128,2048]{2,1,0:T(8,128)(2,1)}, u32[]{:S(2)}) copy-start(bf16[1,128,2048]{2,1,0:T(8,128)(2,1)} %param.10) | copy-start | bytes 1572868
  51.9 33.3 %all-to-all-start.1 = ((bf16[8,128,512]{2,1,0:T(8,128)(2,1)}), bf16[8,128,512]{2,1,0:T(8,128)(2,1)S(1)}, u32[]{:S(2)}, u32[]{:S(2)}) async-start(bf16[8,128,512]{2,1,0:T(8,128)(2,1)} %rank_grad_rows.1), calls=%async_computation.1 | async-start | bytes 2097152 | tf_op jit(solution)/shard_map/all_to_all | solution.py:346
  61.7 0.7 copy-start.10
  61.7 0.7 copy-start.7
  61.7 0.8 copy-start.8
  61.8 0.9 copy-start.9
  64.8 7.8 %collective-permute-start.5 = (bf16[8,3,128,128]{3,2,1,0:T(8,128)(2,1)}, bf16[8,3,128,128]{3,2,1,0:T(8,128)(2,1)S(1)}, u32[]{:S(2)}, u32[]{:S(2)}) collective-permute-start(bf16[8,3,128,128]{3,2,1,0:T(8,128)(2,1)} %merge_rows.1), channel_id=1, source_target_pairs={{0,64},{64,0},{128,192},{192,128},{256,320},{320,256},{384,448},{4... | collective-permute-start | bytes 2359304 | tf_op jit(solution)/shard_map/ppermute | solution.py:357
  72.6 0.9 copy-start.5
  85.2 2.7 %copy-start.3 = (bf16[8,128,512]{2,1,0:T(8,128)(2,1)}, bf16[8,128,512]{2,1,0:T(8,128)(2,1)S(1)}, u32[]{:S(2)}) copy-start(bf16[8,128,512]{2,1,0:T(8,128)(2,1)S(1)} %all-to-all-done.1) | copy-start | bytes 3145732
  85.2 6.8 %collective-permute-start.6 = (bf16[1024,512]{1,0:T(8,128)(2,1)S(1)}, bf16[1024,512]{1,0:T(8,128)(2,1)S(1)}, u32[]{:S(2)}, u32[]{:S(2)}) collective-permute-start(bf16[1024,512]{1,0:T(8,128)(2,1)S(1)} %bitcast.26), channel_id=1, source_target_pairs={{0,64},{64,0},{128,192},{192,128},{256,320},{320,256},{384,448},{4... | collective-permute-start | bytes 3145736 | tf_op jit(solution)/shard_map/ppermute | solution.py:374
  92.0 1.0 %copy-start.4 = (bf16[1024,512]{1,0:T(8,128)(2,1)}, bf16[1024,512]{1,0:T(8,128)(2,1)S(1)}, u32[]{:S(2)}) copy-start(bf16[1024,512]{1,0:T(8,128)(2,1)S(1)} %collective-permute-done.6.refs_0_) | copy-start | bytes 3145732

commit v7 on v6

--- a/solution.py
+++ b/solution.py
@@ -21,7 +21,7 @@
 PACK_FLOPS = 270_000_000
 RANK_FLOPS = 270_000_000
 MERGE_FLOPS = 16_000_000_000
-COUNTS_FLOPS = 500_000_000
+COUNTS_FLOPS = 2_000_000_000
 
 NEAR = CHIPS // 2 - 1
 SAME_CORE = [[chip * CORES + core for chip in range(CHIPS)] for core in range(CORES)]

time: 98.1 us -> 113 us (1.15)
  waiting for transfers between devices: 9.26 us -> 24.5 us
    ppermute x4, waiting for transfers between devices: 0.01 us -> 22.4 us  [on_device(): lax.ppermute(block, 'tower', both_ways(step))]
    all_to_all x1, waiting for transfers between devices: 7.15 us -> 0.01 us  [on_device(): lax.all_to_all(rows_out, 'tower', split_axis=0, concat_axis=0, tiled=True...]
    ppermute x1, starting transfers between devices: 5.7 us -> 2.43 us  [on_device(): taken = lax.ppermute(give, 'tower', SWAP)]
    ppermute x4, starting transfers between devices: 17.3 us -> 18.9 us  [on_device(): lax.ppermute(block, 'tower', both_ways(step))]
    all_to_all x1, starting transfers between devices: 3.56 us -> 5.03 us  [on_device(): lax.all_to_all(rows_out, 'tower', split_axis=0, concat_axis=0, tiled=True...]
    unnamed x23 -> x25, local copies, waits for them, and re-layouts: 6.12 us -> 6.15 us
  transfers between devices with their start and end apart: 9 -> 9, of which waited for: 2 -> 2; matrix products, arithmetic and copies ran while one was open for 2% -> 1% of each run, Pallas kernels for 23% -> 20%
where the time goes in v7:
time: 113 us; the launch traced here: 112 us
  starting transfers between devices  54.1 us (48%)
  Pallas kernels  26.6 us (24%)
  waiting for transfers between devices  24.5 us (22%)
  local copies, waits for them, and re-layouts  6.18 us (5%)
    ppermute x4, waiting for transfers between devices, on_device(): lax.ppermute(block, 'tower', both_ways(step))  22.4 us
    ppermute x4, starting transfers between devices, on_device(): lax.ppermute(block, 'tower', both_ways(step))  18.9 us
    ppermute x1, starting transfers between devices, on_device(): partner = lax.ppermute(inputs, 'tower', SWAP)  16.2 us
    pallas_call x4, Pallas kernels, call(): pl.pallas_call(kernel, grid=(1,), in_specs=[SCALARS] * len(scalars) + [fe...  16 us
    all_to_all x1, starting transfers between devices, on_device(): lax.all_to_all(top_grad, 'hst', split_axis=1, concat_axis=0, tiled=True)  9.3 us
    pallas_call x2, Pallas kernels, half(): pl.pallas_call(half_kernel, grid=(STEPS,), in_specs=in_specs, out_specs=[...  8.62 us
    unnamed x25, local copies, waits for them, and re-layouts  6.15 us
    all_to_all x1, starting transfers between devices, on_device(): lax.all_to_all(rows_out, 'tower', split_axis=0, concat_axis=0, tiled=True...  5.03 us
  transfers between devices with their start and end apart: 9, of which 2 were waited for; matrix products, arithmetic and copies ran while one was open for 1% of the time, Pallas kernels for 20%

profile of v7, /device:TPU:1, one launch (start us, length us, event | category | flops | bytes accessed | tf_op | source)
XLA Modules:
  0.0 112.2 jit_solution(11404647759344336514)
XLA Ops:
  0.6 0.0 copy-start
  0.6 0.0 copy-start.1
  0.7 16.2 %collective-permute-start = (bf16[128,2048]{1,0:T(8,128)(2,1)}, bf16[128,2048]{1,0:T(8,128)(2,1)S(1)}, u32[]{:S(2)}, u32[]{:S(2)}) collective-permute-start(bf16[128,2048]{1,0:T(8,128)(2,1)} %bitcast.21), channel_id=1, source_target_pairs={{0,64},{64,0},{128,192},{192,128},{256,320},{320,256},{384,448},{4... | collective-permute-start | bytes 1572872 | tf_op jit(solution)/shard_map/ppermute | solution.py:323
  16.9 1.5 %copy.15 = bf16[2,64,256]{2,0,1:T(2,128)(2,1)} copy(bf16[2,64,256]{2,1,0:T(8,128)(2,1)} %param.9) | data formatting | bytes 131072 | tf_op args[0]
  18.4 9.3 %all-to-all-start = ((bf16[2,64,256]{2,0,1:T(2,128)(2,1)}), bf16[2,64,256]{2,0,1:T(2,128)(2,1)S(1)}, u32[]{:S(2)}, u32[]{:S(2)}) async-start(bf16[2,64,256]{2,0,1:T(2,128)(2,1)} %copy.15), calls=%async_computation | async-start | bytes 131072 | tf_op jit(solution)/shard_map/all_to_all | solution.py:319
  27.7 0.0 collective-permute-done.partner_ref
  27.7 0.0 copy-start.6
  27.7 0.8 copy-done.6
  28.5 3.0 %low_rank_and_columns.1 = (bf16[4,128,128]{2,1,0:T(8,128)(2,1)}, bf16[2,4,128,128]{3,2,1,0:T(8,128)(2,1)}, bf16[2,4,128,128]{3,2,1,0:T(8,128)(2,1)}, bf16[2,4,12...) custom-call(bf16[128,2048]{1,0:T(8,128)(2,1)} %bitcast.22, bf16[128,2048]{1,0:T(8,128)(2,1)} %copy-done.6, bf16[2048,256]{1,0:T(8,128)(2,1)} %bitcast.24), custom_call_target="tpu_custom_call" | custom-call | flops 270000000 | bytes 3000000 | tf_op jit(solution)/shard_map/low_rank_and_columns/pallas_call | solution.py:165
  31.5 5.1 %collective-permute-start.1 = (bf16[2,4,128,128]{3,2,1,0:T(8,128)(2,1)}, bf16[2,4,128,128]{3,2,1,0:T(8,128)(2,1)S(1)}, u32[]{:S(2)}, u32[]{:S(2)}) collective-permute-start(bf16[2,4,128,128]{3,2,1,0:T(8,128)(2,1)} %get-tuple-element.50), channel_id=1, source_target_pairs={{0,128},{64,960},{128,256},{192,64},{256,384},{320,192},{384,512},... | collective-permute-start | bytes 786440 | tf_op jit(solution)/shard_map/ppermute | solution.py:333
  36.6 3.8 %collective-permute-start.2 = (bf16[2,4,128,128]{3,2,1,0:T(8,128)(2,1)}, bf16[2,4,128,128]{3,2,1,0:T(8,128)(2,1)S(1)}, u32[]{:S(2)}, u32[]{:S(2)}) collective-permute-start(bf16[2,4,128,128]{3,2,1,0:T(8,128)(2,1)} %get-tuple-element.51), channel_id=1, source_target_pairs={{0,256},{64,832},{128,384},{192,960},{256,512},{320,64},{384,640},... | collective-permute-start | bytes 786440 | tf_op jit(solution)/shard_map/ppermute | solution.py:333
  40.4 2.7 %collective-permute-start.3 = (bf16[2,4,128,128]{3,2,1,0:T(8,128)(2,1)}, bf16[2,4,128,128]{3,2,1,0:T(8,128)(2,1)S(1)}, u32[]{:S(2)}, u32[]{:S(2)}) collective-permute-start(bf16[2,4,128,128]{3,2,1,0:T(8,128)(2,1)} %get-tuple-element.52), channel_id=1, source_target_pairs={{0,384},{64,704},{128,512},{192,832},{256,640},{320,960},{384,768}... | collective-permute-start | bytes 786440 | tf_op jit(solution)/shard_map/ppermute | solution.py:333
  43.1 0.0 all-to-all-done
  43.2 0.0 copy-done
  43.2 0.0 copy-done.1
  43.2 0.0 copy-start.2
  43.2 1.0 copy-done.2
  44.2 0.0 copy-start.11
  44.2 2.0 %rank_grad_rows.1 = bf16[8,128,512]{2,1,0:T(8,128)(2,1)} custom-call(bf16[128,256]{1,0:T(8,128)(2,1)S(1)} %reshape.17.grad_ref, bf16[128,2048]{1,0:T(8,128)(2,1)S(1)} %bitcast.23, bf16[2048,256]{1,0:T(8,128)(2,1)S(1)} %bitcast.18, bf16[256,2048]{1,0:T(8,128)(2,1)S(1)} %bitcast.20), custom_call_target="tpu_custom_call" | custom-call | flops 270000000 | bytes 3600000 | tf_op jit(solution)/shard_map/rank_grad_rows/pallas_call | solution.py:303
  46.2 5.0 %all-to-all-start.1 = ((bf16[8,128,512]{2,1,0:T(8,128)(2,1)}), bf16[8,128,512]{2,1,0:T(8,128)(2,1)S(1)}, u32[]{:S(2)}, u32[]{:S(2)}) async-start(bf16[8,128,512]{2,1,0:T(8,128)(2,1)} %rank_grad_rows.1), calls=%async_computation.1 | async-start | bytes 2097152 | tf_op jit(solution)/shard_map/all_to_all | solution.py:346
  51.2 0.0 copy-done.11
  51.3 7.3 %collective-permute-start.4 = (bf16[4,128,128]{2,1,0:T(8,128)(2,1)S(1)}, bf16[4,128,128]{2,1,0:T(8,128)(2,1)S(1)}, u32[]{:S(2)}, u32[]{:S(2)}) collective-permute-start(bf16[4,128,128]{2,1,0:T(8,128)(2,1)S(1)} %copy-done.11), channel_id=1, source_target_pairs={{0,512},{64,576},{128,640},{192,704},{256,768},{320,832},{384,896}... | collective-permute-start | bytes 393224 | tf_op jit(solution)/shard_map/ppermute | solution.py:333
  58.5 6.3 %bag_counts.1 = (bf16[2,512,1024]{2,1,0:T(8,128)(2,1)}, f32[2,1024,128]{2,1,0:T(8,128)}) custom-call(s32[8,2048]{1,0:T(8,128)} %bitcast.33, s32[1,2048]{1,0:T(1,128)} %bitcast.34), custom_call_target="tpu_custom_call" | custom-call | flops 2000000000 | bytes 1000 | tf_op jit(solution)/shard_map/bag_counts/pallas_call | solution.py:165
  64.8 22.4 %collective-permute-done.4.refs_4_.far_ref = bf16[4,128,128]{2,1,0:T(8,128)(2,1)S(1)} collective-permute-done((bf16[4,128,128]{2,1,0:T(8,128)(2,1)S(1)}, bf16[4,128,128]{2,1,0:T(8,128)(2,1)S(1)}, u32[]{:S(2)}, u32[]{:S(2)}) %collective-permute-start.4) | collective-permute-done | bytes 131104 | tf_op jit(solution)/shard_map/ppermute | solution.py:333
  87.2 0.0 copy-start.10
  87.2 0.0 collective-permute-done.1.refs_1_.first_ref
  87.2 0.0 copy-start.7
  87.2 0.0 collective-permute-done.2.refs_2_.second_ref
  87.2 0.0 copy-start.8
  87.2 0.0 collective-permute-done.3.refs_3_.third_ref
  87.3 0.0 copy-start.9
  87.3 0.6 copy-done.10
  87.9 0.1 copy-done.7
  88.0 0.1 copy-done.8
  88.1 0.1 copy-done.9
  88.2 2.1 %merge_rows.1 = bf16[8,3,128,128]{3,2,1,0:T(8,128)(2,1)} custom-call(bf16[4,128,128]{2,1,0:T(8,128)(2,1)} %get-tuple-element.46.refs_0_.self_ref, bf16[2,4,128,128]{3,2,1,0:T(8,128)(2,1)} %copy-done.7, bf16[2,4,128,128]{3,2,1,0:T(8,128)(2,1)} %copy-done.8, bf16[2,4,128,128]{3,2,1,0:T(8,128)(2,1)} %copy-done.9, bf16[4,128,128]{2,1,0:T(8,128)(2,1)} %copy-done.10), custom_call_target="tpu_custom_call" | custom-call | flops 16000000000 | bytes 1000 | tf_op jit(solution)/shard_map/merge_rows/pallas_call | solution.py:165
  90.3 2.4 %collective-permute-start.5 = (bf16[8,3,128,128]{3,2,1,0:T(8,128)(2,1)}, bf16[8,3,128,128]{3,2,1,0:T(8,128)(2,1)S(1)}, u32[]{:S(2)}, u32[]{:S(2)}) collective-permute-start(bf16[8,3,128,128]{3,2,1,0:T(8,128)(2,1)} %merge_rows.1), channel_id=1, source_target_pairs={{0,64},{64,0},{128,192},{192,128},{256,320},{320,256},{384,448},{4... | collective-permute-start | bytes 2359304 | tf_op jit(solution)/shard_map/ppermute | solution.py:357
  92.7 2.1 %collective-permute-done.5.taken_ref = bf16[8,3,128,128]{3,2,1,0:T(8,128)(2,1)S(1)} collective-permute-done((bf16[8,3,128,128]{3,2,1,0:T(8,128)(2,1)}, bf16[8,3,128,128]{3,2,1,0:T(8,128)(2,1)S(1)}, u32[]{:S(2)}, u32[]{:S(2)}) %collective-permute-start.5) | collective-permute-done | bytes 786464 | tf_op jit(solution)/shard_map/ppermute | solution.py:357
  94.8 0.0 copy-start.5
  94.8 0.9 copy-done.5
  95.7 4.6 %saved_rows.1 = (bf16[2,1024,256]{2,1,0:T(8,128)(2,1)}, bf16[2,1024,128]{2,1,0:T(8,128)(2,1)}, bf16[2,1024,128]{2,1,0:T(8,128)(2,1)}, f32[2,1024,128]{2,1,0:T(8,...) custom-call(s32[1,16]{1,0:T(1,128)} %slots_ref.1, bf16[4,128,128]{2,1,0:T(8,128)(2,1)} %get-tuple-element.46.refs_0_.self_ref, ...), custom_call_target="tpu_custom_call" | custom-call | flops 1000 | bytes 1000 | tf_op jit(solution)/shard_map/saved_rows/pallas_call | solution.py:165
  100.3 0.0 all-to-all-done.1
  100.3 0.0 copy-start.3
  100.3 2.3 %collective-permute-start.6 = (bf16[1024,512]{1,0:T(8,128)(2,1)S(1)}, bf16[1024,512]{1,0:T(8,128)(2,1)S(1)}, u32[]{:S(2)}, u32[]{:S(2)}) collective-permute-start(bf16[1024,512]{1,0:T(8,128)(2,1)S(1)} %bitcast.26), channel_id=1, source_target_pairs={{0,64},{64,0},{128,192},{192,128},{256,320},{320,256},{384,448},{4... | collective-permute-start | bytes 3145736 | tf_op jit(solution)/shard_map/ppermute | solution.py:374
  102.6 0.0 copy-done.3
  102.6 4.2 %column_half_first.1 = (f32[128,256]{1,0:T(8,128)}, f32[128,256]{1,0:T(8,128)}, f32[1,128]{1,0:T(1,128)}, f32[128,256]{1,0:T(8,128)}, f32[512,128]{1,0:T(8,128)}) custom-call(bf16[1024,512]{1,0:T(8,128)(2,1)} %bitcast.27, bf16[2,1024,256]{2,1,0:T(8,128)(2,1)} %get-tuple-element.67.refs_1_, bf16[2,1024,128]{2,1,0:T(8,128)(2,1)} %get-tuple-element.68.refs_2_, ...), custom_call_target="tpu_custom_call" | custom-call | flops 1500000000 | bytes 6000000 | tf_op jit(solution)/shard_map/column_half_first/pallas_call | solution.py:111
  106.8 0.0 collective-permute-done.6.refs_0_
  106.8 0.0 copy-start.4
  106.8 1.0 copy-done.4
  107.7 4.5 %column_half_second.1 = (f32[128,256]{1,0:T(8,128)}, f32[256,128]{1,0:T(8,128)}, f32[1,128]{1,0:T(1,128)}, f32[128,256]{1,0:T(8,128)}, f32[512,128]{1,0:T(8,128)}) custom-call(bf16[1024,512]{1,0:T(8,128)(2,1)} %copy-done.4, bf16[2,1024,256]{2,1,0:T(8,128)(2,1)} %get-tuple-element.67.refs_1_, bf16[2,1024,128]{2,1,0:T(8,128)(2,1)} %get-tuple-element.68.refs_2_, ...), custom_call_target="tpu_custom_call" | custom-call | flops 1500000000 | bytes 6000000 | tf_op jit(solution)/shard_map/column_half_second/pallas_call | solution.py:111
  (1 shorter events, 0.0 us)
Async XLA Ops:
  0.6 42.6 %copy-start = (bf16[1,2048,256]{2,1,0:T(8,128)(2,1)S(1)}, bf16[1,2048,256]{2,1,0:T(8,128)(2,1)}, u32[]{:S(2)}) copy-start(bf16[1,2048,256]{2,1,0:T(8,128)(2,1)} %param.14) | copy-start | bytes 3145732
  0.6 42.6 %copy-start.1 = (bf16[1,256,2048]{2,1,0:T(8,128)(2,1)S(1)}, bf16[1,256,2048]{2,1,0:T(8,128)(2,1)}, u32[]{:S(2)}) copy-start(bf16[1,256,2048]{2,1,0:T(8,128)(2,1)} %param.12) | copy-start | bytes 3145732
  0.7 27.1 %collective-permute-start = (bf16[128,2048]{1,0:T(8,128)(2,1)}, bf16[128,2048]{1,0:T(8,128)(2,1)S(1)}, u32[]{:S(2)}, u32[]{:S(2)}) collective-permute-start(bf16[128,2048]{1,0:T(8,128)(2,1)} %bitcast.21), channel_id=1, source_target_pairs={{0,64},{64,0},{128,192},{192,128},{256,320},{320,256},{384,448},{4... | collective-permute-start | bytes 1572872 | tf_op jit(solution)/shard_map/ppermute | solution.py:323
  18.4 24.7 %all-to-all-start = ((bf16[2,64,256]{2,0,1:T(2,128)(2,1)}), bf16[2,64,256]{2,0,1:T(2,128)(2,1)S(1)}, u32[]{:S(2)}, u32[]{:S(2)}) async-start(bf16[2,64,256]{2,0,1:T(2,128)(2,1)} %copy.15), calls=%async_computation | async-start | bytes 131072 | tf_op jit(solution)/shard_map/all_to_all | solution.py:319
  27.7 0.8 copy-start.6
  31.5 55.7 %collective-permute-start.1 = (bf16[2,4,128,128]{3,2,1,0:T(8,128)(2,1)}, bf16[2,4,128,128]{3,2,1,0:T(8,128)(2,1)S(1)}, u32[]{:S(2)}, u32[]{:S(2)}) collective-permute-start(bf16[2,4,128,128]{3,2,1,0:T(8,128)(2,1)} %get-tuple-element.50), channel_id=1, source_target_pairs={{0,128},{64,960},{128,256},{192,64},{256,384},{320,192},{384,512},... | collective-permute-start | bytes 786440 | tf_op jit(solution)/shard_map/ppermute | solution.py:333
  36.6 50.6 %collective-permute-start.2 = (bf16[2,4,128,128]{3,2,1,0:T(8,128)(2,1)}, bf16[2,4,128,128]{3,2,1,0:T(8,128)(2,1)S(1)}, u32[]{:S(2)}, u32[]{:S(2)}) collective-permute-start(bf16[2,4,128,128]{3,2,1,0:T(8,128)(2,1)} %get-tuple-element.51), channel_id=1, source_target_pairs={{0,256},{64,832},{128,384},{192,960},{256,512},{320,64},{384,640},... | collective-permute-start | bytes 786440 | tf_op jit(solution)/shard_map/ppermute | solution.py:333
  40.4 46.9 %collective-permute-start.3 = (bf16[2,4,128,128]{3,2,1,0:T(8,128)(2,1)}, bf16[2,4,128,128]{3,2,1,0:T(8,128)(2,1)S(1)}, u32[]{:S(2)}, u32[]{:S(2)}) collective-permute-start(bf16[2,4,128,128]{3,2,1,0:T(8,128)(2,1)} %get-tuple-element.52), channel_id=1, source_target_pairs={{0,384},{64,704},{128,512},{192,832},{256,640},{320,960},{384,768}... | collective-permute-start | bytes 786440 | tf_op jit(solution)/shard_map/ppermute | solution.py:333
  43.2 1.0 copy-start.2
  44.2 7.0 %copy-start.11 = (bf16[4,128,128]{2,1,0:T(8,128)(2,1)S(1)}, bf16[4,128,128]{2,1,0:T(8,128)(2,1)}, u32[]{:S(2)}) copy-start(bf16[4,128,128]{2,1,0:T(8,128)(2,1)} %get-tuple-element.53) | copy-start | bytes 393220
  46.2 54.1 %all-to-all-start.1 = ((bf16[8,128,512]{2,1,0:T(8,128)(2,1)}), bf16[8,128,512]{2,1,0:T(8,128)(2,1)S(1)}, u32[]{:S(2)}, u32[]{:S(2)}) async-start(bf16[8,128,512]{2,1,0:T(8,128)(2,1)} %rank_grad_rows.1), calls=%async_computation.1 | async-start | bytes 2097152 | tf_op jit(solution)/shard_map/all_to_all | solution.py:346
  51.3 36.0 %collective-permute-start.4 = (bf16[4,128,128]{2,1,0:T(8,128)(2,1)S(1)}, bf16[4,128,128]{2,1,0:T(8,128)(2,1)S(1)}, u32[]{:S(2)}, u32[]{:S(2)}) collective-permute-start(bf16[4,128,128]{2,1,0:T(8,128)(2,1)S(1)} %copy-done.11), channel_id=1, source_target_pairs={{0,512},{64,576},{128,640},{192,704},{256,768},{320,832},{384,896}... | collective-permute-start | bytes 393224 | tf_op jit(solution)/shard_map/ppermute | solution.py:333
  87.2 0.7 copy-start.10
  87.2 0.7 copy-start.7
  87.2 0.8 copy-start.8
  87.3 0.9 copy-start.9
  90.3 4.5 %collective-permute-start.5 = (bf16[8,3,128,128]{3,2,1,0:T(8,128)(2,1)}, bf16[8,3,128,128]{3,2,1,0:T(8,128)(2,1)S(1)}, u32[]{:S(2)}, u32[]{:S(2)}) collective-permute-start(bf16[8,3,128,128]{3,2,1,0:T(8,128)(2,1)} %merge_rows.1), channel_id=1, source_target_pairs={{0,64},{64,0},{128,192},{192,128},{256,320},{320,256},{384,448},{4... | collective-permute-start | bytes 2359304 | tf_op jit(solution)/shard_map/ppermute | solution.py:357
  94.8 0.9 copy-start.5
  100.3 2.3 %copy-start.3 = (bf16[8,128,512]{2,1,0:T(8,128)(2,1)}, bf16[8,128,512]{2,1,0:T(8,128)(2,1)S(1)}, u32[]{:S(2)}) copy-start(bf16[8,128,512]{2,1,0:T(8,128)(2,1)S(1)} %all-to-all-done.1) | copy-start | bytes 3145732
  100.3 6.5 %collective-permute-start.6 = (bf16[1024,512]{1,0:T(8,128)(2,1)S(1)}, bf16[1024,512]{1,0:T(8,128)(2,1)S(1)}, u32[]{:S(2)}, u32[]{:S(2)}) collective-permute-start(bf16[1024,512]{1,0:T(8,128)(2,1)S(1)} %bitcast.26), channel_id=1, source_target_pairs={{0,64},{64,0},{128,192},{192,128},{256,320},{320,256},{384,448},{4... | collective-permute-start | bytes 3145736 | tf_op jit(solution)/shard_map/ppermute | solution.py:374
  106.8 1.0 copy-start.4

commit v8 on v6

--- a/solution.py
+++ b/solution.py
@@ -15,9 +15,8 @@
 BLOCK = 128
 HALF = CHIPS * BLOCK
 
-STEPS = 2
+STEPS = 1
 ROOM = 60 * 1024 * 1024
-HALF_ROOM = 60 * 1024 * 1024
 PACK_FLOPS = 270_000_000
 RANK_FLOPS = 270_000_000
 MERGE_FLOPS = 16_000_000_000
@@ -52,75 +51,93 @@
     return jnp.dot(left, right, preferred_element_type=jnp.float32)
 
 
-def half_kernel(*refs):
-    grads_ref, low_ref, x_ref, crossed_ref, scale_ref, counts_ref, spread_ref, comp_ref, down_ref = (
-        refs[:9]
-    )
-    before, out_refs, up_sum = refs[9:-6], refs[-6:-1], refs[-1]
-    sums = list(out_refs)
-    sums[1] = up_sum
-
-    @pl.when(pl.program_id(0) == 0)
+def columns_kernel(
+    own_ref,
+    other_ref,
+    low_ref,
+    x_ref,
+    crossed_ref,
+    scale_ref,
+    counts_ref,
+    spread_ref,
+    comp_ref,
+    down_ref,
+    down_out,
+    up_out,
+    bias_out,
+    comp_out,
+    table_out,
+    up_sum,
+):
+    step = pl.program_id(0)
+
+    @pl.when(step == 0)
     def _():
-        for index, ref in enumerate(sums):
-            ref[...] = before[index][...] if before else jnp.zeros(ref.shape, ref.dtype)
-
-    out_grad = grads_ref[:, :COMP]
-    rank_grad = grads_ref[:, COMP:]
-    x = x_ref[0]
-    cross = contract_cols(out_grad, comp_ref[...])
-    back = contract_cols(rank_grad, down_ref[...])
-    input_grad = (cross[:, EMBED:] * scale_ref[0] + back).astype(jnp.bfloat16)
-    scaled = input_grad.astype(jnp.float32) * spread_ref[0]
-    high = scaled.astype(jnp.bfloat16)
-    rest = (scaled - high.astype(jnp.float32)).astype(jnp.bfloat16)
-    table = product(counts_ref[0], jnp.concatenate([high, rest], axis=1))
-    scale_grad = (cross[:, :EMBED] * x.astype(jnp.float32)).astype(jnp.bfloat16)
-    down_out, up_out, bias_out, comp_out, table_out = out_refs
-    up_sum[...] += contract_rows(scale_grad, low_ref[0])
-    down_out[...] += contract_rows(x, rank_grad)
-    bias_out[...] += jnp.sum(scale_grad.astype(jnp.float32), axis=0, keepdims=True)
-    comp_out[...] += contract_rows(crossed_ref[0], out_grad)
-    table_out[...] += table[:, :EMBED] + table[:, EMBED:]
-
-    @pl.when(pl.program_id(0) == pl.num_programs(0) - 1)
+        for ref in (down_out, up_sum, bias_out, comp_out, table_out):
+            ref[...] = jnp.zeros(ref.shape, ref.dtype)
+
+    def add(grads_ref):
+        out_grad = grads_ref[:, :COMP]
+        rank_grad = grads_ref[:, COMP:]
+        x = x_ref[0]
+        cross = contract_cols(out_grad, comp_ref[...])
+        back = contract_cols(rank_grad, down_ref[...])
+        input_grad = (cross[:, EMBED:] * scale_ref[0] + back).astype(jnp.bfloat16)
+        scaled = input_grad.astype(jnp.float32) * spread_ref[0]
+        high = scaled.astype(jnp.bfloat16)
+        rest = (scaled - high.astype(jnp.float32)).astype(jnp.bfloat16)
+        table = product(counts_ref[0], jnp.concatenate([high, rest], axis=1))
+        scale_grad = (cross[:, :EMBED] * x.astype(jnp.float32)).astype(jnp.bfloat16)
+        down_out[...] += contract_rows(x, rank_grad)
+        up_sum[...] += contract_rows(scale_grad, low_ref[0])
+        bias_out[...] += jnp.sum(scale_grad.astype(jnp.float32), axis=0, keepdims=True)
+        comp_out[...] += contract_rows(crossed_ref[0], out_grad)
+        table_out[...] += table[:, :EMBED] + table[:, EMBED:]
+
+    @pl.when(step < STEPS)
     def _():
-        up_out[...] = up_sum[...].T if before else up_sum[...]
-
-
-def half(side, grads, saved, before=()):
+        add(own_ref)
+
+    @pl.when(step >= STEPS)
+    def _():
+        add(other_ref)
+
+    @pl.when(step == CORES * STEPS - 1)
+    def _():
+        up_out[...] = up_sum[...].T
+
+
+def columns(own, other, saved):
     step = HALF // STEPS
-    shapes = [(EMBED, RANK), (EMBED, RANK), (1, EMBED), (EMBED, COMP), (TABLE_ROWS, EMBED)]
-    if before:
-        shapes[1] = (RANK, EMBED)
+    shapes = [(EMBED, RANK), (RANK, EMBED), (1, EMBED), (EMBED, COMP), (TABLE_ROWS, EMBED)]
 
     def rows(width):
-        return pl.BlockSpec((1, step, width), lambda i: (side, i, 0))
-
-    in_specs = [
-        pl.BlockSpec((step, COMP + RANK), lambda i: (i, 0)),
-        rows(RANK),
-        rows(EMBED),
-        rows(EMBED),
-        rows(EMBED),
-        pl.BlockSpec((1, TABLE_ROWS, step), lambda i: (side, 0, i)),
-        rows(EMBED),
-        fetched((2 * EMBED, COMP)),
-        fetched((EMBED, RANK)),
-    ] + [fetched(array.shape) for array in before]
+        return pl.BlockSpec((1, step, width), lambda i: (i // STEPS, i % STEPS, 0))
+
     return pl.pallas_call(
-        half_kernel,
-        grid=(STEPS,),
-        in_specs=in_specs,
+        columns_kernel,
+        grid=(CORES * STEPS,),
+        in_specs=[
+            pl.BlockSpec((step, COMP + RANK), lambda i: (jnp.minimum(i, STEPS - 1), 0)),
+            pl.BlockSpec((step, COMP + RANK), lambda i: (jnp.maximum(i - STEPS, 0), 0)),
+            rows(RANK),
+            rows(EMBED),
+            rows(EMBED),
+            rows(EMBED),
+            pl.BlockSpec((1, TABLE_ROWS, step), lambda i: (i // STEPS, 0, i % STEPS)),
+            rows(EMBED),
+            fetched((2 * EMBED, COMP)),
+            fetched((EMBED, RANK)),
+        ],
         out_specs=[fetched(shape) for shape in shapes],
         out_shape=[full_type(*shape) for shape in shapes],
         scratch_shapes=[pltpu.VMEM((EMBED, RANK), jnp.float32)],
-        compiler_params=pltpu.CompilerParams(vmem_limit_bytes=HALF_ROOM),
+        compiler_params=pltpu.CompilerParams(vmem_limit_bytes=ROOM),
         cost_estimate=pl.CostEstimate(
-            flops=1_500_000_000, bytes_accessed=6_000_000, transcendentals=0
+            flops=3_000_000_000, bytes_accessed=12_000_000, transcendentals=0
         ),
-        name="column_half_second" if before else "column_half_first",
-    )(grads, *saved, *before)
+        name="column_sums",
+    )(own, other, *saved)
 
 
 def pack_kernel(
@@ -372,8 +389,7 @@
     saved = (low, x, crossed, scale, counts, spread, comp_two, down_one)
     grads_own, *saved = lax.optimization_barrier((grads_own, *saved))
     grads_other = lax.ppermute(grads_own, "tower", SWAP)
-    first = half(0, grads_own, saved)
-    grad_down, grad_up, grad_bias, grad_comp, tables = half(1, grads_other, saved, first)
+    grad_down, grad_up, grad_bias, grad_comp, tables = columns(grads_own, grads_other, saved)
     return grad_down[None], grad_up[None], grad_bias, grad_comp[None], tables[None, None]
 
 

time: 98.1 us -> 97.9 us (level)
  Pallas kernels: 26.6 us -> 24.1 us
  waiting for transfers between devices: 9.26 us -> 11.4 us
    pallas_call x2 -> x1, Pallas kernels: 8.62 us -> 6.24 us  [columns(): pl.pallas_call(columns_kernel, grid=(CORES * STEPS,), in_specs=[pl.BlockS...]
    ppermute x1, waiting for transfers between devices: 0.01 us -> 2.26 us  [on_device(): grads_other = lax.ppermute(grads_own, 'tower', SWAP)]
  transfers between devices with their start and end apart: 9 -> 9, of which waited for: 2 -> 3; matrix products, arithmetic and copies ran while one was open for 2% -> 2% of each run, Pallas kernels for 23% -> 18%
where the time goes in v8:
time: 97.9 us; the launch traced here: 97.3 us
  starting transfers between devices  54.8 us (56%)
  Pallas kernels  24.1 us (25%)
  waiting for transfers between devices  11.4 us (12%)
  local copies, waits for them, and re-layouts  6.17 us (6%)
    ppermute x4, starting transfers between devices, on_device(): lax.ppermute(block, 'tower', both_ways(step))  17.2 us
    ppermute x1, starting transfers between devices, on_device(): partner = lax.ppermute(inputs, 'tower', SWAP)  16.2 us
    pallas_call x4, Pallas kernels, call(): pl.pallas_call(kernel, grid=(1,), in_specs=[SCALARS] * len(scalars) + [fe...  15.9 us
    all_to_all x1, starting transfers between devices, on_device(): lax.all_to_all(top_grad, 'hst', split_axis=1, concat_axis=0, tiled=True)  9.3 us
    all_to_all x1, waiting for transfers between devices, on_device(): lax.all_to_all(rows_out, 'tower', split_axis=0, concat_axis=0, tiled=True...  7.04 us
    pallas_call x1, Pallas kernels, columns(): pl.pallas_call(columns_kernel, grid=(CORES * STEPS,), in_specs=[pl.BlockS...  6.24 us
    unnamed x23, local copies, waits for them, and re-layouts  6.13 us
    ppermute x1, starting transfers between devices, on_device(): taken = lax.ppermute(give, 'tower', SWAP)  5.8 us
  transfers between devices with their start and end apart: 9, of which 3 were waited for; matrix products, arithmetic and copies ran while one was open for 2% of the time, Pallas kernels for 18%

profile of v8, /device:TPU:1, one launch (start us, length us, event | category | flops | bytes accessed | tf_op | source)
XLA Modules:
  0.0 97.3 jit_solution(2314503299859733214)
XLA Ops:
  0.6 0.0 copy-start
  0.6 0.0 copy-start.1
  0.7 16.2 %collective-permute-start = (bf16[128,2048]{1,0:T(8,128)(2,1)}, bf16[128,2048]{1,0:T(8,128)(2,1)S(1)}, u32[]{:S(2)}, u32[]{:S(2)}) collective-permute-start(bf16[128,2048]{1,0:T(8,128)(2,1)} %bitcast.21), channel_id=1, source_target_pairs={{0,64},{64,0},{128,192},{192,128},{256,320},{320,256},{384,448},{4... | collective-permute-start | bytes 1572872 | tf_op jit(solution)/shard_map/ppermute | solution.py:340
  16.9 1.5 %copy.15 = bf16[2,64,256]{2,0,1:T(2,128)(2,1)} copy(bf16[2,64,256]{2,1,0:T(8,128)(2,1)} %param.9) | data formatting | bytes 131072 | tf_op args[0]
  18.4 9.3 %all-to-all-start = ((bf16[2,64,256]{2,0,1:T(2,128)(2,1)}), bf16[2,64,256]{2,0,1:T(2,128)(2,1)S(1)}, u32[]{:S(2)}, u32[]{:S(2)}) async-start(bf16[2,64,256]{2,0,1:T(2,128)(2,1)} %copy.15), calls=%async_computation | async-start | bytes 131072 | tf_op jit(solution)/shard_map/all_to_all | solution.py:336
  27.7 0.0 collective-permute-done.partner_ref
  27.7 0.0 copy-start.5
  27.7 0.8 copy-done.5
  28.5 3.0 %low_rank_and_columns.1 = (bf16[4,128,128]{2,1,0:T(8,128)(2,1)}, bf16[2,4,128,128]{3,2,1,0:T(8,128)(2,1)}, bf16[2,4,128,128]{3,2,1,0:T(8,128)(2,1)}, bf16[2,4,12...) custom-call(bf16[128,2048]{1,0:T(8,128)(2,1)} %bitcast.22, bf16[128,2048]{1,0:T(8,128)(2,1)} %copy-done.5, bf16[2048,256]{1,0:T(8,128)(2,1)} %bitcast.24), custom_call_target="tpu_custom_call" | custom-call | flops 270000000 | bytes 3000000 | tf_op jit(solution)/shard_map/low_rank_and_columns/pallas_call | solution.py:182
  31.5 5.1 %collective-permute-start.1 = (bf16[2,4,128,128]{3,2,1,0:T(8,128)(2,1)}, bf16[2,4,128,128]{3,2,1,0:T(8,128)(2,1)S(1)}, u32[]{:S(2)}, u32[]{:S(2)}) collective-permute-start(bf16[2,4,128,128]{3,2,1,0:T(8,128)(2,1)} %get-tuple-element.45), channel_id=1, source_target_pairs={{0,128},{64,960},{128,256},{192,64},{256,384},{320,192},{384,512},... | collective-permute-start | bytes 786440 | tf_op jit(solution)/shard_map/ppermute | solution.py:350
  36.6 3.8 %collective-permute-start.2 = (bf16[2,4,128,128]{3,2,1,0:T(8,128)(2,1)}, bf16[2,4,128,128]{3,2,1,0:T(8,128)(2,1)S(1)}, u32[]{:S(2)}, u32[]{:S(2)}) collective-permute-start(bf16[2,4,128,128]{3,2,1,0:T(8,128)(2,1)} %get-tuple-element.46), channel_id=1, source_target_pairs={{0,256},{64,832},{128,384},{192,960},{256,512},{320,64},{384,640},... | collective-permute-start | bytes 786440 | tf_op jit(solution)/shard_map/ppermute | solution.py:350
  40.4 2.7 %collective-permute-start.3 = (bf16[2,4,128,128]{3,2,1,0:T(8,128)(2,1)}, bf16[2,4,128,128]{3,2,1,0:T(8,128)(2,1)S(1)}, u32[]{:S(2)}, u32[]{:S(2)}) collective-permute-start(bf16[2,4,128,128]{3,2,1,0:T(8,128)(2,1)} %get-tuple-element.47), channel_id=1, source_target_pairs={{0,384},{64,704},{128,512},{192,832},{256,640},{320,960},{384,768}... | collective-permute-start | bytes 786440 | tf_op jit(solution)/shard_map/ppermute | solution.py:350
  43.1 5.7 %collective-permute-start.4 = (bf16[4,128,128]{2,1,0:T(8,128)(2,1)}, bf16[4,128,128]{2,1,0:T(8,128)(2,1)S(1)}, u32[]{:S(2)}, u32[]{:S(2)}) collective-permute-start(bf16[4,128,128]{2,1,0:T(8,128)(2,1)} %get-tuple-element.48), channel_id=1, source_target_pairs={{0,512},{64,576},{128,640},{192,704},{256,768},{320,832},{384,896}... | collective-permute-start | bytes 393224 | tf_op jit(solution)/shard_map/ppermute | solution.py:350
  48.8 0.0 all-to-all-done
  48.8 0.0 copy-done
  48.8 0.0 copy-done.1
  48.9 0.0 copy-start.2
  48.9 1.0 %copy-done.2 = bf16[1,128,2048]{2,1,0:T(8,128)(2,1)S(1)} copy-done((bf16[1,128,2048]{2,1,0:T(8,128)(2,1)S(1)}, bf16[1,128,2048]{2,1,0:T(8,128)(2,1)}, u32[]{:S(2)}) %copy-start.2) | copy-done | bytes 524312
  49.9 2.0 %rank_grad_rows.1 = bf16[8,128,512]{2,1,0:T(8,128)(2,1)} custom-call(bf16[128,256]{1,0:T(8,128)(2,1)S(1)} %reshape.17.grad_ref, bf16[128,2048]{1,0:T(8,128)(2,1)S(1)} %bitcast.23, bf16[2048,256]{1,0:T(8,128)(2,1)S(1)} %bitcast.18, bf16[256,2048]{1,0:T(8,128)(2,1)S(1)} %bitcast.20), custom_call_target="tpu_custom_call" | custom-call | flops 270000000 | bytes 3600000 | tf_op jit(solution)/shard_map/rank_grad_rows/pallas_call | solution.py:320
  51.9 3.6 %all-to-all-start.1 = ((bf16[8,128,512]{2,1,0:T(8,128)(2,1)}), bf16[8,128,512]{2,1,0:T(8,128)(2,1)S(1)}, u32[]{:S(2)}, u32[]{:S(2)}) async-start(bf16[8,128,512]{2,1,0:T(8,128)(2,1)} %rank_grad_rows.1), calls=%async_computation.1 | async-start | bytes 2097152 | tf_op jit(solution)/shard_map/all_to_all | solution.py:363
  55.4 6.3 %bag_counts.1 = (bf16[2,512,1024]{2,1,0:T(8,128)(2,1)}, f32[2,1024,128]{2,1,0:T(8,128)}) custom-call(s32[8,2048]{1,0:T(8,128)} %bitcast.29, s32[1,2048]{1,0:T(1,128)} %bitcast.30), custom_call_target="tpu_custom_call" | custom-call | flops 500000000 | bytes 1000 | tf_op jit(solution)/shard_map/bag_counts/pallas_call | solution.py:182
  61.7 0.0 collective-permute-done.4.refs_4_.far_ref
  61.7 0.0 copy-start.9
  61.7 0.0 collective-permute-done.1.refs_1_.first_ref
  61.7 0.0 copy-start.6
  61.7 0.0 collective-permute-done.2.refs_2_.second_ref
  61.7 0.0 copy-start.7
  61.7 0.0 collective-permute-done.3.refs_3_.third_ref
  61.8 0.0 copy-start.8
  61.8 0.6 copy-done.9
  62.4 0.1 copy-done.6
  62.4 0.1 copy-done.7
  62.5 0.1 copy-done.8
  62.6 2.1 %merge_rows.1 = bf16[8,3,128,128]{3,2,1,0:T(8,128)(2,1)} custom-call(bf16[4,128,128]{2,1,0:T(8,128)(2,1)} %get-tuple-element.41.refs_0_.self_ref, bf16[2,4,128,128]{3,2,1,0:T(8,128)(2,1)} %copy-done.6, bf16[2,4,128,128]{3,2,1,0:T(8,128)(2,1)} %copy-done.7, bf16[2,4,128,128]{3,2,1,0:T(8,128)(2,1)} %copy-done.8, bf16[4,128,128]{2,1,0:T(8,128)(2,1)} %copy-done.9), custom_call_target="tpu_custom_call" | custom-call | flops 16000000000 | bytes 1000 | tf_op jit(solution)/shard_map/merge_rows/pallas_call | solution.py:182
  64.7 5.8 %collective-permute-start.5 = (bf16[8,3,128,128]{3,2,1,0:T(8,128)(2,1)}, bf16[8,3,128,128]{3,2,1,0:T(8,128)(2,1)S(1)}, u32[]{:S(2)}, u32[]{:S(2)}) collective-permute-start(bf16[8,3,128,128]{3,2,1,0:T(8,128)(2,1)} %merge_rows.1), channel_id=1, source_target_pairs={{0,64},{64,0},{128,192},{192,128},{256,320},{320,256},{384,448},{4... | collective-permute-start | bytes 2359304 | tf_op jit(solution)/shard_map/ppermute | solution.py:374
  70.6 2.1 %collective-permute-done.5.taken_ref = bf16[8,3,128,128]{3,2,1,0:T(8,128)(2,1)S(1)} collective-permute-done((bf16[8,3,128,128]{3,2,1,0:T(8,128)(2,1)}, bf16[8,3,128,128]{3,2,1,0:T(8,128)(2,1)S(1)}, u32[]{:S(2)}, u32[]{:S(2)}) %collective-permute-start.5) | collective-permute-done | bytes 786464 | tf_op jit(solution)/shard_map/ppermute | solution.py:374
  72.7 0.0 copy-start.4
  72.7 0.9 copy-done.4
  73.6 4.5 %saved_rows.1 = (bf16[2,1024,256]{2,1,0:T(8,128)(2,1)}, bf16[2,1024,128]{2,1,0:T(8,128)(2,1)}, bf16[2,1024,128]{2,1,0:T(8,128)(2,1)}, f32[2,1024,128]{2,1,0:T(8,...) custom-call(s32[1,16]{1,0:T(1,128)} %slots_ref.1, bf16[4,128,128]{2,1,0:T(8,128)(2,1)} %get-tuple-element.41.refs_0_.self_ref, ...), custom_call_target="tpu_custom_call" | custom-call | flops 1000 | bytes 1000 | tf_op jit(solution)/shard_map/saved_rows/pallas_call | solution.py:182
  78.1 7.0 %all-to-all-done.1 = bf16[8,128,512]{2,1,0:T(8,128)(2,1)S(1)} async-done(((bf16[8,128,512]{2,1,0:T(8,128)(2,1)}), bf16[8,128,512]{2,1,0:T(8,128)(2,1)S(1)}, u32[]{:S(2)}, u32[]{:S(2)}) %all-to-all-start.1) | async-done | bytes 1048608 | tf_op jit(solution)/shard_map/all_to_all | solution.py:363
  85.1 0.0 copy-start.3
  85.1 2.7 %collective-permute-start.6 = (bf16[1024,512]{1,0:T(8,128)(2,1)S(1)}, bf16[1024,512]{1,0:T(8,128)(2,1)S(1)}, u32[]{:S(2)}, u32[]{:S(2)}) collective-permute-start(bf16[1024,512]{1,0:T(8,128)(2,1)S(1)} %bitcast.26), channel_id=1, source_target_pairs={{0,64},{64,0},{128,192},{192,128},{256,320},{320,256},{384,448},{4... | collective-permute-start | bytes 3145736 | tf_op jit(solution)/shard_map/ppermute | solution.py:391
  87.8 2.3 %collective-permute-done.6.other_ref = bf16[1024,512]{1,0:T(8,128)(2,1)S(1)} collective-permute-done((bf16[1024,512]{1,0:T(8,128)(2,1)S(1)}, bf16[1024,512]{1,0:T(8,128)(2,1)S(1)}, u32[]{:S(2)}, u32[]{:S(2)}) %collective-permute-start.6) | collective-permute-done | bytes 1048608 | tf_op jit(solution)/shard_map/ppermute | solution.py:391
  90.1 0.0 copy-done.3
  90.1 0.0 copy-start.10
  90.1 1.0 copy-done.10
  91.0 6.2 %column_sums.1 = (f32[128,256]{1,0:T(8,128)}, f32[256,128]{1,0:T(8,128)}, f32[1,128]{1,0:T(1,128)}, f32[128,256]{1,0:T(8,128)}, f32[512,128]{1,0:T(8,128)}) custom-call(bf16[1024,512]{1,0:T(8,128)(2,1)} %bitcast.27, bf16[1024,512]{1,0:T(8,128)(2,1)} %copy-done.10, bf16[2,1024,256]{2,1,0:T(8,128)(2,1)} %get-tuple-element.62.low_ref, ...), custom_call_target="tpu_custom_call" | custom-call | flops 3000000000 | bytes 12000000 | tf_op jit(solution)/shard_map/column_sums/pallas_call | solution.py:117
  (1 shorter events, 0.0 us)
Async XLA Ops:
  0.6 48.2 %copy-start = (bf16[1,2048,256]{2,1,0:T(8,128)(2,1)S(1)}, bf16[1,2048,256]{2,1,0:T(8,128)(2,1)}, u32[]{:S(2)}) copy-start(bf16[1,2048,256]{2,1,0:T(8,128)(2,1)} %param.14) | copy-start | bytes 3145732
  0.6 48.2 %copy-start.1 = (bf16[1,256,2048]{2,1,0:T(8,128)(2,1)S(1)}, bf16[1,256,2048]{2,1,0:T(8,128)(2,1)}, u32[]{:S(2)}) copy-start(bf16[1,256,2048]{2,1,0:T(8,128)(2,1)} %param.12) | copy-start | bytes 3145732
  0.7 27.1 %collective-permute-start = (bf16[128,2048]{1,0:T(8,128)(2,1)}, bf16[128,2048]{1,0:T(8,128)(2,1)S(1)}, u32[]{:S(2)}, u32[]{:S(2)}) collective-permute-start(bf16[128,2048]{1,0:T(8,128)(2,1)} %bitcast.21), channel_id=1, source_target_pairs={{0,64},{64,0},{128,192},{192,128},{256,320},{320,256},{384,448},{4... | collective-permute-start | bytes 1572872 | tf_op jit(solution)/shard_map/ppermute | solution.py:340
  18.4 30.4 %all-to-all-start = ((bf16[2,64,256]{2,0,1:T(2,128)(2,1)}), bf16[2,64,256]{2,0,1:T(2,128)(2,1)S(1)}, u32[]{:S(2)}, u32[]{:S(2)}) async-start(bf16[2,64,256]{2,0,1:T(2,128)(2,1)} %copy.15), calls=%async_computation | async-start | bytes 131072 | tf_op jit(solution)/shard_map/all_to_all | solution.py:336
  27.7 0.8 copy-start.5
  31.5 30.2 %collective-permute-start.1 = (bf16[2,4,128,128]{3,2,1,0:T(8,128)(2,1)}, bf16[2,4,128,128]{3,2,1,0:T(8,128)(2,1)S(1)}, u32[]{:S(2)}, u32[]{:S(2)}) collective-permute-start(bf16[2,4,128,128]{3,2,1,0:T(8,128)(2,1)} %get-tuple-element.45), channel_id=1, source_target_pairs={{0,128},{64,960},{128,256},{192,64},{256,384},{320,192},{384,512},... | collective-permute-start | bytes 786440 | tf_op jit(solution)/shard_map/ppermute | solution.py:350
  36.6 25.1 %collective-permute-start.2 = (bf16[2,4,128,128]{3,2,1,0:T(8,128)(2,1)}, bf16[2,4,128,128]{3,2,1,0:T(8,128)(2,1)S(1)}, u32[]{:S(2)}, u32[]{:S(2)}) collective-permute-start(bf16[2,4,128,128]{3,2,1,0:T(8,128)(2,1)} %get-tuple-element.46), channel_id=1, source_target_pairs={{0,256},{64,832},{128,384},{192,960},{256,512},{320,64},{384,640},... | collective-permute-start | bytes 786440 | tf_op jit(solution)/shard_map/ppermute | solution.py:350
  40.4 21.4 %collective-permute-start.3 = (bf16[2,4,128,128]{3,2,1,0:T(8,128)(2,1)}, bf16[2,4,128,128]{3,2,1,0:T(8,128)(2,1)S(1)}, u32[]{:S(2)}, u32[]{:S(2)}) collective-permute-start(bf16[2,4,128,128]{3,2,1,0:T(8,128)(2,1)} %get-tuple-element.47), channel_id=1, source_target_pairs={{0,384},{64,704},{128,512},{192,832},{256,640},{320,960},{384,768}... | collective-permute-start | bytes 786440 | tf_op jit(solution)/shard_map/ppermute | solution.py:350
  43.1 18.6 %collective-permute-start.4 = (bf16[4,128,128]{2,1,0:T(8,128)(2,1)}, bf16[4,128,128]{2,1,0:T(8,128)(2,1)S(1)}, u32[]{:S(2)}, u32[]{:S(2)}) collective-permute-start(bf16[4,128,128]{2,1,0:T(8,128)(2,1)} %get-tuple-element.48), channel_id=1, source_target_pairs={{0,512},{64,576},{128,640},{192,704},{256,768},{320,832},{384,896}... | collective-permute-start | bytes 393224 | tf_op jit(solution)/shard_map/ppermute | solution.py:350
  48.9 1.0 %copy-start.2 = (bf16[1,128,2048]{2,1,0:T(8,128)(2,1)S(1)}, bf16[1,128,2048]{2,1,0:T(8,128)(2,1)}, u32[]{:S(2)}) copy-start(bf16[1,128,2048]{2,1,0:T(8,128)(2,1)} %param.10) | copy-start | bytes 1572868
  51.9 33.2 %all-to-all-start.1 = ((bf16[8,128,512]{2,1,0:T(8,128)(2,1)}), bf16[8,128,512]{2,1,0:T(8,128)(2,1)S(1)}, u32[]{:S(2)}, u32[]{:S(2)}) async-start(bf16[8,128,512]{2,1,0:T(8,128)(2,1)} %rank_grad_rows.1), calls=%async_computation.1 | async-start | bytes 2097152 | tf_op jit(solution)/shard_map/all_to_all | solution.py:363
  61.7 0.7 copy-start.9
  61.7 0.7 copy-start.6
  61.7 0.8 copy-start.7
  61.8 0.9 copy-start.8
  64.7 7.9 %collective-permute-start.5 = (bf16[8,3,128,128]{3,2,1,0:T(8,128)(2,1)}, bf16[8,3,128,128]{3,2,1,0:T(8,128)(2,1)S(1)}, u32[]{:S(2)}, u32[]{:S(2)}) collective-permute-start(bf16[8,3,128,128]{3,2,1,0:T(8,128)(2,1)} %merge_rows.1), channel_id=1, source_target_pairs={{0,64},{64,0},{128,192},{192,128},{256,320},{320,256},{384,448},{4... | collective-permute-start | bytes 2359304 | tf_op jit(solution)/shard_map/ppermute | solution.py:374
  72.7 0.9 copy-start.4
  85.1 5.0 %copy-start.3 = (bf16[8,128,512]{2,1,0:T(8,128)(2,1)}, bf16[8,128,512]{2,1,0:T(8,128)(2,1)S(1)}, u32[]{:S(2)}) copy-start(bf16[8,128,512]{2,1,0:T(8,128)(2,1)S(1)} %all-to-all-done.1) | copy-start | bytes 3145732
  85.1 5.0 %collective-permute-start.6 = (bf16[1024,512]{1,0:T(8,128)(2,1)S(1)}, bf16[1024,512]{1,0:T(8,128)(2,1)S(1)}, u32[]{:S(2)}, u32[]{:S(2)}) collective-permute-start(bf16[1024,512]{1,0:T(8,128)(2,1)S(1)} %bitcast.26), channel_id=1, source_target_pairs={{0,64},{64,0},{128,192},{192,128},{256,320},{320,256},{384,448},{4... | collective-permute-start | bytes 3145736 | tf_op jit(solution)/shard_map/ppermute | solution.py:391
  90.1 1.0 copy-start.10
